TPU v7x, 768 devices: a whole 4x8x12 slice. The times are simulated.
768 devices in a mesh: row: 16 (over y, core), col: 12 (over z), layer: 4 (over x).
Axes of the slice: x: 4, y: 8, z: 12, core: 2. Of those that a mesh axis runs over, the one named last changes fastest.
Arguments:
- left_blocks: bfloat16 [16, 12, 4, 2, 64, 64], P('row', 'col', 'layer')
- left_coords: int32 [16, 12, 4, 2, 2], P('row', 'col', 'layer'), may hold values from 0 to 383, as said below
- right_blocks: bfloat16 [16, 12, 4, 32, 64, 64], P('row', 'col', 'layer')
- right_coords: int32 [16, 12, 4, 32, 2], P('row', 'col', 'layer'), may hold values from 0 to 383, as said below
Outputs:
- product: float32 [16, 64, 384, 64], P('row', None, ('col', 'layer'))
Inputs may be any that keep to these rules, and one draw needn't show every extreme that they name: `left_coords`: slot s of grid position (r, c, l) holds block row r and an inner index in the l-th quarter of 384, within its c-th of 12 equal pieces. Used slots of one device name distinct blocks; unused slots repeat the coordinates of slot 0 and hold zero blocks. At least half of the slots of every device are used, and all of them on some device. `right_coords`: slot s of grid position (r, c, l) holds an inner index in the l-th quarter of 384, within its r-th of 16 equal pieces, and a block column in c * 32 to (c + 1) * 32 - 1. Used slots of one device name distinct blocks; unused slots repeat the coordinates of slot 0 and hold zero blocks. At least half of the slots of every device are used, and all of them on some device.
All inputs are finite; a program needn't handle non-finite values.
Results may differ from a plain program's by a relative error of at most 0.011.
Values may be sent and summed in bfloat16 or wider, within the bound.
No kernel may reach another device: no remote copies, remote signals or barrier semaphores. Data moves between devices by JAX's collectives and lax.ppermute only.
A program may use at most 128 MiB of HBM per device.

v0:
```python
import jax
import jax.numpy as jnp
from jax import lax
from jax.sharding import PartitionSpec as P

NB = 384
MB = 1


def shards(left_blocks, left_coords, right_blocks, right_coords):
    slots_left = left_blocks.shape[3]
    slots_right = right_blocks.shape[3]
    size = left_blocks.shape[4]
    quarter = NB // lax.axis_size("layer")
    columns = NB // lax.axis_size("col")
    shares = columns // lax.axis_size("layer")
    row_at = lax.axis_index("row")
    col_at = lax.axis_index("col")
    layer_at = lax.axis_index("layer")
    left_flat = left_blocks.reshape(slots_left, size, size)
    left_where = left_coords.reshape(slots_left, 2)
    right_flat = right_blocks.reshape(slots_right, size, size)
    right_where = right_coords.reshape(slots_right, 2)
    positions = jnp.arange(quarter * MB, dtype=jnp.int32)
    inner_range = jnp.arange(quarter, dtype=jnp.int32)
    column_range = jnp.arange(columns, dtype=jnp.int32)
    blocks = lax.all_gather(left_flat, "col", axis=0, tiled=True)
    where = lax.all_gather(left_where, "col", axis=0, tiled=True)
    target = (where[:, 1] - layer_at * quarter) * MB + (where[:, 0] - row_at * MB)
    onehot = (target[:, None] == positions[None, :]).astype(jnp.bfloat16)
    placed = jnp.einsum("np,nab->pab", onehot, blocks, preferred_element_type=jnp.float32)
    panel_flat = placed.astype(jnp.bfloat16)
    panel = panel_flat.reshape(quarter, MB, size, size)

    def multiply(total, blocks, where):
        pick = ((where[:, 0] - layer_at * quarter)[:, None] == inner_range[None, :]).astype(
            jnp.bfloat16
        )
        taken = jnp.einsum("pq,qmab->pmab", pick, panel, preferred_element_type=jnp.float32).astype(
            jnp.bfloat16
        )
        prod = jnp.einsum("pmab,pbc->pmac", taken, blocks, preferred_element_type=jnp.float32)
        place = ((where[:, 1] - col_at * columns)[:, None] == column_range[None, :]).astype(
            jnp.float32
        )
        added = jnp.einsum("pmac,pn->manc", prod, place, precision=lax.Precision.HIGHEST)
        return total + added

    empty_total = jnp.zeros((MB, size, columns, size), jnp.float32)
    all_blocks, all_where = (
        lax.all_gather(right_flat, "row", axis=0, tiled=True),
        lax.all_gather(right_where, "row", axis=0, tiled=True),
    )
    groups = all_blocks.shape[0] // slots_right
    stacked_blocks = all_blocks.reshape(groups, slots_right, size, size)
    stacked_where = all_where.reshape(groups, slots_right, 2)

    def scan_right(total, item):
        return (multiply(total, item[0], item[1]), None)

    total, unused = lax.scan(scan_right, empty_total, (stacked_blocks, stacked_where))
    summed = lax.psum(total.astype(jnp.bfloat16), "layer").astype(jnp.float32)
    product = lax.dynamic_slice_in_dim(summed, layer_at * shares, shares, 2)
    return product


def solution(mesh):
    return jax.shard_map(
        shards,
        mesh=mesh,
        in_specs=(
            P("row", "col", "layer", None, None, None),
            P("row", "col", "layer", None, None),
            P("row", "col", "layer", None, None, None),
            P("row", "col", "layer", None, None),
        ),
        out_specs=P("row", None, ("col", "layer"), None),
        check_vma=False,
    )
```

profile of v0, /device:TPU:1, one launch (start us, length us, event | category | flops | bytes accessed | tf_op | source)
XLA Modules:
  0.0 213.2 jit_solution(12661201030408255463)
XLA Ops:
  7.3 27.9 %all-gather.1 = s32[1,1,1,24,2]{4,2,1,0,3:T(1,128)S(1)} all-gather(s32[1,1,1,2,2]{4,2,1,0,3:T(1,128)} %bitcast.59), channel_id=3, replica_groups=mesh['row'=16,'col'=12,'layer'=4] {'col'}, dimensions={3}, use_global_device_ids=true | all-gather | bytes 208 | tf_op jit(solution)/shard_map/all_gather | solution.py:28
  36.0 25.3 %all-gather = s32[1,1,1,512,2]{4,2,1,0,3:T(1,128)S(1)} all-gather(s32[1,1,1,32,2]{4,2,1,0,3:T(1,128)S(1)} %copy.14), channel_id=2, replica_groups=mesh['row'=16,'col'=12,'layer'=4] {'row'}, dimensions={3}, use_global_device_ids=true | all-gather | bytes 4352 | tf_op jit(solution)/shard_map/all_gather | solution.py:52
  61.5 19.0 %all-gather.2 = bf16[1,1,1,24,64,64]{5,4,2,1,0,3:T(8,128)(2,1)S(1)} all-gather(bf16[1,1,1,2,64,64]{5,4,2,1,0,3:T(8,128)(2,1)} %bitcast.57), channel_id=4, replica_groups=mesh['row'=16,'col'=12,'layer'=4] {'col'}, dimensions={3}, use_global_device_ids=true | all-gather | bytes 212992 | tf_op jit(solution)/shard_map/all_gather | solution.py:27
  81.1 67.4 %while.13 = (s32[]{:T(128)}, f32[1,64,32,64]{3,2,1,0:T(8,128)S(1)}, s32[16,32,2]{1,2,0:T(2,128)S(1)}, s32[]{:T(128)}, s32[]{:T(128)}, /*index=5*/bf16[96,1,64,64...) while((s32[]{:T(128)}, f32[1,64,32,64]{3,2,1,0:T(8,128)S(1)}, ...), condition=%wide.region_1.2_spmd.clone, body=%wide.region_0.1_spmd.clone.sunk | while | flops 92672064 | bytes 3933567 | solution.py:61
  81.1 1.1 convolution_convert_fusion.3
  82.2 1.4 fusion.38
  83.6 1.7 fusion.39
  86.4 1.4 fusion.38
  87.9 1.7 fusion.39
  89.6 1.1 convolution_convert_fusion.3
  90.7 1.4 fusion.38
  92.1 1.7 fusion.39
  94.9 1.4 fusion.38
  96.3 1.7 fusion.39
  98.0 1.1 convolution_convert_fusion.3
  99.1 1.4 fusion.38
  100.5 1.7 fusion.39
  102.2 1.1 convolution_convert_fusion.3
  103.3 1.4 fusion.38
  104.7 1.7 fusion.39
  106.4 1.1 convolution_convert_fusion.3
  107.5 1.4 fusion.38
  108.9 1.7 fusion.39
  110.7 1.1 convolution_convert_fusion.3
  111.7 1.4 fusion.38
  113.1 1.7 fusion.39
  115.9 1.4 fusion.38
  117.4 1.7 fusion.39
  119.1 1.1 convolution_convert_fusion.3
  120.2 1.4 fusion.38
  121.6 1.7 fusion.39
  123.3 1.1 convolution_convert_fusion.3
  124.4 1.4 fusion.38
  125.8 1.7 fusion.39
  127.5 1.1 convolution_convert_fusion.3
  128.6 1.4 fusion.38
  130.0 1.7 fusion.39
  131.7 1.1 convolution_convert_fusion.3
  132.8 1.4 fusion.38
  134.2 1.7 fusion.39
  137.0 1.4 fusion.38
  138.4 1.7 fusion.39
  141.2 1.4 fusion.38
  142.6 1.7 fusion.39
  145.5 1.4 fusion.38
  146.9 1.7 fusion.39
  149.5 55.3 %all-reduce.2.cloned.1.call-done = bf16[1,64,32,64]{3,2,1,0:T(8,128)(2,1)} async-done(((bf16[1,64,32,64]{3,2,1,0:T(8,128)(2,1)}), bf16[1,64,32,64]{3,2,1,0:T(8,128)(2,1)}) %all-reduce.2.cloned.1.call-update) | async-done | bytes 262160 | tf_op jit(solution)/shard_map/psum | solution.py:62
  204.8 1.6 dynamic-slice_convert_fusion
  (50 shorter events, 10.0 us)
Async XLA Ops:
  6.5 74.6 %all-gather.6.cloned.1.call-start = ((), (), s32[]{:S(2)}) async-start(), calls=%async_computation.1 | async-start | bytes 8912896 | tf_op jit(solution)/shard_map/all_gather | solution.py:51
  7.3 197.5 %all-reduce.2.cloned.1.call-start = ((), (), s32[]{:S(2)}) async-start(), calls=%async_computation | async-start | bytes 1048576 | tf_op jit(solution)/shard_map/psum | solution.py:62
Sparse Core Ops, SparseCore 0:
  9.8 70.3 all-gather.5
  149.6 55.1 all-reduce.1
where the time goes:
time: 215 us; the launch traced here: 213 us
  blocking collectives  72.2 us (34%)
  matrix products  67.1 us (31%)
  waiting for transfers between devices  56 us (26%)
  between operations  13.5 us (6%)
  other arithmetic  2.66 us (1%)
    psum x1, waiting for transfers between devices, shards(): summed = lax.psum(total.astype(jnp.bfloat16), 'layer').astype(jnp.float32)  55.3 us
    all_gather x1, blocking collectives, shards(): where = lax.all_gather(left_where, 'col', axis=0, tiled=True)  27.9 us
    dot_general x16, matrix products, multiply(): jnp.einsum('pmac,pn->manc', prod, place, precision=lax.Precision.HIGHEST)  26.8 us
    all_gather x1, blocking collectives, shards(): lax.all_gather(right_where, 'row', axis=0, tiled=True)  25.3 us
    dot_general x16, matrix products, multiply(): jnp.einsum('pmab,pbc->pmac', taken, blocks, preferred_element_type=jnp.fl...  22.5 us
    all_gather x1, blocking collectives, shards(): blocks = lax.all_gather(left_flat, 'col', axis=0, tiled=True)  19 us
    dot_general x16, matrix products, multiply(): jnp.einsum('pq,qmab->pmab', pick, panel, preferred_element_type=jnp.float32)  17.3 us
  transfers between devices with their start and end apart: 2, of which 1 were waited for; matrix products, arithmetic and copies ran while one was open for 1% of the time, Pallas kernels for 0%

commit v1 on v0

v1 whole, which is shorter than its diff:
```python
import functools

import jax
import jax.numpy as jnp
from jax import lax
from jax.experimental import pallas as pl
from jax.experimental.pallas import tpu as pltpu
from jax.sharding import Mesh
from jax.sharding import PartitionSpec as P

NB = 384
BS = 64
N_Y = 8
N_COL = 12
N_LAYER = 4
SLOTS = 32
PAIRS = SLOTS // 2
BODY = PAIRS * BS
MSG = BODY + 16
LMSG = BS + 16
INNER = 6
COLUMNS = NB // N_COL
PIECE = NB // N_LAYER // N_COL
DEPTH = INNER * BS
WIDTH = COLUMNS * BS
STEPS = (0, 1, 1, 2, 2, 3, 3, 4)
OTHER = (0, 0, 1, 0, 1, 0, 1, 0)


def multiply_kernel(own, other, *refs):
    blocks, (out, left, panel, swapped, total, where, places, sem) = refs[:8], refs[8:]
    y = lax.axis_index("y")
    core = lax.axis_index("core")
    for j in range(8):
        tail = blocks[j][BODY:MSG, :].astype(jnp.float32).astype(jnp.int32)
        where[2 * j : 2 * j + 2, :] = tail[0:2, :]
    copy = pltpu.make_async_copy(where, places, sem)
    copy.start()

    to = lax.broadcasted_iota(jnp.int32, (128, 128), 1)
    frm = lax.broadcasted_iota(jnp.int32, (128, 128), 0)
    swap = (to == (frm + BS) % 128).astype(jnp.bfloat16)
    lane = lax.broadcasted_iota(jnp.int32, (BS, 128), 1)
    upper = (lane >= BS).astype(jnp.float32)

    for src, at in ((own, core), (other, 1 - core)):
        rows = pl.ds(pl.multiple_of(at * BS, BS), BS)
        for c in range(N_COL):
            whole = src[c]
            turned = jnp.dot(whole, swap, preferred_element_type=jnp.float32)
            whole = whole.astype(jnp.float32)
            here, there = whole[:BS], turned[:BS]
            k_here, k_there = whole[BS : BS + 1], turned[BS : BS + 1]
            for g in range(PIECE // 2):
                want = upper + 2.0 * g
                value = jnp.where(k_here == want, here, 0.0) + jnp.where(k_there == want, there, 0.0)
                at_lane = (c * PIECE + 2 * g) * BS
                left[rows, at_lane : at_lane + 128] = value.astype(jnp.bfloat16)

    low = (lane < BS).astype(jnp.bfloat16)
    high = (lane >= BS).astype(jnp.bfloat16)
    copy.wait()
    for j in range(8):
        panel[...] = jnp.zeros_like(panel)
        swapped[...] = jnp.dot(
            blocks[j][:BODY, :], swap, preferred_element_type=jnp.float32
        ).astype(jnp.bfloat16)

        def place(p, carry):
            at = pl.ds(pl.multiple_of(p * BS, BS), BS)
            tile = blocks[j][at, :]
            turned = swapped[at, :]
            for half in range(2):
                k = places[2 * j, p + half * PAIRS]
                n = places[2 * j + 1, p + half * PAIRS]
                odd = n % 2
                value = jnp.where(odd == half, tile, turned) * jnp.where(odd == 1, high, low)
                rows = pl.ds(pl.multiple_of(k * BS, BS), BS)
                lanes = pl.ds(pl.multiple_of((n // 2) * 128, 128), 128)
                panel[rows, lanes] = panel[rows, lanes] + value
            return carry

        lax.fori_loop(0, PAIRS, place, 0)
        chip = lax.rem(y + N_Y + jnp.where(core == 0, -STEPS[j], STEPS[j]), N_Y)
        owner = chip * 2 + (1 - core if OTHER[j] else core)
        at = pl.ds(pl.multiple_of(owner * DEPTH, 128), DEPTH)
        part = jnp.dot(left[:, at], panel[...], preferred_element_type=jnp.float32)
        total[...] = part if j == 0 else total[...] + part
    share = WIDTH // N_LAYER
    for m in range(2):
        for s in range(N_LAYER):
            out[m * N_LAYER + s] = total[m * BS : (m + 1) * BS, s * share : (s + 1) * share].astype(
                jnp.bfloat16
            )


def multiply(own, other, blocks):
    vmem = pl.BlockSpec(memory_space=pltpu.VMEM)
    return pl.pallas_call(
        multiply_kernel,
        out_shape=jax.ShapeDtypeStruct((2 * N_LAYER, BS, WIDTH // N_LAYER), jnp.bfloat16),
        in_specs=[vmem] * 10,
        out_specs=vmem,
        scratch_shapes=[
            pltpu.VMEM((2 * BS, NB // N_LAYER * BS), jnp.bfloat16),
            pltpu.VMEM((DEPTH, WIDTH), jnp.bfloat16),
            pltpu.VMEM((BODY, 128), jnp.bfloat16),
            pltpu.VMEM((2 * BS, WIDTH), jnp.float32),
            pltpu.VMEM((16, 128), jnp.int32),
            pltpu.SMEM((16, 128), jnp.int32),
            pltpu.SemaphoreType.DMA,
        ],
        compiler_params=pltpu.CompilerParams(vmem_limit_bytes=40 * 1024 * 1024),
        cost_estimate=pl.CostEstimate(
            flops=2 * 128 * 3072 * 2048, bytes_accessed=4 << 20, transcendentals=0
        ),
    )(own, other, *blocks)


def shards(left_blocks, left_coords, right_blocks, right_coords):
    y = lax.axis_index("y")
    core = lax.axis_index("core")
    col = lax.axis_index("col")
    layer = lax.axis_index("layer")
    base = layer * (NB // N_LAYER)

    r = right_blocks.reshape(SLOTS, BS, BS)
    body = jnp.concatenate([r[:PAIRS], r[PAIRS:]], axis=-1).reshape(BODY, 128)
    rc = right_coords.reshape(SLOTS, 2)
    inner = rc[:, 0] - (base + (y * 2 + core) * INNER)
    column = rc[:, 1] - col * COLUMNS
    tail = jnp.stack([inner, column]).astype(jnp.bfloat16)
    tail = jnp.pad(tail, ((0, 14), (0, 128 - SLOTS)))
    mine = jnp.concatenate([body, tail], axis=0)

    b = left_blocks.reshape(2, BS, BS)
    at = (left_coords.reshape(2, 2)[:, 1] - (base + col * PIECE)).astype(jnp.bfloat16)
    at = jnp.broadcast_to(jnp.repeat(at, BS)[None, :], (16, 128))
    piece = jnp.concatenate([jnp.concatenate([b[0], b[1]], axis=-1), at], axis=0)

    ring = [((2 * i + c), ((2 * ((i + (1 if c == 0 else -1)) % N_Y)) + c)) for i in range(N_Y) for c in (0, 1)]
    cores = [(i, i ^ 1) for i in range(2 * N_Y)]
    axes = ("y", "core")

    a = lax.ppermute(mine, axes, ring)
    theirs = lax.ppermute(mine, axes, cores)
    pieces = lax.all_to_all(jnp.broadcast_to(piece[None], (N_COL, LMSG, 128)), "col", 0, 0)
    blocks = [mine, a]
    o = theirs
    for step in range(1, 4):
        o = lax.ppermute(o, axes, ring)
        blocks.append(o)
        a = lax.ppermute(a, axes, ring)
        blocks.append(a)
    pieces_other = lax.ppermute(pieces, axes, cores)
    part = multiply(pieces, pieces_other, blocks)
    parts = lax.all_to_all(part, ("core", "layer"), 0, 0)
    total = jnp.sum(parts.astype(jnp.float32), axis=0)
    return total.reshape(1, BS, COLUMNS // N_LAYER, BS)


def solution(mesh):
    grid = Mesh(mesh.devices.reshape(N_Y, 2, N_COL, N_LAYER), ("y", "core", "col", "layer"))
    row = ("y", "core")
    return jax.shard_map(
        shards,
        mesh=grid,
        in_specs=(
            P(row, "col", "layer", None, None, None),
            P(row, "col", "layer", None, None),
            P(row, "col", "layer", None, None, None),
            P(row, "col", "layer", None, None),
        ),
        out_specs=P(row, None, ("col", "layer"), None),
        check_vma=False,
    )
```

time: 215 us -> 83.1 us (0.39)
  matrix products: 67.1 us -> 0 us
  blocking collectives: 72.2 us -> 17.2 us
  waiting for transfers between devices: 56 us -> 3.71 us
  starting transfers between devices: 0.04 us -> 46.6 us
  between operations: 13.5 us -> 0.21 us
  Pallas kernels: 0 us -> 10.2 us
  local copies, waits for them, and re-layouts: 1.12 us -> 4.12 us
  other arithmetic: 2.66 us -> 0.51 us
    all_gather x3 -> x0, blocking collectives: 72.2 us -> none  [the longest x1 27.9 us: shards(): where = lax.all_gather(left_where, 'col', axis=0, tiled=True)]
    dot_general x49 -> x0, matrix products: 67.1 us -> none  [the longest x16 26.8 us: multiply(): jnp.einsum('pmac,pn->manc', prod, place, precision=lax.Precision.HIGHEST)]
    psum x1 -> x0, waiting for transfers between devices: 55.3 us -> none  [shards(): summed = lax.psum(total.astype(jnp.bfloat16), 'layer').astype(jnp.float32)]
    ppermute x0 -> x9, starting transfers between devices: none -> 37.6 us  [the longest x1 12.4 us: shards(): theirs = lax.ppermute(mine, axes, cores)]
    all_to_all x0 -> x1, blocking collectives: none -> 17.2 us  [shards(): parts = lax.all_to_all(part, ('core', 'layer'), 0, 0)]
    pallas_call x0 -> x1, Pallas kernels: none -> 10.2 us  [multiply(): pl.pallas_call(multiply_kernel, out_shape=jax.ShapeDtypeStruct((2 * N_LAY...]
    all_to_all x0 -> x1, starting transfers between devices: none -> 9.04 us  [shards(): lax.all_to_all(jnp.broadcast_to(piece[None], (N_COL, LMSG, 128)), 'col',...]
    ppermute x0 -> x9, waiting for transfers between devices: none -> 3.71 us  [the longest x3 1.74 us: shards(): o = lax.ppermute(o, axes, ring)]
  transfers between devices with their start and end apart: 2 -> 10, of which waited for: 1 -> 4; matrix products, arithmetic and copies ran while one was open for 1% -> 1% of each run, Pallas kernels for 0% -> 0%
where the time goes in v1:
time: 83.1 us; the launch traced here: 82.5 us
  starting transfers between devices  46.6 us (56%)
  blocking collectives  17.2 us (21%)
  Pallas kernels  10.2 us (12%)
  local copies, waits for them, and re-layouts  4.12 us (5%)
  waiting for transfers between devices  3.71 us (4%)
    all_to_all x1, blocking collectives, shards(): parts = lax.all_to_all(part, ('core', 'layer'), 0, 0)  17.2 us
    ppermute x1, starting transfers between devices, shards(): theirs = lax.ppermute(mine, axes, cores)  12.4 us
    ppermute x3, starting transfers between devices, shards(): o = lax.ppermute(o, axes, ring)  11.9 us
    pallas_call x1, Pallas kernels, multiply(): pl.pallas_call(multiply_kernel, out_shape=jax.ShapeDtypeStruct((2 * N_LAY...  10.2 us
    ppermute x3, starting transfers between devices, shards(): a = lax.ppermute(a, axes, ring)  9.24 us
    all_to_all x1, starting transfers between devices, shards(): lax.all_to_all(jnp.broadcast_to(piece[None], (N_COL, LMSG, 128)), 'col',...  9.04 us
    ppermute x1, starting transfers between devices, shards(): pieces_other = lax.ppermute(pieces, axes, cores)  2.04 us
    ppermute x1, starting transfers between devices, shards(): a = lax.ppermute(mine, axes, ring)  1.92 us
  transfers between devices with their start and end apart: 10, of which 4 were waited for; matrix products, arithmetic and copies ran while one was open for 1% of the time, Pallas kernels for 0%

profile of v1, /device:TPU:1, one launch (start us, length us, event | category | flops | bytes accessed | tf_op | source)
XLA Modules:
  0.0 82.5 jit_solution(2843270344669322260)
XLA Ops:
  0.0 1.1 %fusion.7 = (bf16[1,1,1,16,64,64]{5,4,3,2,1,0:T(8,128)(2,1)S(1)}, bf16[1,1,1,16,64,64]{5,4,3,2,1,0:T(8,128)(2,1)S(1)}) fusion(bf16[1,1,1,32,64,64]{5,4,3,2,1,0:T(8,128)(2,1)} %param.6), kind=kLoop, calls=%fused_computation.17 | loop fusion | bytes 524288 | tf_op jit(solution)/shard_map/slice | solution.py:128
  1.1 0.0 copy-start.1
  1.1 0.7 copy-done.1
  1.8 0.0 copy-start
  1.8 0.1 pad_maximum_fusion.refs_0_
  2.0 12.4 %collective-permute-start.2 = (bf16[1040,128]{1,0:T(8,128)(2,1)S(1)}, bf16[1040,128]{1,0:T(8,128)(2,1)S(1)}, u32[]{:S(2)}, u32[]{:S(2)}) collective-permute-start(bf16[1040,128]{1,0:T(8,128)(2,1)S(1)} %pad_maximum_fusion.refs_0_), channel_id=1, source_target_pairs={{0,48},{48,0},{96,144},{144,96},{192,240},{240,192},{288,336},{336... | collective-permute-start | bytes 798728 | tf_op jit(solution)/shard_map/ppermute | solution.py:146
  14.4 1.9 %collective-permute-start.1 = (bf16[1040,128]{1,0:T(8,128)(2,1)S(1)}, bf16[1040,128]{1,0:T(8,128)(2,1)S(1)}, u32[]{:S(2)}, u32[]{:S(2)}) collective-permute-start(bf16[1040,128]{1,0:T(8,128)(2,1)S(1)} %pad_maximum_fusion.refs_0_), channel_id=1, source_target_pairs={{0,96},{48,720},{96,192},{144,48},{192,288},{240,144},{288,384},{3... | collective-permute-start | bytes 798728 | tf_op jit(solution)/shard_map/ppermute | solution.py:145
  16.3 0.0 copy-done
  16.3 0.0 copy-start.2
  16.4 0.7 copy-done.2
  17.0 0.2 fusion.6
  17.2 0.1 broadcast_in_dim.16
  17.3 0.1 broadcast_in_dim.17
  17.4 0.1 pad_maximum_fusion.1
  17.5 0.7 broadcast_in_dim.19
  18.2 9.0 %all-to-all-start = ((bf16[12,80,128]{2,1,0:T(8,128)(2,1)}), bf16[12,80,128]{2,1,0:T(8,128)(2,1)S(1)}, u32[]{:S(2)}, u32[]{:S(2)}) async-start(bf16[12,80,128]{2,1,0:T(8,128)(2,1)} %broadcast_in_dim.19), calls=%async_computation | async-start | bytes 491520 | tf_op jit(solution)/shard_map/all_to_all | solution.py:147
  27.2 0.0 collective-permute-done.2
  27.3 3.0 %collective-permute-start.3 = (bf16[1040,128]{1,0:T(8,128)(2,1)S(1)}, bf16[1040,128]{1,0:T(8,128)(2,1)S(1)}, u32[]{:S(2)}, u32[]{:S(2)}) collective-permute-start(bf16[1040,128]{1,0:T(8,128)(2,1)S(1)} %collective-permute-done.2), channel_id=1, source_target_pairs={{0,96},{48,720},{96,192},{144,48},{192,288},{240,144},{288,384},{3... | collective-permute-start | bytes 798728 | tf_op jit(solution)/shard_map/ppermute | solution.py:151
  30.2 0.0 collective-permute-done.1.refs_1_
  30.3 3.0 %collective-permute-start.4 = (bf16[1040,128]{1,0:T(8,128)(2,1)S(1)}, bf16[1040,128]{1,0:T(8,128)(2,1)S(1)}, u32[]{:S(2)}, u32[]{:S(2)}) collective-permute-start(bf16[1040,128]{1,0:T(8,128)(2,1)S(1)} %collective-permute-done.1.refs_1_), channel_id=1, source_target_pairs={{0,96},{48,720},{96,192},{144,48},{192,288},{240,144},{288,384},{3... | collective-permute-start | bytes 798728 | tf_op jit(solution)/shard_map/ppermute | solution.py:153
  33.2 1.5 %collective-permute-done.3.refs_2_ = bf16[1040,128]{1,0:T(8,128)(2,1)S(1)} collective-permute-done((bf16[1040,128]{1,0:T(8,128)(2,1)S(1)}, bf16[1040,128]{1,0:T(8,128)(2,1)S(1)}, u32[]{:S(2)}, u32[]{:S(2)}) %collective-permute-start.3) | collective-permute-done | bytes 266272 | tf_op jit(solution)/shard_map/ppermute | solution.py:151
  34.7 4.0 %collective-permute-start.5 = (bf16[1040,128]{1,0:T(8,128)(2,1)S(1)}, bf16[1040,128]{1,0:T(8,128)(2,1)S(1)}, u32[]{:S(2)}, u32[]{:S(2)}) collective-permute-start(bf16[1040,128]{1,0:T(8,128)(2,1)S(1)} %collective-permute-done.3.refs_2_), channel_id=1, source_target_pairs={{0,96},{48,720},{96,192},{144,48},{192,288},{240,144},{288,384},{3... | collective-permute-start | bytes 798728 | tf_op jit(solution)/shard_map/ppermute | solution.py:151
  38.7 0.0 collective-permute-done.4.refs_3_
  38.8 3.1 %collective-permute-start.6 = (bf16[1040,128]{1,0:T(8,128)(2,1)S(1)}, bf16[1040,128]{1,0:T(8,128)(2,1)S(1)}, u32[]{:S(2)}, u32[]{:S(2)}) collective-permute-start(bf16[1040,128]{1,0:T(8,128)(2,1)S(1)} %collective-permute-done.4.refs_3_), channel_id=1, source_target_pairs={{0,96},{48,720},{96,192},{144,48},{192,288},{240,144},{288,384},{3... | collective-permute-start | bytes 798728 | tf_op jit(solution)/shard_map/ppermute | solution.py:153
  41.9 0.3 collective-permute-done.5.refs_4_
  42.2 4.9 %collective-permute-start.7 = (bf16[1040,128]{1,0:T(8,128)(2,1)S(1)}, bf16[1040,128]{1,0:T(8,128)(2,1)S(1)}, u32[]{:S(2)}, u32[]{:S(2)}) collective-permute-start(bf16[1040,128]{1,0:T(8,128)(2,1)S(1)} %collective-permute-done.5.refs_4_), channel_id=1, source_target_pairs={{0,96},{48,720},{96,192},{144,48},{192,288},{240,144},{288,384},{3... | collective-permute-start | bytes 798728 | tf_op jit(solution)/shard_map/ppermute | solution.py:151
  47.1 0.0 collective-permute-done.6.refs_5_
  47.1 3.1 %collective-permute-start.8 = (bf16[1040,128]{1,0:T(8,128)(2,1)S(1)}, bf16[1040,128]{1,0:T(8,128)(2,1)S(1)}, u32[]{:S(2)}, u32[]{:S(2)}) collective-permute-start(bf16[1040,128]{1,0:T(8,128)(2,1)S(1)} %collective-permute-done.6.refs_5_), channel_id=1, source_target_pairs={{0,96},{48,720},{96,192},{144,48},{192,288},{240,144},{288,384},{3... | collective-permute-start | bytes 798728 | tf_op jit(solution)/shard_map/ppermute | solution.py:153
  50.3 0.0 all-to-all-done.own
  50.3 2.0 %collective-permute-start = (bf16[12,80,128]{2,1,0:T(8,128)(2,1)S(1)}, bf16[12,80,128]{2,1,0:T(8,128)(2,1)S(1)}, u32[]{:S(2)}, u32[]{:S(2)}) collective-permute-start(bf16[12,80,128]{2,1,0:T(8,128)(2,1)S(1)} %all-to-all-done.own), channel_id=1, source_target_pairs={{0,48},{48,0},{96,144},{144,96},{192,240},{240,192},{288,336},{336... | collective-permute-start | bytes 737288 | tf_op jit(solution)/shard_map/ppermute | solution.py:155
  52.3 1.4 %collective-permute-done.other = bf16[12,80,128]{2,1,0:T(8,128)(2,1)S(1)} collective-permute-done((bf16[12,80,128]{2,1,0:T(8,128)(2,1)S(1)}, bf16[12,80,128]{2,1,0:T(8,128)(2,1)S(1)}, u32[]{:S(2)}, u32[]{:S(2)}) %collective-permute-start) | collective-permute-done | bytes 245792 | tf_op jit(solution)/shard_map/ppermute | solution.py:155
  53.7 0.0 collective-permute-done.7.refs_6_
  53.7 0.6 collective-permute-done.8.refs_7_
  54.3 10.2 %shard_map.46 = bf16[8,64,512]{2,1,0:T(8,128)(2,1)S(1)} custom-call(bf16[12,80,128]{2,1,0:T(8,128)(2,1)S(1)} %all-to-all-done.own, bf16[12,80,128]{2,1,0:T(8,128)(2,1)S(1)} %collective-permute-done.other, bf16[1040,128]{1,0:T(8,128)(2,1)S(1)} %pad_maximum_fusion.refs_0_, bf16[1040,128]{1,0:T(8,128)(2,1)S(1)} %collective-permute-done.1.refs_1_, ...), custom_call_target="tpu_custom_call" | custom-call | flops 1610612736 | bytes 4194304 | tf_op jit(solution)/shard_map/pallas_call | solution.py:99
  64.4 17.2 %all_to_all.10 = bf16[8,64,512]{2,1,0:T(8,128)(2,1)S(1)} all-to-all(bf16[8,64,512]{2,1,0:T(8,128)(2,1)S(1)} %shard_map.46), channel_id=1, replica_groups=mesh['y'=8,'core'=2,'col'=12,'layer'=4] {'core','layer'}, dimensions={0} | all-to-all | bytes 1048576 | tf_op jit(solution)/shard_map/all_to_all | solution.py:157
  81.6 0.1 convert_reduce_fusion
  81.7 0.8 reshape.55
  (4 shorter events, 0.0 us)
Async XLA Ops:
  1.1 0.7 copy-start.1
  1.8 14.5 %copy-start = (bf16[1,1,1,2,64,64]{5,4,3,2,1,0:T(8,128)(2,1)S(1)}, bf16[1,1,1,2,64,64]{5,4,3,2,1,0:T(8,128)(2,1)}, u32[]{:S(2)}) copy-start(bf16[1,1,1,2,64,64]{5,4,3,2,1,0:T(8,128)(2,1)} %param.4) | copy-start | bytes 49156
  2.0 25.3 %collective-permute-start.2 = (bf16[1040,128]{1,0:T(8,128)(2,1)S(1)}, bf16[1040,128]{1,0:T(8,128)(2,1)S(1)}, u32[]{:S(2)}, u32[]{:S(2)}) collective-permute-start(bf16[1040,128]{1,0:T(8,128)(2,1)S(1)} %pad_maximum_fusion.refs_0_), channel_id=1, source_target_pairs={{0,48},{48,0},{96,144},{144,96},{192,240},{240,192},{288,336},{336... | collective-permute-start | bytes 798728 | tf_op jit(solution)/shard_map/ppermute | solution.py:146
  14.4 15.9 %collective-permute-start.1 = (bf16[1040,128]{1,0:T(8,128)(2,1)S(1)}, bf16[1040,128]{1,0:T(8,128)(2,1)S(1)}, u32[]{:S(2)}, u32[]{:S(2)}) collective-permute-start(bf16[1040,128]{1,0:T(8,128)(2,1)S(1)} %pad_maximum_fusion.refs_0_), channel_id=1, source_target_pairs={{0,96},{48,720},{96,192},{144,48},{192,288},{240,144},{288,384},{3... | collective-permute-start | bytes 798728 | tf_op jit(solution)/shard_map/ppermute | solution.py:145
  16.3 0.7 copy-start.2
  18.2 32.1 %all-to-all-start = ((bf16[12,80,128]{2,1,0:T(8,128)(2,1)}), bf16[12,80,128]{2,1,0:T(8,128)(2,1)S(1)}, u32[]{:S(2)}, u32[]{:S(2)}) async-start(bf16[12,80,128]{2,1,0:T(8,128)(2,1)} %broadcast_in_dim.19), calls=%async_computation | async-start | bytes 491520 | tf_op jit(solution)/shard_map/all_to_all | solution.py:147
  27.3 7.5 %collective-permute-start.3 = (bf16[1040,128]{1,0:T(8,128)(2,1)S(1)}, bf16[1040,128]{1,0:T(8,128)(2,1)S(1)}, u32[]{:S(2)}, u32[]{:S(2)}) collective-permute-start(bf16[1040,128]{1,0:T(8,128)(2,1)S(1)} %collective-permute-done.2), channel_id=1, source_target_pairs={{0,96},{48,720},{96,192},{144,48},{192,288},{240,144},{288,384},{3... | collective-permute-start | bytes 798728 | tf_op jit(solution)/shard_map/ppermute | solution.py:151
  30.3 8.5 %collective-permute-start.4 = (bf16[1040,128]{1,0:T(8,128)(2,1)S(1)}, bf16[1040,128]{1,0:T(8,128)(2,1)S(1)}, u32[]{:S(2)}, u32[]{:S(2)}) collective-permute-start(bf16[1040,128]{1,0:T(8,128)(2,1)S(1)} %collective-permute-done.1.refs_1_), channel_id=1, source_target_pairs={{0,96},{48,720},{96,192},{144,48},{192,288},{240,144},{288,384},{3... | collective-permute-start | bytes 798728 | tf_op jit(solution)/shard_map/ppermute | solution.py:153
  34.7 7.4 %collective-permute-start.5 = (bf16[1040,128]{1,0:T(8,128)(2,1)S(1)}, bf16[1040,128]{1,0:T(8,128)(2,1)S(1)}, u32[]{:S(2)}, u32[]{:S(2)}) collective-permute-start(bf16[1040,128]{1,0:T(8,128)(2,1)S(1)} %collective-permute-done.3.refs_2_), channel_id=1, source_target_pairs={{0,96},{48,720},{96,192},{144,48},{192,288},{240,144},{288,384},{3... | collective-permute-start | bytes 798728 | tf_op jit(solution)/shard_map/ppermute | solution.py:151
  38.8 8.4 %collective-permute-start.6 = (bf16[1040,128]{1,0:T(8,128)(2,1)S(1)}, bf16[1040,128]{1,0:T(8,128)(2,1)S(1)}, u32[]{:S(2)}, u32[]{:S(2)}) collective-permute-start(bf16[1040,128]{1,0:T(8,128)(2,1)S(1)} %collective-permute-done.4.refs_3_), channel_id=1, source_target_pairs={{0,96},{48,720},{96,192},{144,48},{192,288},{240,144},{288,384},{3... | collective-permute-start | bytes 798728 | tf_op jit(solution)/shard_map/ppermute | solution.py:153
  42.2 11.5 %collective-permute-start.7 = (bf16[1040,128]{1,0:T(8,128)(2,1)S(1)}, bf16[1040,128]{1,0:T(8,128)(2,1)S(1)}, u32[]{:S(2)}, u32[]{:S(2)}) collective-permute-start(bf16[1040,128]{1,0:T(8,128)(2,1)S(1)} %collective-permute-done.5.refs_4_), channel_id=1, source_target_pairs={{0,96},{48,720},{96,192},{144,48},{192,288},{240,144},{288,384},{3... | collective-permute-start | bytes 798728 | tf_op jit(solution)/shard_map/ppermute | solution.py:151
  47.1 7.2 %collective-permute-start.8 = (bf16[1040,128]{1,0:T(8,128)(2,1)S(1)}, bf16[1040,128]{1,0:T(8,128)(2,1)S(1)}, u32[]{:S(2)}, u32[]{:S(2)}) collective-permute-start(bf16[1040,128]{1,0:T(8,128)(2,1)S(1)} %collective-permute-done.6.refs_5_), channel_id=1, source_target_pairs={{0,96},{48,720},{96,192},{144,48},{192,288},{240,144},{288,384},{3... | collective-permute-start | bytes 798728 | tf_op jit(solution)/shard_map/ppermute | solution.py:153
  50.3 3.4 %collective-permute-start = (bf16[12,80,128]{2,1,0:T(8,128)(2,1)S(1)}, bf16[12,80,128]{2,1,0:T(8,128)(2,1)S(1)}, u32[]{:S(2)}, u32[]{:S(2)}) collective-permute-start(bf16[12,80,128]{2,1,0:T(8,128)(2,1)S(1)} %all-to-all-done.own), channel_id=1, source_target_pairs={{0,48},{48,0},{96,144},{144,96},{192,240},{240,192},{288,336},{336... | collective-permute-start | bytes 737288 | tf_op jit(solution)/shard_map/ppermute | solution.py:155

commit v2 on v1

v2 whole, which is shorter than its diff:
```python
import jax
import jax.numpy as jnp
from jax import lax
from jax.experimental import pallas as pl
from jax.experimental.pallas import tpu as pltpu
from jax.sharding import Mesh
from jax.sharding import PartitionSpec as P

NB = 384
BS = 64
N_Y = 8
N_COL = 12
N_LAYER = 4
SLOTS = 32
PAIRS = SLOTS // 2
BODY = PAIRS * BS
MSG = BODY + 16
LMSG = BS + 16
INNER = 6
COLUMNS = NB // N_COL
PIECE = NB // N_LAYER // N_COL
DEPTH = INNER * BS
WIDTH = COLUMNS * BS
STEPS = (0, 1, 1, 2, 2, 3, 3, 4)
OTHER = (0, 0, 1, 0, 1, 0, 1, 0)
EARLY_COST = 64 << 20
EARLY = 5


def pack_kernel(right, right_where, left, left_where, out, tail):
    y = lax.axis_index("y")
    core = lax.axis_index("core")
    col = lax.axis_index("col")
    base = lax.axis_index("layer") * (NB // N_LAYER)
    for p in range(PAIRS):
        out[p * BS : (p + 1) * BS, :] = jnp.concatenate([right[p], right[p + PAIRS]], axis=-1)
    tail[...] = jnp.zeros_like(tail)
    inner = right_where[0:1, :] - (base + (y * 2 + core) * INNER)
    column = right_where[1:2, :] - col * COLUMNS
    tail[0:1, 0:SLOTS] = inner.astype(jnp.float32)
    tail[1:2, 0:SLOTS] = column.astype(jnp.float32)
    out[BODY:MSG, :] = tail[...].astype(jnp.bfloat16)
    out[MSG : MSG + BS, :] = jnp.concatenate([left[0], left[1]], axis=-1)
    lane = lax.broadcasted_iota(jnp.int32, (16, 128), 1)
    first = jnp.broadcast_to(left_where[0:1, 1:2], (16, 128))
    second = jnp.broadcast_to(left_where[1:2, 1:2], (16, 128))
    at = jnp.where(lane < BS, first, second) - (base + col * PIECE)
    out[MSG + BS :, :] = at.astype(jnp.float32).astype(jnp.bfloat16)


def pack(right, right_where, left, left_where):
    vmem = pl.BlockSpec(memory_space=pltpu.VMEM)
    return pl.pallas_call(
        pack_kernel,
        out_shape=jax.ShapeDtypeStruct((MSG + LMSG, 128), jnp.bfloat16),
        in_specs=[vmem] * 4,
        out_specs=vmem,
        scratch_shapes=[pltpu.VMEM((16, 128), jnp.float32)],
        cost_estimate=pl.CostEstimate(flops=0, bytes_accessed=1 << 20, transcendentals=0),
    )(right, right_where, left, left_where)


def spread_kernel(mine, theirs, out):
    first = lax.broadcasted_iota(jnp.int32, (16, 128), 0) == 0
    tail = jnp.where(
        first, mine[MSG + BS :, :].astype(jnp.float32), theirs[MSG + BS :, :].astype(jnp.float32)
    ).astype(jnp.bfloat16)
    for c in range(N_COL):
        out[c, :BS, :] = mine[MSG : MSG + BS, :]
        out[c, BS : 2 * BS, :] = theirs[MSG : MSG + BS, :]
        out[c, 2 * BS :, :] = tail


def spread(mine, theirs):
    vmem = pl.BlockSpec(memory_space=pltpu.VMEM)
    return pl.pallas_call(
        spread_kernel,
        out_shape=jax.ShapeDtypeStruct((N_COL, 2 * BS + 16, 128), jnp.bfloat16),
        in_specs=[vmem, vmem],
        out_specs=vmem,
        cost_estimate=pl.CostEstimate(flops=0, bytes_accessed=1 << 20, transcendentals=0),
    )(mine, theirs)


def half_swap():
    to = lax.broadcasted_iota(jnp.int32, (128, 128), 1)
    frm = lax.broadcasted_iota(jnp.int32, (128, 128), 0)
    return (to == (frm + BS) % 128).astype(jnp.bfloat16)


def read_places(blocks, where, places, sem):
    for j, (ref, top) in enumerate(blocks):
        tail = ref[top + BODY : top + MSG, :].astype(jnp.float32).astype(jnp.int32)
        where[2 * j : 2 * j + 2, :] = tail[0:2, :]
    copy = pltpu.make_async_copy(where, places, sem)
    copy.start()
    return copy


def place_slots(blocks, first, panels, swapped, places):
    lane = lax.broadcasted_iota(jnp.int32, (BS, 128), 1)
    low = (lane < BS).astype(jnp.bfloat16)
    high = (lane >= BS).astype(jnp.bfloat16)

    def place(p, carry):
        for half in range(2):
            for i, (ref, top) in enumerate(blocks):
                k = places[2 * (first + i), p + half * PAIRS]
                n = places[2 * (first + i) + 1, p + half * PAIRS]
                odd = n & 1
                tile = ref[pl.ds(pl.multiple_of(top + p * BS, 16), BS), :]
                turned = swapped[i][pl.ds(pl.multiple_of(p * BS, BS), BS), :]
                value = jnp.where(odd == half, tile, turned) * jnp.where(odd == 1, high, low)
                rows = pl.ds(pl.multiple_of(k * BS, BS), BS)
                lanes = pl.ds(pl.multiple_of((n >> 1) * 128, 128), 128)
                panels[i][rows, lanes] = panels[i][rows, lanes] + value
        return carry

    lax.fori_loop(0, PAIRS, place, 0, unroll=2)


def clear_and_swap(blocks, panels, swapped):
    swap = half_swap()
    for i, (ref, top) in enumerate(blocks):
        panels[i][...] = jnp.zeros_like(panels[i])
        swapped[i][...] = jnp.dot(
            ref[top : top + BODY, :], swap, preferred_element_type=jnp.float32
        ).astype(jnp.bfloat16)


def early_kernel(mine, one, two, out, where, places, sem, sems, *scratch):
    panels, swapped = scratch[:EARLY], scratch[EARLY:]
    blocks = ((mine, 0), (one, 0), (one, MSG), (two, 0), (two, MSG))
    copy = read_places(blocks, where, places, sem)
    copies = [pltpu.make_async_copy(panels[j], out.at[j], sems.at[j]) for j in range(EARLY)]
    for lo, hi in ((0, 3), (3, EARLY)):
        clear_and_swap(blocks[lo:hi], panels[lo:hi], swapped[lo:hi])
        if lo == 0:
            copy.wait()
        place_slots(blocks[lo:hi], lo, panels[lo:hi], swapped[lo:hi], places)
        for j in range(lo, hi):
            copies[j].start()
    for c in copies:
        c.wait()


def early(mine, one, two):
    vmem = pl.BlockSpec(memory_space=pltpu.VMEM)
    return pl.pallas_call(
        early_kernel,
        out_shape=jax.ShapeDtypeStruct((EARLY, DEPTH, WIDTH), jnp.bfloat16),
        in_specs=[vmem] * 3,
        out_specs=pl.BlockSpec(memory_space=pl.ANY),
        scratch_shapes=[
            pltpu.VMEM((16, 128), jnp.int32),
            pltpu.SMEM((16, 128), jnp.int32),
            pltpu.SemaphoreType.DMA,
            pltpu.SemaphoreType.DMA((EARLY,)),
        ]
        + [pltpu.VMEM((DEPTH, WIDTH), jnp.bfloat16)] * EARLY
        + [pltpu.VMEM((BODY, 128), jnp.bfloat16)] * EARLY,
        compiler_params=pltpu.CompilerParams(vmem_limit_bytes=24 * 1024 * 1024),
        cost_estimate=pl.CostEstimate(flops=0, bytes_accessed=EARLY_COST, transcendentals=0),
    )(mine, one, two)


def multiply_kernel(pieces, ready, three, four, out, left, total, where, places, sem, sems, *scratch):
    panels, swapped = scratch[:8], scratch[8:]
    blocks = ((three, 0), (three, MSG), (four, 0))
    y = lax.axis_index("y")
    core = lax.axis_index("core")
    copies = [pltpu.make_async_copy(ready.at[j], panels[j], sems.at[j]) for j in range(EARLY)]
    for c in copies:
        c.start()
    copy = read_places(blocks, where, places, sem)

    swap = half_swap()
    lane = lax.broadcasted_iota(jnp.int32, (BS, 128), 1)
    upper = (lane >= BS).astype(jnp.float32)
    for m, at in ((0, core), (1, 1 - core)):
        rows = pl.ds(pl.multiple_of(at * BS, BS), BS)
        for c in range(N_COL):
            here = pieces[c, m * BS : (m + 1) * BS, :]
            marks = pieces[c, 2 * BS :, :]
            there = jnp.dot(here, swap, preferred_element_type=jnp.float32)
            k_there = jnp.dot(marks, swap, preferred_element_type=jnp.float32)[m : m + 1]
            here = here.astype(jnp.float32)
            k_here = marks.astype(jnp.float32)[m : m + 1]
            for g in range(PIECE // 2):
                want = upper + 2.0 * g
                value = jnp.where(k_here == want, here, 0.0) + jnp.where(k_there == want, there, 0.0)
                at_lane = (c * PIECE + 2 * g) * BS
                left[rows, at_lane : at_lane + 128] = value.astype(jnp.bfloat16)

    clear_and_swap(blocks, panels[EARLY:], swapped)
    copy.wait()
    place_slots(blocks, 0, panels[EARLY:], swapped, places)
    for j in range(8):
        if j < EARLY:
            copies[j].wait()
        chip = lax.rem(y + N_Y + jnp.where(core == 0, -STEPS[j], STEPS[j]), N_Y)
        owner = chip * 2 + (1 - core if OTHER[j] else core)
        at = pl.ds(pl.multiple_of(owner * DEPTH, 128), DEPTH)
        part = jnp.dot(left[:, at], panels[j][...], preferred_element_type=jnp.float32)
        total[...] = part if j == 0 else total[...] + part
    share = WIDTH // N_LAYER
    for m in range(2):
        for s in range(N_LAYER):
            out[m * N_LAYER + s] = total[m * BS : (m + 1) * BS, s * share : (s + 1) * share].astype(
                jnp.bfloat16
            )


def multiply(pieces, ready, three, four):
    vmem = pl.BlockSpec(memory_space=pltpu.VMEM)
    return pl.pallas_call(
        multiply_kernel,
        out_shape=jax.ShapeDtypeStruct((2 * N_LAYER, BS, WIDTH // N_LAYER), jnp.bfloat16),
        in_specs=[vmem, pl.BlockSpec(memory_space=pl.ANY), vmem, vmem],
        out_specs=vmem,
        scratch_shapes=[
            pltpu.VMEM((2 * BS, NB // N_LAYER * BS), jnp.bfloat16),
            pltpu.VMEM((2 * BS, WIDTH), jnp.float32),
            pltpu.VMEM((16, 128), jnp.int32),
            pltpu.SMEM((16, 128), jnp.int32),
            pltpu.SemaphoreType.DMA,
            pltpu.SemaphoreType.DMA((EARLY,)),
        ]
        + [pltpu.VMEM((DEPTH, WIDTH), jnp.bfloat16)] * 8
        + [pltpu.VMEM((BODY, 128), jnp.bfloat16)] * (8 - EARLY),
        compiler_params=pltpu.CompilerParams(vmem_limit_bytes=32 * 1024 * 1024),
        cost_estimate=pl.CostEstimate(
            flops=2 * 128 * 3072 * 2048, bytes_accessed=16 << 20, transcendentals=0
        ),
    )(pieces, ready, three, four)


def around(distance):
    return [
        (2 * i + c, 2 * ((i + (distance if c == 0 else -distance)) % N_Y) + c)
        for i in range(N_Y)
        for c in (0, 1)
    ]


def shards(left_blocks, left_coords, right_blocks, right_coords):
    axes = ("y", "core")
    mine = pack(
        right_blocks.reshape(SLOTS, BS, BS),
        right_coords.reshape(SLOTS, 2).T,
        left_blocks.reshape(2, BS, BS),
        left_coords.reshape(2, 2),
    )
    theirs = lax.ppermute(mine, axes, [(i, i ^ 1) for i in range(2 * N_Y)])
    both = jnp.concatenate([mine[:MSG], theirs[:MSG]], axis=0)
    one = lax.ppermute(both, axes, around(1))
    two = lax.ppermute(both, axes, around(2))
    pieces = lax.all_to_all(spread(mine, theirs), "col", 0, 0)
    three = lax.ppermute(two, axes, around(1))
    four = lax.ppermute(two[:MSG], axes, around(2))
    part = multiply(pieces, early(mine, one, two), three, four)
    parts = lax.all_to_all(part, ("core", "layer"), 0, 0)
    total = jnp.sum(parts.astype(jnp.float32), axis=0)
    return total.reshape(1, BS, COLUMNS // N_LAYER, BS)


def solution(mesh):
    grid = Mesh(mesh.devices.reshape(N_Y, 2, N_COL, N_LAYER), ("y", "core", "col", "layer"))
    row = ("y", "core")
    return jax.shard_map(
        shards,
        mesh=grid,
        in_specs=(
            P(row, "col", "layer", None, None, None),
            P(row, "col", "layer", None, None),
            P(row, "col", "layer", None, None, None),
            P(row, "col", "layer", None, None),
        ),
        out_specs=P(row, None, ("col", "layer"), None),
        check_vma=False,
    )
```

time: 83.1 us -> 86.9 us (1.046)
  starting transfers between devices: 46.6 us -> 35.3 us
  waiting for transfers between devices: 3.71 us -> 11.8 us
  local copies, waits for them, and re-layouts: 4.12 us -> 8.81 us
  Pallas kernels: 10.2 us -> 13.9 us
  blocking collectives: 17.2 us -> 15.9 us
    ppermute x9 -> x5, starting transfers between devices: 37.6 us -> 29.3 us  [the longest x1 12.4 us: shards(): theirs = lax.ppermute(mine, axes, [(i, i ^ 1) for i in range(2 * N_Y)])]
    ppermute x9 -> x5, waiting for transfers between devices: 3.71 us -> 11.8 us  [the longest x1 8.91 us: shards(): two = lax.ppermute(both, axes, around(2))]
    pallas_call x0 -> x3, Pallas kernels: none -> 7.38 us  [the longest x1 3.54 us: early(): pl.pallas_call(early_kernel, out_shape=jax.ShapeDtypeStruct((EARLY, DEPTH...]
    unnamed x6 -> x8, local copies, waits for them, and re-layouts: 1.35 us -> 7.01 us
    pallas_call x1, Pallas kernels: 10.2 us -> 6.53 us  [multiply(): pl.pallas_call(multiply_kernel, out_shape=jax.ShapeDtypeStruct((2 * N_LAY...]
    all_to_all x1, starting transfers between devices: 9.04 us -> 6 us  [shards(): pieces = lax.all_to_all(spread(mine, theirs), 'col', 0, 0)]
    all_to_all x1, blocking collectives: 17.2 us -> 15.9 us  [shards(): parts = lax.all_to_all(part, ('core', 'layer'), 0, 0)]
    broadcast_in_dim x4 -> x0, local copies, waits for them, and re-layouts: 0.9 us -> none  [the longest x1 0.73 us: shards(): jnp.broadcast_to(piece[None], (N_COL, LMSG, 128))]
  transfers between devices with their start and end apart: 10 -> 6, of which waited for: 4 -> 3; matrix products, arithmetic and copies ran while one was open for 1% -> 1% of each run, Pallas kernels for 0% -> 4%
where the time goes in v2:
time: 86.9 us; the launch traced here: 86 us
  starting transfers between devices  35.3 us (41%)
  blocking collectives  15.9 us (18%)
  Pallas kernels  13.9 us (16%)
  waiting for transfers between devices  11.8 us (14%)
  local copies, waits for them, and re-layouts  8.81 us (10%)
    all_to_all x1, blocking collectives, shards(): parts = lax.all_to_all(part, ('core', 'layer'), 0, 0)  15.9 us
    ppermute x1, starting transfers between devices, shards(): theirs = lax.ppermute(mine, axes, [(i, i ^ 1) for i in range(2 * N_Y)])  12.4 us
    ppermute x1, waiting for transfers between devices, shards(): two = lax.ppermute(both, axes, around(2))  8.91 us
    unnamed x8, local copies, waits for them, and re-layouts  7.01 us
    pallas_call x1, Pallas kernels, multiply(): pl.pallas_call(multiply_kernel, out_shape=jax.ShapeDtypeStruct((2 * N_LAY...  6.53 us
    ppermute x1, starting transfers between devices, shards(): two = lax.ppermute(both, axes, around(2))  6.01 us
    all_to_all x1, starting transfers between devices, shards(): pieces = lax.all_to_all(spread(mine, theirs), 'col', 0, 0)  6 us
    ppermute x1, starting transfers between devices, shards(): three = lax.ppermute(two, axes, around(1))  4.2 us
  transfers between devices with their start and end apart: 6, of which 3 were waited for; matrix products, arithmetic and copies ran while one was open for 1% of the time, Pallas kernels for 4%

profile of v2, /device:TPU:1, one launch (start us, length us, event | category | flops | bytes accessed | tf_op | source)
XLA Modules:
  0.0 86.0 jit_solution(18285948602483634030)
XLA Ops:
  0.0 1.9 %shard_map.46.mine = bf16[1120,128]{1,0:T(8,128)(2,1)} custom-call(bf16[32,64,64]{2,1,0:T(8,128)(2,1)} %bitcast.6, s32[2,32]{1,0:T(2,128)} %bitcast.8, bf16[2,64,64]{2,1,0:T(8,128)(2,1)} %bitcast.7, s32[2,2]{1,0:T(2,128)} %bitcast.9), custom_call_target="tpu_custom_call" | custom-call | bytes 1048576 | tf_op jit(solution)/shard_map/pallas_call | solution.py:53
  1.9 12.4 %collective-permute-start = (bf16[1120,128]{1,0:T(8,128)(2,1)}, bf16[1120,128]{1,0:T(8,128)(2,1)S(1)}, u32[]{:S(2)}, u32[]{:S(2)}) collective-permute-start(bf16[1120,128]{1,0:T(8,128)(2,1)} %shard_map.46.mine), channel_id=1, source_target_pairs={{0,48},{48,0},{96,144},{144,96},{192,240},{240,192},{288,336},{336... | collective-permute-start | bytes 860168 | tf_op jit(solution)/shard_map/ppermute | solution.py:254
  14.3 1.0 %slice.12 = bf16[1040,128]{1,0:T(8,128)(2,1)S(1)} slice(bf16[1120,128]{1,0:T(8,128)(2,1)} %shard_map.46.mine), slice={[0:1040], [0:128]} | slice | bytes 532480 | tf_op jit(solution)/shard_map/slice | solution.py:255
  15.3 0.4 collective-permute-done.theirs
  15.7 0.0 copy-start.3
  15.7 0.7 copy-done.3
  16.4 1.9 %shard_map.47 = bf16[12,144,128]{2,1,0:T(8,128)(2,1)} custom-call(bf16[1120,128]{1,0:T(8,128)(2,1)} %shard_map.46.mine, bf16[1120,128]{1,0:T(8,128)(2,1)} %copy-done.3), custom_call_target="tpu_custom_call" | custom-call | bytes 1048576 | tf_op jit(solution)/shard_map/pallas_call | solution.py:76
  18.4 0.0 slice-start
  18.4 6.0 %all-to-all-start = ((bf16[12,144,128]{2,1,0:T(8,128)(2,1)}), bf16[12,144,128]{2,1,0:T(8,128)(2,1)S(1)}, u32[]{:S(2)}, u32[]{:S(2)}) async-start(bf16[12,144,128]{2,1,0:T(8,128)(2,1)} %shard_map.47), calls=%async_computation | async-start | bytes 884736 | tf_op jit(solution)/shard_map/all_to_all | solution.py:258
  24.4 0.0 copy-start.2
  24.4 0.0 slice-done
  24.4 6.0 %collective-permute-start.2 = (bf16[2080,128]{1,0:T(8,128)(2,1)S(1)}, bf16[2080,128]{1,0:T(8,128)(2,1)S(1)}, u32[]{:S(2)}, u32[]{:S(2)}) collective-permute-start(bf16[2080,128]{1,0:T(8,128)(2,1)S(1)} %pad_maximum_fusion), channel_id=1, source_target_pairs={{0,192},{48,624},{96,288},{144,720},{192,384},{240,48},{288,480},{... | collective-permute-start | bytes 1597448 | tf_op jit(solution)/shard_map/ppermute | solution.py:257
  30.5 3.0 %collective-permute-start.1 = (bf16[2080,128]{1,0:T(8,128)(2,1)S(1)}, bf16[2080,128]{1,0:T(8,128)(2,1)S(1)}, u32[]{:S(2)}, u32[]{:S(2)}) collective-permute-start(bf16[2080,128]{1,0:T(8,128)(2,1)S(1)} %pad_maximum_fusion), channel_id=1, source_target_pairs={{0,96},{48,720},{96,192},{144,48},{192,288},{240,144},{288,384},{3... | collective-permute-start | bytes 1597448 | tf_op jit(solution)/shard_map/ppermute | solution.py:256
  33.4 8.9 %collective-permute-done.2.two = bf16[2080,128]{1,0:T(8,128)(2,1)S(1)} collective-permute-done((bf16[2080,128]{1,0:T(8,128)(2,1)S(1)}, bf16[2080,128]{1,0:T(8,128)(2,1)S(1)}, u32[]{:S(2)}, u32[]{:S(2)}) %collective-permute-start.2) | collective-permute-done | bytes 532512 | tf_op jit(solution)/shard_map/ppermute | solution.py:257
  42.4 4.2 %collective-permute-start.3 = (bf16[2080,128]{1,0:T(8,128)(2,1)S(1)}, bf16[2080,128]{1,0:T(8,128)(2,1)S(1)}, u32[]{:S(2)}, u32[]{:S(2)}) collective-permute-start(bf16[2080,128]{1,0:T(8,128)(2,1)S(1)} %collective-permute-done.2.two), channel_id=1, source_target_pairs={{0,96},{48,720},{96,192},{144,48},{192,288},{240,144},{288,384},{3... | collective-permute-start | bytes 1597448 | tf_op jit(solution)/shard_map/ppermute | solution.py:259
  46.6 3.7 %collective-permute-start.4 = (bf16[1040,128]{1,0:T(8,128)(2,1)S(1)}, bf16[1040,128]{1,0:T(8,128)(2,1)S(1)}, u32[]{:S(2)}, u32[]{:S(2)}) collective-permute-start(bf16[1040,128]{1,0:T(8,128)(2,1)S(1)} %slice.14), channel_id=1, source_target_pairs={{0,192},{48,624},{96,288},{144,720},{192,384},{240,48},{288,480},{... | collective-permute-start | bytes 798728 | tf_op jit(solution)/shard_map/ppermute | solution.py:260
  50.3 0.0 collective-permute-done.1.one
  50.3 0.0 copy-done.2
  50.4 3.5 %shard_map.48.ready = bf16[5,384,2048]{2,1,0:T(8,128)(2,1)S(1)} custom-call(bf16[1120,128]{1,0:T(8,128)(2,1)S(1)} %copy-done.2, bf16[2080,128]{1,0:T(8,128)(2,1)S(1)} %collective-permute-done.1.one, bf16[2080,128]{1,0:T(8,128)(2,1)S(1)} %collective-permute-done.2.two), custom_call_target="tpu_custom_call" | custom-call | bytes 67108864 | tf_op jit(solution)/shard_map/pallas_call | solution.py:149
  53.9 0.0 copy-start
  53.9 3.1 %copy-done = bf16[5,384,2048]{2,1,0:T(8,128)(2,1)} copy-done((bf16[5,384,2048]{2,1,0:T(8,128)(2,1)}, bf16[5,384,2048]{2,1,0:T(8,128)(2,1)S(1)}, u32[]{:S(2)}) %copy-start) | copy-done | bytes 7864344
  57.0 2.5 %collective-permute-done.4.four = bf16[1040,128]{1,0:T(8,128)(2,1)S(1)} collective-permute-done((bf16[1040,128]{1,0:T(8,128)(2,1)S(1)}, bf16[1040,128]{1,0:T(8,128)(2,1)S(1)}, u32[]{:S(2)}, u32[]{:S(2)}) %collective-permute-start.4) | collective-permute-done | bytes 266272 | tf_op jit(solution)/shard_map/ppermute | solution.py:260
  59.5 0.0 collective-permute-done.3.three
  59.5 0.0 all-to-all-done.pieces
  59.5 0.0 copy-start.1
  59.5 3.2 %copy-done.1 = bf16[5,384,2048]{2,1,0:T(8,128)(2,1)S(1)} copy-done((bf16[5,384,2048]{2,1,0:T(8,128)(2,1)S(1)}, bf16[5,384,2048]{2,1,0:T(8,128)(2,1)}, u32[]{:S(2)}) %copy-start.1) | copy-done | bytes 7864344
  62.7 6.5 %shard_map.49 = bf16[8,64,512]{2,1,0:T(8,128)(2,1)S(1)} custom-call(bf16[12,144,128]{2,1,0:T(8,128)(2,1)S(1)} %all-to-all-done.pieces, bf16[5,384,2048]{2,1,0:T(8,128)(2,1)S(1)} %copy-done.1, bf16[2080,128]{1,0:T(8,128)(2,1)S(1)} %collective-permute-done.3.three, bf16[1040,128]{1,0:T(8,128)(2,1)S(1)} %collective-permute-done.4.four), custom_call_target="tpu_custom_call" | custom-call | flops 1610612736 | bytes 16777216 | tf_op jit(solution)/shard_map/pallas_call | solution.py:216
  69.2 15.9 %all_to_all.10 = bf16[8,64,512]{2,1,0:T(8,128)(2,1)S(1)} all-to-all(bf16[8,64,512]{2,1,0:T(8,128)(2,1)S(1)} %shard_map.49), channel_id=1, replica_groups=mesh['y'=8,'core'=2,'col'=12,'layer'=4] {'core','layer'}, dimensions={0} | all-to-all | bytes 1048576 | tf_op jit(solution)/shard_map/all_to_all | solution.py:262
  85.1 0.1 convert_reduce_fusion
  85.2 0.8 reshape.19
  (2 shorter events, 0.1 us)
Async XLA Ops:
  1.9 13.8 %collective-permute-start = (bf16[1120,128]{1,0:T(8,128)(2,1)}, bf16[1120,128]{1,0:T(8,128)(2,1)S(1)}, u32[]{:S(2)}, u32[]{:S(2)}) collective-permute-start(bf16[1120,128]{1,0:T(8,128)(2,1)} %shard_map.46.mine), channel_id=1, source_target_pairs={{0,48},{48,0},{96,144},{144,96},{192,240},{240,192},{288,336},{336... | collective-permute-start | bytes 860168 | tf_op jit(solution)/shard_map/ppermute | solution.py:254
  15.7 0.7 copy-start.3
  18.4 6.0 %slice-start = ((bf16[1120,128]{1,0:T(8,128)(2,1)}), bf16[1040,128]{1,0:T(8,128)(2,1)S(1)}, s32[]{:S(2)}) async-start(bf16[1120,128]{1,0:T(8,128)(2,1)} %copy-done.3), calls=%async_computation.2 | async-start | bytes 532480 | tf_op jit(solution)/shard_map/slice | solution.py:255
  18.4 41.1 %all-to-all-start = ((bf16[12,144,128]{2,1,0:T(8,128)(2,1)}), bf16[12,144,128]{2,1,0:T(8,128)(2,1)S(1)}, u32[]{:S(2)}, u32[]{:S(2)}) async-start(bf16[12,144,128]{2,1,0:T(8,128)(2,1)} %shard_map.47), calls=%async_computation | async-start | bytes 884736 | tf_op jit(solution)/shard_map/all_to_all | solution.py:258
  24.4 26.0 %copy-start.2 = (bf16[1120,128]{1,0:T(8,128)(2,1)S(1)}, bf16[1120,128]{1,0:T(8,128)(2,1)}, u32[]{:S(2)}) copy-start(bf16[1120,128]{1,0:T(8,128)(2,1)} %shard_map.46.mine) | copy-start | bytes 860164
  24.4 17.9 %collective-permute-start.2 = (bf16[2080,128]{1,0:T(8,128)(2,1)S(1)}, bf16[2080,128]{1,0:T(8,128)(2,1)S(1)}, u32[]{:S(2)}, u32[]{:S(2)}) collective-permute-start(bf16[2080,128]{1,0:T(8,128)(2,1)S(1)} %pad_maximum_fusion), channel_id=1, source_target_pairs={{0,192},{48,624},{96,288},{144,720},{192,384},{240,48},{288,480},{... | collective-permute-start | bytes 1597448 | tf_op jit(solution)/shard_map/ppermute | solution.py:257
  30.5 19.9 %collective-permute-start.1 = (bf16[2080,128]{1,0:T(8,128)(2,1)S(1)}, bf16[2080,128]{1,0:T(8,128)(2,1)S(1)}, u32[]{:S(2)}, u32[]{:S(2)}) collective-permute-start(bf16[2080,128]{1,0:T(8,128)(2,1)S(1)} %pad_maximum_fusion), channel_id=1, source_target_pairs={{0,96},{48,720},{96,192},{144,48},{192,288},{240,144},{288,384},{3... | collective-permute-start | bytes 1597448 | tf_op jit(solution)/shard_map/ppermute | solution.py:256
  42.4 17.1 %collective-permute-start.3 = (bf16[2080,128]{1,0:T(8,128)(2,1)S(1)}, bf16[2080,128]{1,0:T(8,128)(2,1)S(1)}, u32[]{:S(2)}, u32[]{:S(2)}) collective-permute-start(bf16[2080,128]{1,0:T(8,128)(2,1)S(1)} %collective-permute-done.2.two), channel_id=1, source_target_pairs={{0,96},{48,720},{96,192},{144,48},{192,288},{240,144},{288,384},{3... | collective-permute-start | bytes 1597448 | tf_op jit(solution)/shard_map/ppermute | solution.py:259
  46.6 12.9 %collective-permute-start.4 = (bf16[1040,128]{1,0:T(8,128)(2,1)S(1)}, bf16[1040,128]{1,0:T(8,128)(2,1)S(1)}, u32[]{:S(2)}, u32[]{:S(2)}) collective-permute-start(bf16[1040,128]{1,0:T(8,128)(2,1)S(1)} %slice.14), channel_id=1, source_target_pairs={{0,192},{48,624},{96,288},{144,720},{192,384},{240,48},{288,480},{... | collective-permute-start | bytes 798728 | tf_op jit(solution)/shard_map/ppermute | solution.py:260
  53.9 3.1 %copy-start = (bf16[5,384,2048]{2,1,0:T(8,128)(2,1)}, bf16[5,384,2048]{2,1,0:T(8,128)(2,1)S(1)}, u32[]{:S(2)}) copy-start(bf16[5,384,2048]{2,1,0:T(8,128)(2,1)S(1)} %shard_map.48.ready) | copy-start | bytes 23592964
  59.5 3.2 %copy-start.1 = (bf16[5,384,2048]{2,1,0:T(8,128)(2,1)S(1)}, bf16[5,384,2048]{2,1,0:T(8,128)(2,1)}, u32[]{:S(2)}) copy-start(bf16[5,384,2048]{2,1,0:T(8,128)(2,1)} %copy-done) | copy-start | bytes 23592964

commit v3 on v2

v3 whole, which is shorter than its diff:
```python
import jax
import jax.numpy as jnp
from jax import lax
from jax.experimental import pallas as pl
from jax.experimental.pallas import tpu as pltpu
from jax.sharding import Mesh
from jax.sharding import PartitionSpec as P

NB = 384
BS = 64
N_YH = 4
N_COL = 12
N_LAYER = 4
SLOTS = 32
PAIRS = SLOTS // 2
BODY = PAIRS * BS
MSG = BODY + 16
LMSG = BS + 16
INNER = 6
COLUMNS = NB // N_COL
PIECE = NB // N_LAYER // N_COL
DEPTH = INNER * BS
WIDTH = COLUMNS * BS
GROUP = 4
WINDOW = 2 * PIECE * BS


def pack_kernel(right, right_where, left, left_where, out, piece, tail):
    y = lax.axis_index("yh") * 2 + lax.axis_index("yl")
    core = lax.axis_index("core")
    col = lax.axis_index("col")
    base = lax.axis_index("layer") * (NB // N_LAYER)
    for p in range(PAIRS):
        pair = jnp.concatenate([right[p], right[p + PAIRS]], axis=-1)
        for q in range(N_YH):
            out[q, p * BS : (p + 1) * BS, :] = pair
    tail[...] = jnp.zeros_like(tail)
    inner = right_where[0:1, :] - (base + (y * 2 + core) * INNER)
    column = right_where[1:2, :] - col * COLUMNS
    tail[0:1, 0:SLOTS] = inner.astype(jnp.float32)
    tail[1:2, 0:SLOTS] = column.astype(jnp.float32)
    for q in range(N_YH):
        out[q, BODY:MSG, :] = tail[...].astype(jnp.bfloat16)
    lane = lax.broadcasted_iota(jnp.int32, (16, 128), 1)
    first = jnp.broadcast_to(left_where[0:1, 1:2], (16, 128))
    second = jnp.broadcast_to(left_where[1:2, 1:2], (16, 128))
    at = jnp.where(lane < BS, first, second) - (base + col * PIECE)
    at = at.astype(jnp.float32).astype(jnp.bfloat16)
    pair = jnp.concatenate([left[0], left[1]], axis=-1)
    piece[:BS, :] = pair
    piece[BS:, :] = at


def pack(right, right_where, left, left_where):
    vmem = pl.BlockSpec(memory_space=pltpu.VMEM)
    return pl.pallas_call(
        pack_kernel,
        out_shape=(
            jax.ShapeDtypeStruct((N_YH, MSG, 128), jnp.bfloat16),
            jax.ShapeDtypeStruct((LMSG, 128), jnp.bfloat16),
        ),
        in_specs=[vmem] * 4,
        out_specs=(vmem, vmem),
        scratch_shapes=[pltpu.VMEM((16, 128), jnp.float32)],
        cost_estimate=pl.CostEstimate(flops=0, bytes_accessed=2 << 20, transcendentals=0),
    )(right, right_where, left, left_where)


def half_swap():
    to = lax.broadcasted_iota(jnp.int32, (128, 128), 1)
    frm = lax.broadcasted_iota(jnp.int32, (128, 128), 0)
    return (to == (frm + BS) % 128).astype(jnp.bfloat16)


def read_places(blocks, where, places, sem):
    for i, block in enumerate(blocks):
        tail = block[BODY:MSG, :].astype(jnp.float32).astype(jnp.int32)
        where[2 * i : 2 * i + 2, :] = tail[0:2, :]
    copy = pltpu.make_async_copy(where, places, sem)
    copy.start()
    return copy


def place_slots(blocks, first, panels, swapped, places):
    lane = lax.broadcasted_iota(jnp.int32, (BS, 128), 1)
    low = (lane < BS).astype(jnp.bfloat16)
    high = (lane >= BS).astype(jnp.bfloat16)

    def place(p, carry):
        at = pl.ds(pl.multiple_of(p * BS, BS), BS)
        for half in range(2):
            for i, block in enumerate(blocks):
                k = places[2 * (first + i), p + half * PAIRS]
                n = places[2 * (first + i) + 1, p + half * PAIRS]
                odd = n & 1
                value = jnp.where(odd == half, block[at, :], swapped[i][at, :])
                value = value * jnp.where(odd == 1, high, low)
                rows = pl.ds(pl.multiple_of(k * BS, BS), BS)
                lanes = pl.ds(pl.multiple_of((n >> 1) * 128, 128), 128)
                panels[i][rows, lanes] = panels[i][rows, lanes] + value
        return carry

    lax.fori_loop(0, PAIRS, place, 0, unroll=2)


def place_kernel(own, other, left_own, left_other, out, left, total, where, places, sem, *scratch):
    panels, swapped = scratch[:GROUP], scratch[GROUP:]
    yl = lax.axis_index("yl")
    core = lax.axis_index("core")
    blocks = [own.at[q] for q in range(N_YH)] + [other.at[q] for q in range(N_YH)]
    copy = read_places(blocks, where, places, sem)
    swap = half_swap()

    lane = lax.broadcasted_iota(jnp.int32, (BS, 128), 1)
    upper = (lane >= BS).astype(jnp.float32)
    for src, at in ((left_own, yl), (left_other, 1 - yl)):
        rows = pl.ds(pl.multiple_of(at * BS, BS), BS)
        for q in range(N_YH):
            for u in range(2):
                whole = src[3 * q + yl + u] if src is left_own else src[2 * q + u]
                there = jnp.dot(whole, swap, preferred_element_type=jnp.float32)
                here = whole.astype(jnp.float32)
                for g in range(PIECE // 2):
                    want = upper + 2.0 * g
                    value = jnp.where(here[BS : BS + 1] == want, here[:BS], 0.0)
                    value = value + jnp.where(there[BS : BS + 1] == want, there[:BS], 0.0)
                    at_lane = q * WINDOW + (u * PIECE + 2 * g) * BS
                    left[rows, at_lane : at_lane + 128] = value.astype(jnp.bfloat16)

    for j0 in range(0, 2 * N_YH, GROUP):
        now = blocks[j0 : j0 + GROUP]
        for i, block in enumerate(now):
            panels[i][...] = jnp.zeros_like(panels[i])
            swapped[i][...] = jnp.dot(
                block[:BODY, :], swap, preferred_element_type=jnp.float32
            ).astype(jnp.bfloat16)
        if j0 == 0:
            copy.wait()
        place_slots(now, j0, panels, swapped, places)
        for i in range(len(now)):
            j = j0 + i
            side = core if j < N_YH else 1 - core
            start = (j % N_YH) * WINDOW + yl * (4 * BS) + side * DEPTH
            at = pl.ds(pl.multiple_of(start, 128), DEPTH)
            part = jnp.dot(left[:, at], panels[i][...], preferred_element_type=jnp.float32)
            total[...] = part if j == 0 else total[...] + part
    share = WIDTH // N_LAYER
    for m in range(2):
        for s in range(N_LAYER):
            out[m * N_LAYER + s] = total[m * BS : (m + 1) * BS, s * share : (s + 1) * share].astype(
                jnp.bfloat16
            )


def multiply(*operands):
    vmem = pl.BlockSpec(memory_space=pltpu.VMEM)
    return pl.pallas_call(
        place_kernel,
        out_shape=jax.ShapeDtypeStruct((2 * N_LAYER, BS, WIDTH // N_LAYER), jnp.bfloat16),
        in_specs=[vmem] * len(operands),
        out_specs=vmem,
        scratch_shapes=[
            pltpu.VMEM((2 * BS, N_YH * WINDOW), jnp.bfloat16),
            pltpu.VMEM((2 * BS, WIDTH), jnp.float32),
            pltpu.VMEM((16, 128), jnp.int32),
            pltpu.SMEM((16, 128), jnp.int32),
            pltpu.SemaphoreType.DMA,
        ]
        + [pltpu.VMEM((DEPTH, WIDTH), jnp.bfloat16)] * GROUP
        + [pltpu.VMEM((BODY, 128), jnp.bfloat16)] * GROUP,
        compiler_params=pltpu.CompilerParams(vmem_limit_bytes=24 * 1024 * 1024),
        cost_estimate=pl.CostEstimate(
            flops=2 * 128 * 3072 * 2048, bytes_accessed=4 << 20, transcendentals=0
        ),
    )(*operands)


def nothing_kernel(whole, when, out):
    pass


def after(whole, when):
    return pl.pallas_call(
        nothing_kernel,
        out_shape=jax.ShapeDtypeStruct(whole.shape, whole.dtype),
        in_specs=[pl.BlockSpec(memory_space=pl.ANY)] * 2,
        out_specs=pl.BlockSpec(memory_space=pl.ANY),
        input_output_aliases={0: 0},
    )(whole, when)


def shards(left_blocks, left_coords, right_blocks, right_coords):
    mine, piece = pack(
        right_blocks.reshape(SLOTS, BS, BS),
        right_coords.reshape(SLOTS, 2).T,
        left_blocks.reshape(2, BS, BS),
        left_coords.reshape(2, 2),
    )
    yl = lax.axis_index("yl")
    own = lax.all_to_all(mine, "yh", 0, 0)
    pieces = lax.all_gather(piece, "col")
    wanted = lax.dynamic_slice_in_dim(pieces.reshape(N_YH, 3, LMSG, 128), 1 - yl, 2, 1)
    wanted = wanted.reshape(2 * N_YH, LMSG, 128)
    other = lax.ppermute(after(own, pieces), "core", [(0, 1), (1, 0)])
    pieces_other = lax.ppermute(wanted, "yl", [(0, 1), (1, 0)])
    part = multiply(own, other, pieces, pieces_other)
    parts = lax.all_to_all(part, ("yl", "layer"), 0, 0)
    total = jnp.sum(parts.astype(jnp.float32), axis=0)
    return total.reshape(1, BS, COLUMNS // N_LAYER, BS)


def solution(mesh):
    grid = Mesh(mesh.devices.reshape(N_YH, 2, 2, N_COL, N_LAYER), ("yh", "yl", "core", "col", "layer"))
    row = ("yh", "yl", "core")
    return jax.shard_map(
        shards,
        mesh=grid,
        in_specs=(
            P(row, "col", "layer", None, None, None),
            P(row, "col", "layer", None, None),
            P(row, "col", "layer", None, None, None),
            P(row, "col", "layer", None, None),
        ),
        out_specs=P(row, None, ("col", "layer"), None),
        check_vma=False,
    )
```

time: 86.9 us -> 78.7 us (0.906)
  the two profiles are of different devices: /device:TPU:1 before, /device:TPU:16 now
where the time goes in v3:
time: 78.7 us; the launch traced here: 78.4 us
  blocking collectives  44 us (56%)
  starting transfers between devices  17.6 us (22%)
  Pallas kernels  8.95 us (11%)
  waiting for transfers between devices  5.91 us (8%)
  local copies, waits for them, and re-layouts  1.81 us (2%)
    all_gather x1, blocking collectives, shards(): pieces = lax.all_gather(piece, 'col')  29.8 us
    all_to_all x1, blocking collectives, shards(): parts = lax.all_to_all(part, ('yl', 'layer'), 0, 0)  14.2 us
    all_to_all x1, starting transfers between devices, shards(): own = lax.all_to_all(mine, 'yh', 0, 0)  13 us
    pallas_call x1, Pallas kernels, multiply(): pl.pallas_call(place_kernel, out_shape=jax.ShapeDtypeStruct((2 * N_LAYER,...  6.69 us
    ppermute x1, waiting for transfers between devices, shards(): pieces_other = lax.ppermute(wanted, 'yl', [(0, 1), (1, 0)])  5.9 us
    ppermute x1, starting transfers between devices, shards(): pieces_other = lax.ppermute(wanted, 'yl', [(0, 1), (1, 0)])  2.59 us
    pallas_call x1, Pallas kernels, pack(): pl.pallas_call(pack_kernel, out_shape=(jax.ShapeDtypeStruct((N_YH, MSG, 1...  2.26 us
    ppermute x1, starting transfers between devices, shards(): other = lax.ppermute(after(own, pieces), 'core', [(0, 1), (1, 0)])  2.04 us
  transfers between devices with their start and end apart: 3, of which 1 were waited for; matrix products, arithmetic and copies ran while one was open for 0% of the time, Pallas kernels for 0%

profile of v3, /device:TPU:16, one launch (start us, length us, event | category | flops | bytes accessed | tf_op | source)
XLA Modules:
  0.0 78.4 jit_solution(15125542537374718223)
XLA Ops:
  0.0 2.3 %shard_map.46 = (bf16[4,1040,128]{2,1,0:T(8,128)(2,1)}, bf16[80,128]{1,0:T(8,128)(2,1)}) custom-call(bf16[32,64,64]{2,1,0:T(8,128)(2,1)} %bitcast.12, s32[2,32]{1,0:T(2,128)} %bitcast.15, bf16[2,64,64]{2,1,0:T(8,128)(2,1)} %bitcast.14, s32[2,2]{1,0:T(2,128)} %bitcast.16), custom_call_target="tpu_custom_call" | custom-call | bytes 2097152 | tf_op jit(solution)/shard_map/pallas_call | solution.py:56
  2.3 0.0 copy-start.1
  2.3 13.0 %all-to-all-start = ((bf16[4,1040,128]{2,1,0:T(8,128)(2,1)}), bf16[4,1040,128]{2,1,0:T(8,128)(2,1)S(1)}, u32[]{:S(2)}, u32[]{:S(2)}) async-start(bf16[4,1040,128]{2,1,0:T(8,128)(2,1)} %get-tuple-element.7), calls=%async_computation | async-start | bytes 2129920 | tf_op jit(solution)/shard_map/all_to_all | solution.py:200
  15.2 0.0 copy-done.1
  15.2 29.8 %all-gather = bf16[960,128]{1,0:T(8,128)(2,1)} all-gather(bf16[80,128]{1,0:T(8,128)(2,1)S(1)} %copy-done.1), channel_id=2, replica_groups=mesh['yh'=4,'yl'=2,'core'=2,'col'=12,'layer'=4] {'col'}, dimensions={0}, use_global_device_ids=true | all-gather | bytes 266240 | tf_op jit(solution)/shard_map/all_gather | solution.py:201
  45.1 0.0 all-to-all-done.own
  45.1 1.0 %copy.6.whole = bf16[4,1040,128]{2,1,0:T(8,128)(2,1)} copy(bf16[4,1040,128]{2,1,0:T(8,128)(2,1)S(1)} %all-to-all-done.own) | data formatting | bytes 2129920
  46.1 0.0 copy-start
  46.1 2.0 %collective-permute-start = (bf16[4,1040,128]{2,1,0:T(8,128)(2,1)}, bf16[4,1040,128]{2,1,0:T(8,128)(2,1)S(1)}, u32[]{:S(2)}, u32[]{:S(2)}) collective-permute-start(bf16[4,1040,128]{2,1,0:T(8,128)(2,1)} %shard_map.47), channel_id=1, source_target_pairs={{0,48},{48,0},{1,49},{49,1},{2,50},{50,2},{3,51},{51,3},{4,52},{52... | collective-permute-start | bytes 3194888 | tf_op jit(solution)/shard_map/ppermute | solution.py:204
  48.1 0.0 copy-done
  48.1 2.6 %collective-permute-start.1 = (bf16[8,80,128]{2,1,0:T(8,128)(2,1)S(1)}, bf16[8,80,128]{2,1,0:T(8,128)(2,1)S(1)}, u32[]{:S(2)}, u32[]{:S(2)}) collective-permute-start(bf16[8,80,128]{2,1,0:T(8,128)(2,1)S(1)} %bitcast.13), channel_id=1, source_target_pairs={{0,96},{96,0},{1,97},{97,1},{2,98},{98,2},{3,99},{99,3},{4,100},{1... | collective-permute-start | bytes 491528 | tf_op jit(solution)/shard_map/ppermute | solution.py:205
  50.7 5.9 %collective-permute-done.1.left_other = bf16[8,80,128]{2,1,0:T(8,128)(2,1)S(1)} collective-permute-done((bf16[8,80,128]{2,1,0:T(8,128)(2,1)S(1)}, bf16[8,80,128]{2,1,0:T(8,128)(2,1)S(1)}, u32[]{:S(2)}, u32[]{:S(2)}) %collective-permute-start.1) | collective-permute-done | bytes 163872 | tf_op jit(solution)/shard_map/ppermute | solution.py:205
  56.6 0.0 collective-permute-done.other
  56.6 6.7 %shard_map.48 = bf16[8,64,512]{2,1,0:T(8,128)(2,1)S(1)} custom-call(bf16[4,1040,128]{2,1,0:T(8,128)(2,1)S(1)} %all-to-all-done.own, bf16[4,1040,128]{2,1,0:T(8,128)(2,1)S(1)} %collective-permute-done.other, bf16[12,80,128]{2,1,0:T(8,128)(2,1)S(1)} %bitcast.11, bf16[8,80,128]{2,1,0:T(8,128)(2,1)S(1)} %collective-permute-done.1.left_other), custom_call_target="tpu_custom_call" | custom-call | flops 1610612736 | bytes 4194304 | tf_op jit(solution)/shard_map/pallas_call | solution.py:157
  63.3 14.2 %all_to_all.10 = bf16[8,64,512]{2,1,0:T(8,128)(2,1)S(1)} all-to-all(bf16[8,64,512]{2,1,0:T(8,128)(2,1)S(1)} %shard_map.48), channel_id=1, replica_groups=mesh['yh'=4,'yl'=2,'core'=2,'col'=12,'layer'=4] {'yl','layer'}, dimensions={0} | all-to-all | bytes 1048576 | tf_op jit(solution)/shard_map/all_to_all | solution.py:207
  77.5 0.1 convert_reduce_fusion
  77.6 0.8 %reshape.27 = f32[1,64,8,64]{3,2,1,0:T(8,128)} reshape(f32[64,512]{1,0:T(8,128)S(1)} %convert_reduce_fusion) | data formatting | bytes 262144 | tf_op jit(solution)/shard_map/reshape | solution.py:209
  (2 shorter events, 0.0 us)
Async XLA Ops:
  2.3 13.0 %copy-start.1 = (bf16[80,128]{1,0:T(8,128)(2,1)S(1)}, bf16[80,128]{1,0:T(8,128)(2,1)}, u32[]{:S(2)}) copy-start(bf16[80,128]{1,0:T(8,128)(2,1)} %get-tuple-element.8) | copy-start | bytes 61444
  2.3 42.8 %all-to-all-start = ((bf16[4,1040,128]{2,1,0:T(8,128)(2,1)}), bf16[4,1040,128]{2,1,0:T(8,128)(2,1)S(1)}, u32[]{:S(2)}, u32[]{:S(2)}) async-start(bf16[4,1040,128]{2,1,0:T(8,128)(2,1)} %get-tuple-element.7), calls=%async_computation | async-start | bytes 2129920 | tf_op jit(solution)/shard_map/all_to_all | solution.py:200
  46.1 2.1 %copy-start = (bf16[960,128]{1,0:T(8,128)(2,1)S(1)}, bf16[960,128]{1,0:T(8,128)(2,1)}, u32[]{:S(2)}) copy-start(bf16[960,128]{1,0:T(8,128)(2,1)} %all-gather) | copy-start | bytes 737284
  46.1 10.6 %collective-permute-start = (bf16[4,1040,128]{2,1,0:T(8,128)(2,1)}, bf16[4,1040,128]{2,1,0:T(8,128)(2,1)S(1)}, u32[]{:S(2)}, u32[]{:S(2)}) collective-permute-start(bf16[4,1040,128]{2,1,0:T(8,128)(2,1)} %shard_map.47), channel_id=1, source_target_pairs={{0,48},{48,0},{1,49},{49,1},{2,50},{50,2},{3,51},{51,3},{4,52},{52... | collective-permute-start | bytes 3194888 | tf_op jit(solution)/shard_map/ppermute | solution.py:204
  48.1 8.5 %collective-permute-start.1 = (bf16[8,80,128]{2,1,0:T(8,128)(2,1)S(1)}, bf16[8,80,128]{2,1,0:T(8,128)(2,1)S(1)}, u32[]{:S(2)}, u32[]{:S(2)}) collective-permute-start(bf16[8,80,128]{2,1,0:T(8,128)(2,1)S(1)} %bitcast.13), channel_id=1, source_target_pairs={{0,96},{96,0},{1,97},{97,1},{2,98},{98,2},{3,99},{99,3},{4,100},{1... | collective-permute-start | bytes 491528 | tf_op jit(solution)/shard_map/ppermute | solution.py:205

commit v4 on v3

--- a/solution.py
+++ b/solution.py
@@ -31,16 +31,13 @@
     col = lax.axis_index("col")
     base = lax.axis_index("layer") * (NB // N_LAYER)
     for p in range(PAIRS):
-        pair = jnp.concatenate([right[p], right[p + PAIRS]], axis=-1)
-        for q in range(N_YH):
-            out[q, p * BS : (p + 1) * BS, :] = pair
+        out[p * BS : (p + 1) * BS, :] = jnp.concatenate([right[p], right[p + PAIRS]], axis=-1)
     tail[...] = jnp.zeros_like(tail)
     inner = right_where[0:1, :] - (base + (y * 2 + core) * INNER)
     column = right_where[1:2, :] - col * COLUMNS
     tail[0:1, 0:SLOTS] = inner.astype(jnp.float32)
     tail[1:2, 0:SLOTS] = column.astype(jnp.float32)
-    for q in range(N_YH):
-        out[q, BODY:MSG, :] = tail[...].astype(jnp.bfloat16)
+    out[BODY:MSG, :] = tail[...].astype(jnp.bfloat16)
     lane = lax.broadcasted_iota(jnp.int32, (16, 128), 1)
     first = jnp.broadcast_to(left_where[0:1, 1:2], (16, 128))
     second = jnp.broadcast_to(left_where[1:2, 1:2], (16, 128))
@@ -56,7 +53,7 @@
     return pl.pallas_call(
         pack_kernel,
         out_shape=(
-            jax.ShapeDtypeStruct((N_YH, MSG, 128), jnp.bfloat16),
+            jax.ShapeDtypeStruct((MSG, 128), jnp.bfloat16),
             jax.ShapeDtypeStruct((LMSG, 128), jnp.bfloat16),
         ),
         in_specs=[vmem] * 4,
@@ -103,11 +100,10 @@
     lax.fori_loop(0, PAIRS, place, 0, unroll=2)
 
 
-def place_kernel(own, other, left_own, left_other, out, left, total, where, places, sem, *scratch):
+def place_kernel(gathered, left_own, left_other, out, left, total, where, places, sem, *scratch):
     panels, swapped = scratch[:GROUP], scratch[GROUP:]
     yl = lax.axis_index("yl")
-    core = lax.axis_index("core")
-    blocks = [own.at[q] for q in range(N_YH)] + [other.at[q] for q in range(N_YH)]
+    blocks = [gathered.at[j] for j in range(2 * N_YH)]
     copy = read_places(blocks, where, places, sem)
     swap = half_swap()
 
@@ -139,8 +135,7 @@
         place_slots(now, j0, panels, swapped, places)
         for i in range(len(now)):
             j = j0 + i
-            side = core if j < N_YH else 1 - core
-            start = (j % N_YH) * WINDOW + yl * (4 * BS) + side * DEPTH
+            start = (j // 2) * WINDOW + yl * (4 * BS) + (j % 2) * DEPTH
             at = pl.ds(pl.multiple_of(start, 128), DEPTH)
             part = jnp.dot(left[:, at], panels[i][...], preferred_element_type=jnp.float32)
             total[...] = part if j == 0 else total[...] + part
@@ -175,20 +170,6 @@
     )(*operands)
 
 
-def nothing_kernel(whole, when, out):
-    pass
-
-
-def after(whole, when):
-    return pl.pallas_call(
-        nothing_kernel,
-        out_shape=jax.ShapeDtypeStruct(whole.shape, whole.dtype),
-        in_specs=[pl.BlockSpec(memory_space=pl.ANY)] * 2,
-        out_specs=pl.BlockSpec(memory_space=pl.ANY),
-        input_output_aliases={0: 0},
-    )(whole, when)
-
-
 def shards(left_blocks, left_coords, right_blocks, right_coords):
     mine, piece = pack(
         right_blocks.reshape(SLOTS, BS, BS),
@@ -197,13 +178,12 @@
         left_coords.reshape(2, 2),
     )
     yl = lax.axis_index("yl")
-    own = lax.all_to_all(mine, "yh", 0, 0)
+    gathered = lax.all_gather(mine, ("yh", "core"))
     pieces = lax.all_gather(piece, "col")
     wanted = lax.dynamic_slice_in_dim(pieces.reshape(N_YH, 3, LMSG, 128), 1 - yl, 2, 1)
     wanted = wanted.reshape(2 * N_YH, LMSG, 128)
-    other = lax.ppermute(after(own, pieces), "core", [(0, 1), (1, 0)])
     pieces_other = lax.ppermute(wanted, "yl", [(0, 1), (1, 0)])
-    part = multiply(own, other, pieces, pieces_other)
+    part = multiply(gathered, pieces, pieces_other)
     parts = lax.all_to_all(part, ("yl", "layer"), 0, 0)
     total = jnp.sum(parts.astype(jnp.float32), axis=0)
     return total.reshape(1, BS, COLUMNS // N_LAYER, BS)

time: 78.7 us -> 91.9 us (1.17)
  the two profiles are of different devices: /device:TPU:16 before, /device:TPU:1 now
where the time goes in v4:
time: 91.9 us; the launch traced here: 91.2 us
  blocking collectives  41.8 us (45%)
  waiting for transfers between devices  21.7 us (24%)
  between operations  13.4 us (15%)
  Pallas kernels  8.63 us (9%)
  starting transfers between devices  3.21 us (3%)
  local copies, waits for them, and re-layouts  2.42 us (3%)
    all_gather x1, blocking collectives, shards(): pieces = lax.all_gather(piece, 'col')  29.5 us
    ppermute x1, waiting for transfers between devices, shards(): pieces_other = lax.ppermute(wanted, 'yl', [(0, 1), (1, 0)])  12.5 us
    all_to_all x1, blocking collectives, shards(): parts = lax.all_to_all(part, ('yl', 'layer'), 0, 0)  12.3 us
    all_gather x1, waiting for transfers between devices, shards(): gathered = lax.all_gather(mine, ('yh', 'core'))  9.24 us
    pallas_call x1, Pallas kernels, multiply(): pl.pallas_call(place_kernel, out_shape=jax.ShapeDtypeStruct((2 * N_LAYER,...  6.71 us
    ppermute x1, starting transfers between devices, shards(): pieces_other = lax.ppermute(wanted, 'yl', [(0, 1), (1, 0)])  3.2 us
    pallas_call x1, Pallas kernels, pack(): pl.pallas_call(pack_kernel, out_shape=(jax.ShapeDtypeStruct((MSG, 128), j...  1.92 us
  transfers between devices with their start and end apart: 2, of which 2 were waited for; matrix products, arithmetic and copies ran while one was open for 0% of the time, Pallas kernels for 0%

profile of v4, /device:TPU:1, one launch (start us, length us, event | category | flops | bytes accessed | tf_op | source)
XLA Modules:
  0.0 91.2 jit_solution(26936342419115194)
XLA Ops:
  6.5 0.0 all-gather.4.cloned.1.call-start
  6.5 1.9 %shard_map.46 = (bf16[1040,128]{1,0:T(8,128)(2,1)}, bf16[80,128]{1,0:T(8,128)(2,1)}) custom-call(bf16[32,64,64]{2,1,0:T(8,128)(2,1)} %bitcast.13, s32[2,32]{1,0:T(2,128)} %bitcast.16, bf16[2,64,64]{2,1,0:T(8,128)(2,1)} %bitcast.15, s32[2,2]{1,0:T(2,128)} %bitcast.17), custom_call_target="tpu_custom_call" | custom-call | bytes 2097152 | tf_op jit(solution)/shard_map/pallas_call | solution.py:53
  8.5 0.0 all-gather.4.cloned.1.call-update
  8.5 29.5 %all-gather.1 = bf16[960,128]{1,0:T(8,128)(2,1)S(1)} all-gather(bf16[80,128]{1,0:T(8,128)(2,1)} %get-tuple-element.8), channel_id=3, replica_groups=mesh['yh'=4,'yl'=2,'core'=2,'col'=12,'layer'=4] {'col'}, dimensions={0}, use_global_device_ids=true | all-gather | bytes 266240 | tf_op jit(solution)/shard_map/all_gather | solution.py:182
  38.0 3.2 %collective-permute-start = (bf16[8,80,128]{2,1,0:T(8,128)(2,1)S(1)}, bf16[8,80,128]{2,1,0:T(8,128)(2,1)S(1)}, u32[]{:S(2)}, u32[]{:S(2)}) collective-permute-start(bf16[8,80,128]{2,1,0:T(8,128)(2,1)S(1)} %bitcast.14), channel_id=1, source_target_pairs={{0,96},{96,0},{1,97},{97,1},{2,98},{98,2},{3,99},{99,3},{4,100},{1... | collective-permute-start | bytes 491528 | tf_op jit(solution)/shard_map/ppermute | solution.py:185
  41.2 12.5 %collective-permute-done.left_other = bf16[8,80,128]{2,1,0:T(8,128)(2,1)S(1)} collective-permute-done((bf16[8,80,128]{2,1,0:T(8,128)(2,1)S(1)}, bf16[8,80,128]{2,1,0:T(8,128)(2,1)S(1)}, u32[]{:S(2)}, u32[]{:S(2)}) %collective-permute-start) | collective-permute-done | bytes 163872 | tf_op jit(solution)/shard_map/ppermute | solution.py:185
  53.7 9.2 %all-gather.4.cloned.1.call-done = bf16[8320,128]{1,0:T(8,128)(2,1)} async-done(((bf16[1040,128]{1,0:T(8,128)(2,1)}), bf16[8320,128]{1,0:T(8,128)(2,1)}) %all-gather.4.cloned.1.call-update) | async-done | bytes 2129936 | tf_op jit(solution)/shard_map/all_gather | solution.py:181
  62.9 0.0 copy-start
  62.9 1.6 %copy-done = bf16[8320,128]{1,0:T(8,128)(2,1)S(1)} copy-done((bf16[8320,128]{1,0:T(8,128)(2,1)S(1)}, bf16[8320,128]{1,0:T(8,128)(2,1)}, u32[]{:S(2)}) %copy-start) | copy-done | bytes 2129944
  64.5 6.7 %shard_map.47 = bf16[8,64,512]{2,1,0:T(8,128)(2,1)S(1)} custom-call(bf16[8,1040,128]{2,1,0:T(8,128)(2,1)S(1)} %bitcast.12, bf16[12,80,128]{2,1,0:T(8,128)(2,1)S(1)} %bitcast.11, bf16[8,80,128]{2,1,0:T(8,128)(2,1)S(1)} %collective-permute-done.left_other), custom_call_target="tpu_custom_call" | custom-call | flops 1610612736 | bytes 4194304 | tf_op jit(solution)/shard_map/pallas_call | solution.py:152
  71.3 12.3 %all_to_all.5 = bf16[8,64,512]{2,1,0:T(8,128)(2,1)S(1)} all-to-all(bf16[8,64,512]{2,1,0:T(8,128)(2,1)S(1)} %shard_map.47), channel_id=1, replica_groups=mesh['yh'=4,'yl'=2,'core'=2,'col'=12,'layer'=4] {'yl','layer'}, dimensions={0} | all-to-all | bytes 1048576 | tf_op jit(solution)/shard_map/all_to_all | solution.py:187
  83.5 0.1 convert_reduce_fusion
  83.6 0.8 reshape.27
  (1 shorter events, 0.0 us)
Async XLA Ops:
  6.5 56.4 %all-gather.4.cloned.1.call-start = ((), (), s32[]{:S(2)}) async-start(), calls=%async_computation.1 | async-start | bytes 2396160 | tf_op jit(solution)/shard_map/all_gather | solution.py:181
  38.0 15.7 %collective-permute-start = (bf16[8,80,128]{2,1,0:T(8,128)(2,1)S(1)}, bf16[8,80,128]{2,1,0:T(8,128)(2,1)S(1)}, u32[]{:S(2)}, u32[]{:S(2)}) collective-permute-start(bf16[8,80,128]{2,1,0:T(8,128)(2,1)S(1)} %bitcast.14), channel_id=1, source_target_pairs={{0,96},{96,0},{1,97},{97,1},{2,98},{98,2},{3,99},{99,3},{4,100},{1... | collective-permute-start | bytes 491528 | tf_op jit(solution)/shard_map/ppermute | solution.py:185
  62.9 1.6 %copy-start = (bf16[8320,128]{1,0:T(8,128)(2,1)S(1)}, bf16[8320,128]{1,0:T(8,128)(2,1)}, u32[]{:S(2)}) copy-start(bf16[8320,128]{1,0:T(8,128)(2,1)} %all-gather.4.cloned.1.call-done) | copy-start | bytes 6389764
Sparse Core Ops, SparseCore 0:
  9.8 53.1 all-gather.3

commit v5 on v4

v5 whole, which is shorter than its diff:
```python
import jax
import jax.numpy as jnp
from jax import lax
from jax.experimental import pallas as pl
from jax.experimental.pallas import tpu as pltpu
from jax.sharding import Mesh
from jax.sharding import PartitionSpec as P

NB = 384
BS = 64
N_YH = 4
N_COL = 12
N_LAYER = 4
SLOTS = 32
PAIRS = SLOTS // 2
BODY = PAIRS * BS
MSG = BODY + 16
LMSG = BS + 16
INNER = 6
COLUMNS = NB // N_COL
PIECE = NB // N_LAYER // N_COL
DEPTH = INNER * BS
WIDTH = COLUMNS * BS
NEAR = 3
CUT = 512
WINDOW = 2 * PIECE * BS


def pack_kernel(right, right_where, left, left_where, out, piece, tail):
    y = lax.axis_index("yh") * 2 + lax.axis_index("yl")
    core = lax.axis_index("core")
    col = lax.axis_index("col")
    base = lax.axis_index("layer") * (NB // N_LAYER)
    for p in range(PAIRS):
        out[p * BS : (p + 1) * BS, :] = jnp.concatenate([right[p], right[p + PAIRS]], axis=-1)
    tail[...] = jnp.zeros_like(tail)
    inner = right_where[0:1, :] - (base + (y * 2 + core) * INNER)
    column = right_where[1:2, :] - col * COLUMNS
    tail[0:1, 0:SLOTS] = inner.astype(jnp.float32)
    tail[1:2, 0:SLOTS] = column.astype(jnp.float32)
    out[BODY:MSG, :] = tail[...].astype(jnp.bfloat16)
    lane = lax.broadcasted_iota(jnp.int32, (16, 128), 1)
    first = jnp.broadcast_to(left_where[0:1, 1:2], (16, 128))
    second = jnp.broadcast_to(left_where[1:2, 1:2], (16, 128))
    at = jnp.where(lane < BS, first, second) - (base + col * PIECE)
    at = at.astype(jnp.float32).astype(jnp.bfloat16)
    pair = jnp.concatenate([left[0], left[1]], axis=-1)
    piece[:BS, :] = pair
    piece[BS:, :] = at


def pack(right, right_where, left, left_where):
    vmem = pl.BlockSpec(memory_space=pltpu.VMEM)
    return pl.pallas_call(
        pack_kernel,
        out_shape=(
            jax.ShapeDtypeStruct((MSG, 128), jnp.bfloat16),
            jax.ShapeDtypeStruct((LMSG, 128), jnp.bfloat16),
        ),
        in_specs=[vmem] * 4,
        out_specs=(vmem, vmem),
        scratch_shapes=[pltpu.VMEM((16, 128), jnp.float32)],
        cost_estimate=pl.CostEstimate(flops=0, bytes_accessed=2 << 20, transcendentals=0),
    )(right, right_where, left, left_where)


def half_swap():
    to = lax.broadcasted_iota(jnp.int32, (128, 128), 1)
    frm = lax.broadcasted_iota(jnp.int32, (128, 128), 0)
    return (to == (frm + BS) % 128).astype(jnp.bfloat16)


def place_slots(blocks, panels, swapped, places):
    lane = lax.broadcasted_iota(jnp.int32, (BS, 128), 1)
    low = (lane < BS).astype(jnp.bfloat16)
    high = (lane >= BS).astype(jnp.bfloat16)

    def place(p, carry):
        at = pl.ds(pl.multiple_of(p * BS, BS), BS)
        for half in range(2):
            for i, block in enumerate(blocks):
                k = places[2 * i, p + half * PAIRS]
                n = places[2 * i + 1, p + half * PAIRS]
                odd = n & 1
                value = jnp.where(odd == half, block[at, :], swapped[i][at, :])
                value = value * jnp.where(odd == 1, high, low)
                rows = pl.ds(pl.multiple_of(k * BS, BS), BS)
                lanes = pl.ds(pl.multiple_of((n >> 1) * 128, 128), 128)
                panels[i][rows, lanes] = panels[i][rows, lanes] + value
        return carry

    lax.fori_loop(0, PAIRS, place, 0, unroll=2)


def read_places(blocks, where, places, sem):
    for i, block in enumerate(blocks):
        tail = block[BODY:MSG, :].astype(jnp.float32).astype(jnp.int32)
        where[2 * i : 2 * i + 2, :] = tail[0:2, :]
    copy = pltpu.make_async_copy(where, places, sem)
    copy.start()
    return copy


def fill_panels(blocks, panels, swapped, places, copy):
    swap = half_swap()
    for i, block in enumerate(blocks):
        panels[i][...] = jnp.zeros_like(panels[i])
        swapped[i][...] = jnp.dot(
            block[:BODY, :], swap, preferred_element_type=jnp.float32
        ).astype(jnp.bfloat16)
    copy.wait()
    place_slots(blocks, panels, swapped, places)


def scratch_for(blocks):
    return (
        [
            pltpu.VMEM((16, 128), jnp.int32),
            pltpu.SMEM((16, 128), jnp.int32),
            pltpu.SemaphoreType.DMA,
            pltpu.SemaphoreType.DMA((NEAR,)),
        ]
        + [pltpu.VMEM((DEPTH, WIDTH), jnp.bfloat16)] * blocks
        + [pltpu.VMEM((BODY, 128), jnp.bfloat16)] * blocks
    )


def early_kernel(near, out, where, places, sem, sems, *scratch):
    panels, swapped = scratch[:NEAR], scratch[NEAR:]
    blocks = [near.at[j] for j in range(NEAR)]
    fill_panels(blocks, panels, swapped, places, read_places(blocks, where, places, sem))
    copies = [pltpu.make_async_copy(panels[j], out.at[j], sems.at[j]) for j in range(NEAR)]
    for copy in copies:
        copy.start()
    for copy in copies:
        copy.wait()


def early(near):
    return pl.pallas_call(
        early_kernel,
        out_shape=pltpu.HBM((NEAR, DEPTH, WIDTH), jnp.bfloat16),
        in_specs=[pl.BlockSpec(memory_space=pltpu.VMEM)],
        out_specs=pl.BlockSpec(memory_space=pltpu.HBM),
        scratch_shapes=scratch_for(NEAR),
        compiler_params=pltpu.CompilerParams(vmem_limit_bytes=12 * 1024 * 1024),
        cost_estimate=pl.CostEstimate(flops=0, bytes_accessed=10 << 20, transcendentals=0),
    )(near)


def multiply_kernel(pieces, ready, far, near_other, far_other, out, *scratch):
    (left, total, *held), (where, places, sem, sems) = scratch[: 2 + NEAR], scratch[2 + NEAR : 6 + NEAR]
    panels, swapped = scratch[6 + NEAR : 11 + NEAR], scratch[11 + NEAR :]
    blocks = [far] + [near_other.at[j] for j in range(NEAR)] + [far_other]
    copies = [pltpu.make_async_copy(ready.at[j], held[j], sems.at[j]) for j in range(NEAR)]
    for copy in copies:
        copy.start()
    copy = read_places(blocks, where, places, sem)
    yl = lax.axis_index("yl")
    core = lax.axis_index("core")
    yh = lax.axis_index("yh")
    swap = half_swap()

    lane = lax.broadcasted_iota(jnp.int32, (BS, 128), 1)
    upper = (lane >= BS).astype(jnp.float32)
    for m, at in ((0, yl), (1, 1 - yl)):
        rows = pl.ds(pl.multiple_of(at * BS, BS), BS)
        for q in range(N_YH):
            for u in range(2):
                piece = pieces.at[3 * q + yl + u]
                here = piece[m * BS : (m + 1) * BS, :]
                marks = piece[2 * BS :, :]
                there = jnp.dot(here, swap, preferred_element_type=jnp.float32)
                k_there = jnp.dot(marks, swap, preferred_element_type=jnp.float32)[m : m + 1]
                here = here.astype(jnp.float32)
                k_here = marks.astype(jnp.float32)[m : m + 1]
                for g in range(PIECE // 2):
                    want = upper + 2.0 * g
                    value = jnp.where(k_here == want, here, 0.0)
                    value = value + jnp.where(k_there == want, there, 0.0)
                    at_lane = q * WINDOW + (u * PIECE + 2 * g) * BS
                    left[rows, at_lane : at_lane + 128] = value.astype(jnp.bfloat16)

    fill_panels(blocks, panels, swapped, places, copy)
    for copy in copies:
        copy.wait()
    order = ((0, core), (3, core), (1, core), (2, core))
    order += tuple((away, 1 - core) for away, _ in order)
    for j, (away, side) in enumerate(order):
        panel = held[j] if j < NEAR else panels[j - NEAR]
        start = ((yh + away) % N_YH) * WINDOW + yl * (4 * BS) + side * DEPTH
        at = pl.ds(pl.multiple_of(start, 128), DEPTH)
        part = jnp.dot(left[:, at], panel[...], preferred_element_type=jnp.float32)
        total[...] = part if j == 0 else total[...] + part
    share = WIDTH // N_LAYER
    for m in range(2):
        for s in range(N_LAYER):
            out[m * N_LAYER + s] = total[m * BS : (m + 1) * BS, s * share : (s + 1) * share].astype(
                jnp.bfloat16
            )


def multiply(pieces, ready, far, near_other, far_other):
    vmem = pl.BlockSpec(memory_space=pltpu.VMEM)
    return pl.pallas_call(
        multiply_kernel,
        out_shape=jax.ShapeDtypeStruct((2 * N_LAYER, BS, WIDTH // N_LAYER), jnp.bfloat16),
        in_specs=[vmem, pl.BlockSpec(memory_space=pltpu.HBM), vmem, vmem, vmem],
        out_specs=vmem,
        scratch_shapes=[
            pltpu.VMEM((2 * BS, N_YH * WINDOW), jnp.bfloat16),
            pltpu.VMEM((2 * BS, WIDTH), jnp.float32),
        ]
        + [pltpu.VMEM((DEPTH, WIDTH), jnp.bfloat16)] * NEAR
        + scratch_for(5),
        compiler_params=pltpu.CompilerParams(vmem_limit_bytes=24 * 1024 * 1024),
        cost_estimate=pl.CostEstimate(
            flops=2 * 128 * 3072 * 2048, bytes_accessed=4 << 20, transcendentals=0
        ),
    )(pieces, pltpu.with_memory_space_constraint(ready, pltpu.HBM), far, near_other, far_other)


def spread_kernel(mine, theirs, out):
    first = lax.broadcasted_iota(jnp.int32, (16, 128), 0) == 0
    tail = jnp.where(first, mine[BS:, :].astype(jnp.float32), theirs[BS:, :].astype(jnp.float32))
    for c in range(N_COL):
        out[c, :BS, :] = mine[:BS, :]
        out[c, BS : 2 * BS, :] = theirs[:BS, :]
        out[c, 2 * BS :, :] = tail.astype(jnp.bfloat16)


def spread(mine, theirs):
    vmem = pl.BlockSpec(memory_space=pltpu.VMEM)
    return pl.pallas_call(
        spread_kernel,
        out_shape=jax.ShapeDtypeStruct((N_COL, 2 * BS + 16, 128), jnp.bfloat16),
        in_specs=[vmem] * 2,
        out_specs=vmem,
        cost_estimate=pl.CostEstimate(flops=0, bytes_accessed=1 << 20, transcendentals=0),
    )(mine, theirs)


def shards(left_blocks, left_coords, right_blocks, right_coords):
    mine, piece = pack(
        right_blocks.reshape(SLOTS, BS, BS),
        right_coords.reshape(SLOTS, 2).T,
        left_blocks.reshape(2, BS, BS),
        left_coords.reshape(2, 2),
    )
    up = [(i, (i + 1) % N_YH) for i in range(N_YH)]
    down = [(i, (i - 1) % N_YH) for i in range(N_YH)]
    cross = [(0, 1), (1, 0)]
    neighbour = lax.ppermute(piece, "yl", cross)
    below = lax.ppermute(mine, "yh", up)
    above = lax.ppermute(mine, "yh", down)
    pieces = lax.all_to_all(spread(piece, neighbour), "col", 0, 0)
    far_low = lax.ppermute(below[:CUT], "yh", up)
    far_high = lax.ppermute(above[CUT:], "yh", down)
    near = jnp.stack([mine, below, above])
    near_other = lax.ppermute(near, "core", cross)
    far = jnp.concatenate([far_low, far_high])
    far_other = lax.ppermute(far, "core", cross)
    part = multiply(pieces, early(near), far, near_other, far_other)
    parts = lax.all_to_all(part, ("yl", "layer"), 0, 0)
    total = jnp.sum(parts.astype(jnp.float32), axis=0)
    return total.reshape(1, BS, COLUMNS // N_LAYER, BS)


def solution(mesh):
    grid = Mesh(mesh.devices.reshape(N_YH, 2, 2, N_COL, N_LAYER), ("yh", "yl", "core", "col", "layer"))
    row = ("yh", "yl", "core")
    return jax.shard_map(
        shards,
        mesh=grid,
        in_specs=(
            P(row, "col", "layer", None, None, None),
            P(row, "col", "layer", None, None),
            P(row, "col", "layer", None, None, None),
            P(row, "col", "layer", None, None),
        ),
        out_specs=P(row, None, ("col", "layer"), None),
        check_vma=False,
    )
```

time: 91.9 us -> 88.6 us (0.964)
  the two profiles are of different devices: /device:TPU:1 before, /device:TPU:16 now
where the time goes in v5:
time: 88.6 us; the launch traced here: 88.1 us
  starting transfers between devices  43.2 us (49%)
  blocking collectives  14.6 us (16%)
  Pallas kernels  13.8 us (16%)
  waiting for transfers between devices  13.7 us (15%)
  local copies, waits for them, and re-layouts  1.45 us (2%)
  other arithmetic  1.11 us (1%)
    all_to_all x1, blocking collectives, shards(): parts = lax.all_to_all(part, ('yl', 'layer'), 0, 0)  14.6 us
    all_to_all x1, starting transfers between devices, shards(): pieces = lax.all_to_all(spread(piece, neighbour), 'col', 0, 0)  13.6 us
    ppermute x1, starting transfers between devices, shards(): far_low = lax.ppermute(below[:CUT], 'yh', up)  8.79 us
    ppermute x1, starting transfers between devices, shards(): above = lax.ppermute(mine, 'yh', down)  7.47 us
    ppermute x1, waiting for transfers between devices, shards(): far_high = lax.ppermute(above[CUT:], 'yh', down)  6.3 us
    pallas_call x1, Pallas kernels, multiply(): pl.pallas_call(multiply_kernel, out_shape=jax.ShapeDtypeStruct((2 * N_LAY...  6.2 us
    ppermute x1, starting transfers between devices, shards(): below = lax.ppermute(mine, 'yh', up)  5.7 us
    pallas_call x1, Pallas kernels, early(): pl.pallas_call(early_kernel, out_shape=pltpu.HBM((NEAR, DEPTH, WIDTH), jn...  4.15 us
  transfers between devices with their start and end apart: 8, of which 3 were waited for; matrix products, arithmetic and copies ran while one was open for 1% of the time, Pallas kernels for 7%

profile of v5, /device:TPU:16, one launch (start us, length us, event | category | flops | bytes accessed | tf_op | source)
XLA Modules:
  0.0 88.1 jit_solution(9666149387964726657)
XLA Ops:
  0.0 1.9 %shard_map.46 = (bf16[1040,128]{1,0:T(8,128)(2,1)}, bf16[80,128]{1,0:T(8,128)(2,1)}) custom-call(bf16[32,64,64]{2,1,0:T(8,128)(2,1)} %bitcast.11, s32[2,32]{1,0:T(2,128)} %bitcast.14, bf16[2,64,64]{2,1,0:T(8,128)(2,1)} %bitcast.13, s32[2,2]{1,0:T(2,128)} %bitcast.15), custom_call_target="tpu_custom_call" | custom-call | bytes 2097152 | tf_op jit(solution)/shard_map/pallas_call | solution.py:54
  1.9 5.7 %collective-permute-start.1 = (bf16[1040,128]{1,0:T(8,128)(2,1)}, bf16[1040,128]{1,0:T(8,128)(2,1)S(1)}, u32[]{:S(2)}, u32[]{:S(2)}) collective-permute-start(bf16[1040,128]{1,0:T(8,128)(2,1)} %get-tuple-element.8), channel_id=1, source_target_pairs={{0,192},{192,384},{384,576},{576,0},{1,193},{193,385},{385,577},{5... | collective-permute-start | bytes 798728 | tf_op jit(solution)/shard_map/ppermute | solution.py:254
  7.6 7.5 %collective-permute-start.2 = (bf16[1040,128]{1,0:T(8,128)(2,1)}, bf16[1040,128]{1,0:T(8,128)(2,1)S(1)}, u32[]{:S(2)}, u32[]{:S(2)}) collective-permute-start(bf16[1040,128]{1,0:T(8,128)(2,1)} %get-tuple-element.8), channel_id=1, source_target_pairs={{0,576},{192,0},{384,192},{576,384},{1,577},{193,1},{385,193},{577... | collective-permute-start | bytes 798728 | tf_op jit(solution)/shard_map/ppermute | solution.py:255
  15.1 1.9 %collective-permute-start = (bf16[80,128]{1,0:T(8,128)(2,1)}, bf16[80,128]{1,0:T(8,128)(2,1)S(1)}, u32[]{:S(2)}, u32[]{:S(2)}) collective-permute-start(bf16[80,128]{1,0:T(8,128)(2,1)} %get-tuple-element.7.mine), channel_id=1, source_target_pairs={{0,96},{96,0},{1,97},{97,1},{2,98},{98,2},{3,99},{99,3},{4,100},{1... | collective-permute-start | bytes 61448 | tf_op jit(solution)/shard_map/ppermute | solution.py:253
  17.0 4.0 %collective-permute-done.theirs = bf16[80,128]{1,0:T(8,128)(2,1)S(1)} collective-permute-done((bf16[80,128]{1,0:T(8,128)(2,1)}, bf16[80,128]{1,0:T(8,128)(2,1)S(1)}, u32[]{:S(2)}, u32[]{:S(2)}) %collective-permute-start) | collective-permute-done | bytes 20512 | tf_op jit(solution)/shard_map/ppermute | solution.py:253
  21.0 0.0 copy-start
  21.0 0.6 copy-done
  21.6 1.6 %shard_map.47 = bf16[12,144,128]{2,1,0:T(8,128)(2,1)} custom-call(bf16[80,128]{1,0:T(8,128)(2,1)} %get-tuple-element.7.mine, bf16[80,128]{1,0:T(8,128)(2,1)} %copy-done), custom_call_target="tpu_custom_call" | custom-call | bytes 1048576 | tf_op jit(solution)/shard_map/pallas_call | solution.py:234
  23.2 13.6 %all-to-all-start = ((bf16[12,144,128]{2,1,0:T(8,128)(2,1)}), bf16[12,144,128]{2,1,0:T(8,128)(2,1)S(1)}, u32[]{:S(2)}, u32[]{:S(2)}) async-start(bf16[12,144,128]{2,1,0:T(8,128)(2,1)} %shard_map.47), calls=%async_computation | async-start | bytes 884736 | tf_op jit(solution)/shard_map/all_to_all | solution.py:256
  36.8 0.0 collective-permute-done.1
  36.8 0.0 collective-permute-done.2
  36.8 1.0 %pad_maximum_fusion.near = bf16[3,1040,128]{2,1,0:T(8,128)(2,1)S(1)} fusion(bf16[1,1040,128]{2,1,0:T(8,128)(2,1)S(1)} %bitcast.9, bf16[1,1040,128]{2,1,0:T(8,128)(2,1)S(1)} %bitcast.10, bf16[1,1040,128]{2,1,0:T(8,128)(2,1)} %bitcast.12), kind=kLoop, calls=%fused_computation.1 | loop fusion | flops 798720 | bytes 1597440 | tf_op jit(solution)/shard_map/stack | solution.py:259
  37.8 1.9 %collective-permute-start.5 = (bf16[3,1040,128]{2,1,0:T(8,128)(2,1)S(1)}, bf16[3,1040,128]{2,1,0:T(8,128)(2,1)S(1)}, u32[]{:S(2)}, u32[]{:S(2)}) collective-permute-start(bf16[3,1040,128]{2,1,0:T(8,128)(2,1)S(1)} %pad_maximum_fusion.near), channel_id=1, source_target_pairs={{0,48},{48,0},{1,49},{49,1},{2,50},{50,2},{3,51},{51,3},{4,52},{52... | collective-permute-start | bytes 2396168 | tf_op jit(solution)/shard_map/ppermute | solution.py:260
  39.8 8.8 %collective-permute-start.3 = (bf16[512,128]{1,0:T(8,128)(2,1)S(1)}, bf16[512,128]{1,0:T(8,128)(2,1)S(1)}, u32[]{:S(2)}, u32[]{:S(2)}) collective-permute-start(bf16[512,128]{1,0:T(8,128)(2,1)S(1)} %slice.8), channel_id=1, source_target_pairs={{0,192},{192,384},{384,576},{576,0},{1,193},{193,385},{385,577},{5... | collective-permute-start | bytes 393224 | tf_op jit(solution)/shard_map/ppermute | solution.py:257
  48.6 1.9 %collective-permute-start.4 = (bf16[528,128]{1,0:T(8,128)(2,1)S(1)}, bf16[528,128]{1,0:T(8,128)(2,1)S(1)}, u32[]{:S(2)}, u32[]{:S(2)}) collective-permute-start(bf16[528,128]{1,0:T(8,128)(2,1)S(1)} %slice.9), channel_id=1, source_target_pairs={{0,576},{192,0},{384,192},{576,384},{1,577},{193,1},{385,193},{577... | collective-permute-start | bytes 405512 | tf_op jit(solution)/shard_map/ppermute | solution.py:258
  50.5 3.4 %collective-permute-done.3 = bf16[512,128]{1,0:T(8,128)(2,1)S(1)} collective-permute-done((bf16[512,128]{1,0:T(8,128)(2,1)S(1)}, bf16[512,128]{1,0:T(8,128)(2,1)S(1)}, u32[]{:S(2)}, u32[]{:S(2)}) %collective-permute-start.3) | collective-permute-done | bytes 131104 | tf_op jit(solution)/shard_map/ppermute | solution.py:257
  53.9 6.3 %collective-permute-done.4 = bf16[528,128]{1,0:T(8,128)(2,1)S(1)} collective-permute-done((bf16[528,128]{1,0:T(8,128)(2,1)S(1)}, bf16[528,128]{1,0:T(8,128)(2,1)S(1)}, u32[]{:S(2)}, u32[]{:S(2)}) %collective-permute-start.4) | collective-permute-done | bytes 135200 | tf_op jit(solution)/shard_map/ppermute | solution.py:258
  60.3 1.9 %collective-permute-start.6 = (bf16[1040,128]{1,0:T(8,128)(2,1)S(1)}, bf16[1040,128]{1,0:T(8,128)(2,1)S(1)}, u32[]{:S(2)}, u32[]{:S(2)}) collective-permute-start(bf16[1040,128]{1,0:T(8,128)(2,1)S(1)} %constant_dynamic-update-slice_fusion.far), channel_id=1, source_target_pairs={{0,48},{48,0},{1,49},{49,1},{2,50},{50,2},{3,51},{51,3},{4,52},{52... | collective-permute-start | bytes 798728 | tf_op jit(solution)/shard_map/ppermute | solution.py:262
  62.2 4.1 %shard_map.48.ready = bf16[3,384,2048]{2,1,0:T(8,128)(2,1)} custom-call(bf16[3,1040,128]{2,1,0:T(8,128)(2,1)S(1)} %pad_maximum_fusion.near), custom_call_target="tpu_custom_call" | custom-call | bytes 10485760 | tf_op jit(solution)/shard_map/pallas_call | solution.py:140
  66.3 0.0 collective-permute-done.6.far_other
  66.4 0.0 collective-permute-done.5.near_other
  66.4 0.0 all-to-all-done.pieces
  66.4 6.2 %shard_map.49 = bf16[8,64,512]{2,1,0:T(8,128)(2,1)S(1)} custom-call(bf16[12,144,128]{2,1,0:T(8,128)(2,1)S(1)} %all-to-all-done.pieces, bf16[3,384,2048]{2,1,0:T(8,128)(2,1)} %shard_map.48.ready, bf16[1040,128]{1,0:T(8,128)(2,1)S(1)} %constant_dynamic-update-slice_fusion.far, bf16[3,1040,128]{2,1,0:T(8,128)(2,1)S(1)} %collective-permute-done.5.near_other, ...), custom_call_target="tpu_custom_call" | custom-call | flops 1610612736 | bytes 4194304 | tf_op jit(solution)/shard_map/pallas_call | solution.py:205
  72.6 14.6 %all_to_all.10 = bf16[8,64,512]{2,1,0:T(8,128)(2,1)S(1)} all-to-all(bf16[8,64,512]{2,1,0:T(8,128)(2,1)S(1)} %shard_map.49), channel_id=1, replica_groups=mesh['yh'=4,'yl'=2,'core'=2,'col'=12,'layer'=4] {'yl','layer'}, dimensions={0} | all-to-all | bytes 1048576 | tf_op jit(solution)/shard_map/all_to_all | solution.py:264
  87.2 0.1 convert_reduce_fusion
  87.3 0.8 reshape.19
  (4 shorter events, 0.0 us)
Async XLA Ops:
  1.9 34.9 %collective-permute-start.1 = (bf16[1040,128]{1,0:T(8,128)(2,1)}, bf16[1040,128]{1,0:T(8,128)(2,1)S(1)}, u32[]{:S(2)}, u32[]{:S(2)}) collective-permute-start(bf16[1040,128]{1,0:T(8,128)(2,1)} %get-tuple-element.8), channel_id=1, source_target_pairs={{0,192},{192,384},{384,576},{576,0},{1,193},{193,385},{385,577},{5... | collective-permute-start | bytes 798728 | tf_op jit(solution)/shard_map/ppermute | solution.py:254
  7.6 29.2 %collective-permute-start.2 = (bf16[1040,128]{1,0:T(8,128)(2,1)}, bf16[1040,128]{1,0:T(8,128)(2,1)S(1)}, u32[]{:S(2)}, u32[]{:S(2)}) collective-permute-start(bf16[1040,128]{1,0:T(8,128)(2,1)} %get-tuple-element.8), channel_id=1, source_target_pairs={{0,576},{192,0},{384,192},{576,384},{1,577},{193,1},{385,193},{577... | collective-permute-start | bytes 798728 | tf_op jit(solution)/shard_map/ppermute | solution.py:255
  15.1 5.9 %collective-permute-start = (bf16[80,128]{1,0:T(8,128)(2,1)}, bf16[80,128]{1,0:T(8,128)(2,1)S(1)}, u32[]{:S(2)}, u32[]{:S(2)}) collective-permute-start(bf16[80,128]{1,0:T(8,128)(2,1)} %get-tuple-element.7.mine), channel_id=1, source_target_pairs={{0,96},{96,0},{1,97},{97,1},{2,98},{98,2},{3,99},{99,3},{4,100},{1... | collective-permute-start | bytes 61448 | tf_op jit(solution)/shard_map/ppermute | solution.py:253
  21.0 0.6 copy-start
  23.2 43.2 %all-to-all-start = ((bf16[12,144,128]{2,1,0:T(8,128)(2,1)}), bf16[12,144,128]{2,1,0:T(8,128)(2,1)S(1)}, u32[]{:S(2)}, u32[]{:S(2)}) async-start(bf16[12,144,128]{2,1,0:T(8,128)(2,1)} %shard_map.47), calls=%async_computation | async-start | bytes 884736 | tf_op jit(solution)/shard_map/all_to_all | solution.py:256
  37.8 28.5 %collective-permute-start.5 = (bf16[3,1040,128]{2,1,0:T(8,128)(2,1)S(1)}, bf16[3,1040,128]{2,1,0:T(8,128)(2,1)S(1)}, u32[]{:S(2)}, u32[]{:S(2)}) collective-permute-start(bf16[3,1040,128]{2,1,0:T(8,128)(2,1)S(1)} %pad_maximum_fusion.near), channel_id=1, source_target_pairs={{0,48},{48,0},{1,49},{49,1},{2,50},{50,2},{3,51},{51,3},{4,52},{52... | collective-permute-start | bytes 2396168 | tf_op jit(solution)/shard_map/ppermute | solution.py:260
  39.8 14.1 %collective-permute-start.3 = (bf16[512,128]{1,0:T(8,128)(2,1)S(1)}, bf16[512,128]{1,0:T(8,128)(2,1)S(1)}, u32[]{:S(2)}, u32[]{:S(2)}) collective-permute-start(bf16[512,128]{1,0:T(8,128)(2,1)S(1)} %slice.8), channel_id=1, source_target_pairs={{0,192},{192,384},{384,576},{576,0},{1,193},{193,385},{385,577},{5... | collective-permute-start | bytes 393224 | tf_op jit(solution)/shard_map/ppermute | solution.py:257
  48.6 11.6 %collective-permute-start.4 = (bf16[528,128]{1,0:T(8,128)(2,1)S(1)}, bf16[528,128]{1,0:T(8,128)(2,1)S(1)}, u32[]{:S(2)}, u32[]{:S(2)}) collective-permute-start(bf16[528,128]{1,0:T(8,128)(2,1)S(1)} %slice.9), channel_id=1, source_target_pairs={{0,576},{192,0},{384,192},{576,384},{1,577},{193,1},{385,193},{577... | collective-permute-start | bytes 405512 | tf_op jit(solution)/shard_map/ppermute | solution.py:258
  60.3 6.1 %collective-permute-start.6 = (bf16[1040,128]{1,0:T(8,128)(2,1)S(1)}, bf16[1040,128]{1,0:T(8,128)(2,1)S(1)}, u32[]{:S(2)}, u32[]{:S(2)}) collective-permute-start(bf16[1040,128]{1,0:T(8,128)(2,1)S(1)} %constant_dynamic-update-slice_fusion.far), channel_id=1, source_target_pairs={{0,48},{48,0},{1,49},{49,1},{2,50},{50,2},{3,51},{51,3},{4,52},{52... | collective-permute-start | bytes 798728 | tf_op jit(solution)/shard_map/ppermute | solution.py:262

commit v6 on v5

--- a/solution.py
+++ b/solution.py
@@ -21,8 +21,7 @@
 PIECE = NB // N_LAYER // N_COL
 DEPTH = INNER * BS
 WIDTH = COLUMNS * BS
-NEAR = 3
-CUT = 512
+NEAR = 4
 WINDOW = 2 * PIECE * BS
 
 
@@ -125,9 +124,9 @@
     )
 
 
-def early_kernel(near, out, where, places, sem, sems, *scratch):
+def early_kernel(first, second, out, where, places, sem, sems, *scratch):
     panels, swapped = scratch[:NEAR], scratch[NEAR:]
-    blocks = [near.at[j] for j in range(NEAR)]
+    blocks = [first.at[0], first.at[1], second.at[0], second.at[1]]
     fill_panels(blocks, panels, swapped, places, read_places(blocks, where, places, sem))
     copies = [pltpu.make_async_copy(panels[j], out.at[j], sems.at[j]) for j in range(NEAR)]
     for copy in copies:
@@ -136,22 +135,22 @@
         copy.wait()
 
 
-def early(near):
+def early(first, second):
     return pl.pallas_call(
         early_kernel,
         out_shape=pltpu.HBM((NEAR, DEPTH, WIDTH), jnp.bfloat16),
-        in_specs=[pl.BlockSpec(memory_space=pltpu.VMEM)],
+        in_specs=[pl.BlockSpec(memory_space=pltpu.VMEM)] * 2,
         out_specs=pl.BlockSpec(memory_space=pltpu.HBM),
         scratch_shapes=scratch_for(NEAR),
-        compiler_params=pltpu.CompilerParams(vmem_limit_bytes=12 * 1024 * 1024),
-        cost_estimate=pl.CostEstimate(flops=0, bytes_accessed=10 << 20, transcendentals=0),
-    )(near)
-
-
-def multiply_kernel(pieces, ready, far, near_other, far_other, out, *scratch):
+        compiler_params=pltpu.CompilerParams(vmem_limit_bytes=14 * 1024 * 1024),
+        cost_estimate=pl.CostEstimate(flops=40_000_000_000, bytes_accessed=10 << 20, transcendentals=0),
+    )(first, second)
+
+
+def multiply_kernel(left_own, left_other, ready, first, second, out, *scratch):
     (left, total, *held), (where, places, sem, sems) = scratch[: 2 + NEAR], scratch[2 + NEAR : 6 + NEAR]
-    panels, swapped = scratch[6 + NEAR : 11 + NEAR], scratch[11 + NEAR :]
-    blocks = [far] + [near_other.at[j] for j in range(NEAR)] + [far_other]
+    panels, swapped = scratch[6 + NEAR : 6 + 2 * NEAR], scratch[6 + 2 * NEAR :]
+    blocks = [first.at[0], first.at[1], second.at[0], second.at[1]]
     copies = [pltpu.make_async_copy(ready.at[j], held[j], sems.at[j]) for j in range(NEAR)]
     for copy in copies:
         copy.start()
@@ -163,28 +162,24 @@
 
     lane = lax.broadcasted_iota(jnp.int32, (BS, 128), 1)
     upper = (lane >= BS).astype(jnp.float32)
-    for m, at in ((0, yl), (1, 1 - yl)):
+    for src, at in ((left_own, yl), (left_other, 1 - yl)):
         rows = pl.ds(pl.multiple_of(at * BS, BS), BS)
         for q in range(N_YH):
             for u in range(2):
-                piece = pieces.at[3 * q + yl + u]
-                here = piece[m * BS : (m + 1) * BS, :]
-                marks = piece[2 * BS :, :]
-                there = jnp.dot(here, swap, preferred_element_type=jnp.float32)
-                k_there = jnp.dot(marks, swap, preferred_element_type=jnp.float32)[m : m + 1]
-                here = here.astype(jnp.float32)
-                k_here = marks.astype(jnp.float32)[m : m + 1]
+                whole = src[3 * q + yl + u] if src is left_own else src[2 * q + u]
+                there = jnp.dot(whole, swap, preferred_element_type=jnp.float32)
+                here = whole.astype(jnp.float32)
                 for g in range(PIECE // 2):
                     want = upper + 2.0 * g
-                    value = jnp.where(k_here == want, here, 0.0)
-                    value = value + jnp.where(k_there == want, there, 0.0)
+                    value = jnp.where(here[BS : BS + 1] == want, here[:BS], 0.0)
+                    value = value + jnp.where(there[BS : BS + 1] == want, there[:BS], 0.0)
                     at_lane = q * WINDOW + (u * PIECE + 2 * g) * BS
                     left[rows, at_lane : at_lane + 128] = value.astype(jnp.bfloat16)
 
     fill_panels(blocks, panels, swapped, places, copy)
     for copy in copies:
         copy.wait()
-    order = ((0, core), (3, core), (1, core), (2, core))
+    order = tuple((away, core) for away in (0, 3, 1, 2))
     order += tuple((away, 1 - core) for away, _ in order)
     for j, (away, side) in enumerate(order):
         panel = held[j] if j < NEAR else panels[j - NEAR]
@@ -200,44 +195,41 @@
             )
 
 
-def multiply(pieces, ready, far, near_other, far_other):
+def multiply(left_own, left_other, ready, first, second):
     vmem = pl.BlockSpec(memory_space=pltpu.VMEM)
     return pl.pallas_call(
         multiply_kernel,
         out_shape=jax.ShapeDtypeStruct((2 * N_LAYER, BS, WIDTH // N_LAYER), jnp.bfloat16),
-        in_specs=[vmem, pl.BlockSpec(memory_space=pltpu.HBM), vmem, vmem, vmem],
+        in_specs=[vmem, vmem, pl.BlockSpec(memory_space=pltpu.HBM), vmem, vmem],
         out_specs=vmem,
         scratch_shapes=[
             pltpu.VMEM((2 * BS, N_YH * WINDOW), jnp.bfloat16),
             pltpu.VMEM((2 * BS, WIDTH), jnp.float32),
         ]
         + [pltpu.VMEM((DEPTH, WIDTH), jnp.bfloat16)] * NEAR
-        + scratch_for(5),
+        + scratch_for(NEAR),
         compiler_params=pltpu.CompilerParams(vmem_limit_bytes=24 * 1024 * 1024),
         cost_estimate=pl.CostEstimate(
             flops=2 * 128 * 3072 * 2048, bytes_accessed=4 << 20, transcendentals=0
         ),
-    )(pieces, pltpu.with_memory_space_constraint(ready, pltpu.HBM), far, near_other, far_other)
-
-
-def spread_kernel(mine, theirs, out):
-    first = lax.broadcasted_iota(jnp.int32, (16, 128), 0) == 0
-    tail = jnp.where(first, mine[BS:, :].astype(jnp.float32), theirs[BS:, :].astype(jnp.float32))
+    )(left_own, left_other, pltpu.with_memory_space_constraint(ready, pltpu.HBM), first, second)
+
+
+def spread_kernel(piece, when, out):
+    del when
     for c in range(N_COL):
-        out[c, :BS, :] = mine[:BS, :]
-        out[c, BS : 2 * BS, :] = theirs[:BS, :]
-        out[c, 2 * BS :, :] = tail.astype(jnp.bfloat16)
-
-
-def spread(mine, theirs):
+        out[c] = piece[...]
+
+
+def spread(piece, when):
     vmem = pl.BlockSpec(memory_space=pltpu.VMEM)
     return pl.pallas_call(
         spread_kernel,
-        out_shape=jax.ShapeDtypeStruct((N_COL, 2 * BS + 16, 128), jnp.bfloat16),
-        in_specs=[vmem] * 2,
+        out_shape=jax.ShapeDtypeStruct((N_COL, LMSG, 128), jnp.bfloat16),
+        in_specs=[vmem, pl.BlockSpec(memory_space=pl.ANY)],
         out_specs=vmem,
         cost_estimate=pl.CostEstimate(flops=0, bytes_accessed=1 << 20, transcendentals=0),
-    )(mine, theirs)
+    )(piece, when)
 
 
 def shards(left_blocks, left_coords, right_blocks, right_coords):
@@ -247,20 +239,17 @@
         left_blocks.reshape(2, BS, BS),
         left_coords.reshape(2, 2),
     )
-    up = [(i, (i + 1) % N_YH) for i in range(N_YH)]
-    down = [(i, (i - 1) % N_YH) for i in range(N_YH)]
+    yl = lax.axis_index("yl")
+    away = [[(i, (i + d) % N_YH) for i in range(N_YH)] for d in range(N_YH)]
     cross = [(0, 1), (1, 0)]
-    neighbour = lax.ppermute(piece, "yl", cross)
-    below = lax.ppermute(mine, "yh", up)
-    above = lax.ppermute(mine, "yh", down)
-    pieces = lax.all_to_all(spread(piece, neighbour), "col", 0, 0)
-    far_low = lax.ppermute(below[:CUT], "yh", up)
-    far_high = lax.ppermute(above[CUT:], "yh", down)
-    near = jnp.stack([mine, below, above])
-    near_other = lax.ppermute(near, "core", cross)
-    far = jnp.concatenate([far_low, far_high])
-    far_other = lax.ppermute(far, "core", cross)
-    part = multiply(pieces, early(near), far, near_other, far_other)
+    below, far, above = (lax.ppermute(mine, "yh", away[d]) for d in (1, 2, 3))
+    tick = lax.ppermute(piece[BS:], "core", cross)
+    pieces = lax.all_to_all(spread(piece, tick), "col", 0, 0)
+    wanted = lax.dynamic_slice_in_dim(pieces.reshape(N_YH, 3, LMSG, 128), 1 - yl, 2, 1)
+    pieces_other = lax.ppermute(wanted.reshape(2 * N_YH, LMSG, 128), "yl", cross)
+    near = (jnp.stack([mine, below]), jnp.stack([above, far]))
+    near_other = [lax.ppermute(two, "core", cross) for two in near]
+    part = multiply(pieces, pieces_other, early(*near), *near_other)
     parts = lax.all_to_all(part, ("yl", "layer"), 0, 0)
     total = jnp.sum(parts.astype(jnp.float32), axis=0)
     return total.reshape(1, BS, COLUMNS // N_LAYER, BS)

time: 88.6 us -> 84.4 us (0.953)
  the two profiles are of different devices: /device:TPU:16 before, /device:TPU:1 now
where the time goes in v6:
time: 84.4 us; the launch traced here: 83.5 us
  starting transfers between devices  45.4 us (54%)
  Pallas kernels  14.7 us (17%)
  blocking collectives  12.6 us (15%)
  waiting for transfers between devices  7.34 us (9%)
  local copies, waits for them, and re-layouts  2.09 us (2%)
  other arithmetic  1.12 us (1%)
    ppermute x3, starting transfers between devices, shards(): below, far, above = (lax.ppermute(mine, 'yh', away[d]) for d in (1, 2, 3))  14.5 us
    all_to_all x1, blocking collectives, shards(): parts = lax.all_to_all(part, ('yl', 'layer'), 0, 0)  12.6 us
    all_to_all x1, starting transfers between devices, shards(): pieces = lax.all_to_all(spread(piece, tick), 'col', 0, 0)  12 us
    ppermute x1, starting transfers between devices, shards(): lax.ppermute(wanted.reshape(2 * N_YH, LMSG, 128), 'yl', cross)  7.05 us
    ppermute x3, waiting for transfers between devices, shards(): below, far, above = (lax.ppermute(mine, 'yh', away[d]) for d in (1, 2, 3))  6.53 us
    pallas_call x1, Pallas kernels, multiply(): pl.pallas_call(multiply_kernel, out_shape=jax.ShapeDtypeStruct((2 * N_LAY...  6.26 us
    ppermute x1, starting transfers between devices, shards(): tick = lax.ppermute(piece[BS:], 'core', cross)  6.01 us
    ppermute x2, starting transfers between devices, shards(): near_other = [lax.ppermute(two, 'core', cross) for two in near]  5.94 us
  transfers between devices with their start and end apart: 8, of which 2 were waited for; matrix products, arithmetic and copies ran while one was open for 2% of the time, Pallas kernels for 8%

profile of v6, /device:TPU:1, one launch (start us, length us, event | category | flops | bytes accessed | tf_op | source)
XLA Modules:
  0.0 83.5 jit_solution(2597159316150411588)
XLA Ops:
  0.0 1.9 %shard_map.46 = (bf16[1040,128]{1,0:T(8,128)(2,1)}, bf16[80,128]{1,0:T(8,128)(2,1)}) custom-call(bf16[32,64,64]{2,1,0:T(8,128)(2,1)} %bitcast.13, s32[2,32]{1,0:T(2,128)} %bitcast.20, bf16[2,64,64]{2,1,0:T(8,128)(2,1)} %bitcast.19, s32[2,2]{1,0:T(2,128)} %bitcast.21), custom_call_target="tpu_custom_call" | custom-call | bytes 2097152 | tf_op jit(solution)/shard_map/pallas_call | solution.py:53
  1.9 8.3 %collective-permute-start.4 = (bf16[1040,128]{1,0:T(8,128)(2,1)}, bf16[1040,128]{1,0:T(8,128)(2,1)S(1)}, u32[]{:S(2)}, u32[]{:S(2)}) collective-permute-start(bf16[1040,128]{1,0:T(8,128)(2,1)} %get-tuple-element.8), channel_id=1, source_target_pairs={{0,384},{192,576},{384,0},{576,192},{1,385},{193,577},{385,1},{577... | collective-permute-start | bytes 798728 | tf_op jit(solution)/shard_map/ppermute | solution.py:245
  10.2 2.0 %collective-permute-start.3 = (bf16[1040,128]{1,0:T(8,128)(2,1)}, bf16[1040,128]{1,0:T(8,128)(2,1)S(1)}, u32[]{:S(2)}, u32[]{:S(2)}) collective-permute-start(bf16[1040,128]{1,0:T(8,128)(2,1)} %get-tuple-element.8), channel_id=1, source_target_pairs={{0,576},{192,0},{384,192},{576,384},{1,577},{193,1},{385,193},{577... | collective-permute-start | bytes 798728 | tf_op jit(solution)/shard_map/ppermute | solution.py:245
  12.2 0.7 slice.3
  12.8 6.0 %collective-permute-start = (bf16[16,128]{1,0:T(8,128)(2,1)S(1)}, bf16[16,128]{1,0:T(8,128)(2,1)S(1)}, u32[]{:S(2)}, u32[]{:S(2)}) collective-permute-start(bf16[16,128]{1,0:T(8,128)(2,1)S(1)} %slice.3), channel_id=1, source_target_pairs={{0,48},{48,0},{1,49},{49,1},{2,50},{50,2},{3,51},{51,3},{4,52},{52... | collective-permute-start | bytes 12296 | tf_op jit(solution)/shard_map/ppermute | solution.py:246
  18.9 0.8 collective-permute-done.when
  19.7 0.0 copy-start
  19.7 0.6 copy-done
  20.2 1.5 %shard_map.47 = bf16[12,80,128]{2,1,0:T(8,128)(2,1)} custom-call(bf16[80,128]{1,0:T(8,128)(2,1)} %get-tuple-element.7.piece, bf16[16,128]{1,0:T(8,128)(2,1)} %copy-done), custom_call_target="tpu_custom_call" | custom-call | bytes 1048576 | tf_op jit(solution)/shard_map/pallas_call | solution.py:226
  21.7 12.0 %all-to-all-start = ((bf16[12,80,128]{2,1,0:T(8,128)(2,1)}), bf16[12,80,128]{2,1,0:T(8,128)(2,1)S(1)}, u32[]{:S(2)}, u32[]{:S(2)}) async-start(bf16[12,80,128]{2,1,0:T(8,128)(2,1)} %shard_map.47), calls=%async_computation | async-start | bytes 491520 | tf_op jit(solution)/shard_map/all_to_all | solution.py:247
  33.7 4.2 %collective-permute-start.2 = (bf16[1040,128]{1,0:T(8,128)(2,1)}, bf16[1040,128]{1,0:T(8,128)(2,1)S(1)}, u32[]{:S(2)}, u32[]{:S(2)}) collective-permute-start(bf16[1040,128]{1,0:T(8,128)(2,1)} %get-tuple-element.8), channel_id=1, source_target_pairs={{0,192},{192,384},{384,576},{576,0},{1,193},{193,385},{385,577},{5... | collective-permute-start | bytes 798728 | tf_op jit(solution)/shard_map/ppermute | solution.py:245
  37.9 0.0 collective-permute-done.4
  38.0 0.0 collective-permute-done.3
  38.0 0.1 pad_maximum_fusion.1.second
  38.0 2.8 %collective-permute-start.6 = (bf16[2,1040,128]{2,1,0:T(8,128)(2,1)S(1)}, bf16[2,1040,128]{2,1,0:T(8,128)(2,1)S(1)}, u32[]{:S(2)}, u32[]{:S(2)}) collective-permute-start(bf16[2,1040,128]{2,1,0:T(8,128)(2,1)S(1)} %pad_maximum_fusion.1.second), channel_id=1, source_target_pairs={{0,48},{48,0},{1,49},{49,1},{2,50},{50,2},{3,51},{51,3},{4,52},{52... | collective-permute-start | bytes 1597448 | tf_op jit(solution)/shard_map/ppermute | solution.py:251
  40.8 6.5 %collective-permute-done.2 = bf16[1040,128]{1,0:T(8,128)(2,1)S(1)} collective-permute-done((bf16[1040,128]{1,0:T(8,128)(2,1)}, bf16[1040,128]{1,0:T(8,128)(2,1)S(1)}, u32[]{:S(2)}, u32[]{:S(2)}) %collective-permute-start.2) | collective-permute-done | bytes 266272 | tf_op jit(solution)/shard_map/ppermute | solution.py:245
  47.4 1.0 %pad_maximum_fusion.first = bf16[2,1040,128]{2,1,0:T(8,128)(2,1)S(1)} fusion(bf16[1,1040,128]{2,1,0:T(8,128)(2,1)S(1)} %bitcast.17, bf16[1,1040,128]{2,1,0:T(8,128)(2,1)} %bitcast.14), kind=kLoop, calls=%fused_computation.1 | loop fusion | flops 266240 | bytes 1064960 | tf_op jit(solution)/shard_map/stack | solution.py:250
  48.4 3.1 %collective-permute-start.5 = (bf16[2,1040,128]{2,1,0:T(8,128)(2,1)S(1)}, bf16[2,1040,128]{2,1,0:T(8,128)(2,1)S(1)}, u32[]{:S(2)}, u32[]{:S(2)}) collective-permute-start(bf16[2,1040,128]{2,1,0:T(8,128)(2,1)S(1)} %pad_maximum_fusion.first), channel_id=1, source_target_pairs={{0,48},{48,0},{1,49},{49,1},{2,50},{50,2},{3,51},{51,3},{4,52},{52... | collective-permute-start | bytes 1597448 | tf_op jit(solution)/shard_map/ppermute | solution.py:251
  51.5 0.0 all-to-all-done.left_own
  51.5 7.1 %collective-permute-start.1 = (bf16[8,80,128]{2,1,0:T(8,128)(2,1)S(1)}, bf16[8,80,128]{2,1,0:T(8,128)(2,1)S(1)}, u32[]{:S(2)}, u32[]{:S(2)}) collective-permute-start(bf16[8,80,128]{2,1,0:T(8,128)(2,1)S(1)} %bitcast.18), channel_id=1, source_target_pairs={{0,96},{96,0},{1,97},{97,1},{2,98},{98,2},{3,99},{99,3},{4,100},{1... | collective-permute-start | bytes 491528 | tf_op jit(solution)/shard_map/ppermute | solution.py:249
  58.6 5.1 %shard_map.48.ready = bf16[4,384,2048]{2,1,0:T(8,128)(2,1)} custom-call(bf16[2,1040,128]{2,1,0:T(8,128)(2,1)S(1)} %pad_maximum_fusion.first, bf16[2,1040,128]{2,1,0:T(8,128)(2,1)S(1)} %pad_maximum_fusion.1.second), custom_call_target="tpu_custom_call" | custom-call | flops 40000000000 | bytes 10485760 | tf_op jit(solution)/shard_map/pallas_call | solution.py:139
  63.7 0.0 collective-permute-done.6.second
  63.7 0.0 collective-permute-done.5.first
  63.7 0.0 collective-permute-done.1.left_other
  63.7 6.3 %shard_map.49 = bf16[8,64,512]{2,1,0:T(8,128)(2,1)S(1)} custom-call(bf16[12,80,128]{2,1,0:T(8,128)(2,1)S(1)} %all-to-all-done.left_own, bf16[8,80,128]{2,1,0:T(8,128)(2,1)S(1)} %collective-permute-done.1.left_other, bf16[4,384,2048]{2,1,0:T(8,128)(2,1)} %shard_map.48.ready, bf16[2,1040,128]{2,1,0:T(8,128)(2,1)S(1)} %collective-permute-done.5.first, ...), custom_call_target="tpu_custom_call" | custom-call | flops 1610612736 | bytes 4194304 | tf_op jit(solution)/shard_map/pallas_call | solution.py:200
  70.0 12.6 %all_to_all.10 = bf16[8,64,512]{2,1,0:T(8,128)(2,1)S(1)} all-to-all(bf16[8,64,512]{2,1,0:T(8,128)(2,1)S(1)} %shard_map.49), channel_id=1, replica_groups=mesh['yh'=4,'yl'=2,'core'=2,'col'=12,'layer'=4] {'yl','layer'}, dimensions={0} | all-to-all | bytes 1048576 | tf_op jit(solution)/shard_map/all_to_all | solution.py:253
  82.6 0.1 convert_reduce_fusion
  82.7 0.8 reshape.27
  (1 shorter events, 0.0 us)
Async XLA Ops:
  1.9 36.0 %collective-permute-start.4 = (bf16[1040,128]{1,0:T(8,128)(2,1)}, bf16[1040,128]{1,0:T(8,128)(2,1)S(1)}, u32[]{:S(2)}, u32[]{:S(2)}) collective-permute-start(bf16[1040,128]{1,0:T(8,128)(2,1)} %get-tuple-element.8), channel_id=1, source_target_pairs={{0,384},{192,576},{384,0},{576,192},{1,385},{193,577},{385,1},{577... | collective-permute-start | bytes 798728 | tf_op jit(solution)/shard_map/ppermute | solution.py:245
  10.2 27.8 %collective-permute-start.3 = (bf16[1040,128]{1,0:T(8,128)(2,1)}, bf16[1040,128]{1,0:T(8,128)(2,1)S(1)}, u32[]{:S(2)}, u32[]{:S(2)}) collective-permute-start(bf16[1040,128]{1,0:T(8,128)(2,1)} %get-tuple-element.8), channel_id=1, source_target_pairs={{0,576},{192,0},{384,192},{576,384},{1,577},{193,1},{385,193},{577... | collective-permute-start | bytes 798728 | tf_op jit(solution)/shard_map/ppermute | solution.py:245
  12.8 6.8 %collective-permute-start = (bf16[16,128]{1,0:T(8,128)(2,1)S(1)}, bf16[16,128]{1,0:T(8,128)(2,1)S(1)}, u32[]{:S(2)}, u32[]{:S(2)}) collective-permute-start(bf16[16,128]{1,0:T(8,128)(2,1)S(1)} %slice.3), channel_id=1, source_target_pairs={{0,48},{48,0},{1,49},{49,1},{2,50},{50,2},{3,51},{51,3},{4,52},{52... | collective-permute-start | bytes 12296 | tf_op jit(solution)/shard_map/ppermute | solution.py:246
  19.7 0.6 copy-start
  21.7 29.8 %all-to-all-start = ((bf16[12,80,128]{2,1,0:T(8,128)(2,1)}), bf16[12,80,128]{2,1,0:T(8,128)(2,1)S(1)}, u32[]{:S(2)}, u32[]{:S(2)}) async-start(bf16[12,80,128]{2,1,0:T(8,128)(2,1)} %shard_map.47), calls=%async_computation | async-start | bytes 491520 | tf_op jit(solution)/shard_map/all_to_all | solution.py:247
  33.7 13.7 %collective-permute-start.2 = (bf16[1040,128]{1,0:T(8,128)(2,1)}, bf16[1040,128]{1,0:T(8,128)(2,1)S(1)}, u32[]{:S(2)}, u32[]{:S(2)}) collective-permute-start(bf16[1040,128]{1,0:T(8,128)(2,1)} %get-tuple-element.8), channel_id=1, source_target_pairs={{0,192},{192,384},{384,576},{576,0},{1,193},{193,385},{385,577},{5... | collective-permute-start | bytes 798728 | tf_op jit(solution)/shard_map/ppermute | solution.py:245
  38.0 25.7 %collective-permute-start.6 = (bf16[2,1040,128]{2,1,0:T(8,128)(2,1)S(1)}, bf16[2,1040,128]{2,1,0:T(8,128)(2,1)S(1)}, u32[]{:S(2)}, u32[]{:S(2)}) collective-permute-start(bf16[2,1040,128]{2,1,0:T(8,128)(2,1)S(1)} %pad_maximum_fusion.1.second), channel_id=1, source_target_pairs={{0,48},{48,0},{1,49},{49,1},{2,50},{50,2},{3,51},{51,3},{4,52},{52... | collective-permute-start | bytes 1597448 | tf_op jit(solution)/shard_map/ppermute | solution.py:251
  48.4 15.3 %collective-permute-start.5 = (bf16[2,1040,128]{2,1,0:T(8,128)(2,1)S(1)}, bf16[2,1040,128]{2,1,0:T(8,128)(2,1)S(1)}, u32[]{:S(2)}, u32[]{:S(2)}) collective-permute-start(bf16[2,1040,128]{2,1,0:T(8,128)(2,1)S(1)} %pad_maximum_fusion.first), channel_id=1, source_target_pairs={{0,48},{48,0},{1,49},{49,1},{2,50},{50,2},{3,51},{51,3},{4,52},{52... | collective-permute-start | bytes 1597448 | tf_op jit(solution)/shard_map/ppermute | solution.py:251
  51.5 12.2 %collective-permute-start.1 = (bf16[8,80,128]{2,1,0:T(8,128)(2,1)S(1)}, bf16[8,80,128]{2,1,0:T(8,128)(2,1)S(1)}, u32[]{:S(2)}, u32[]{:S(2)}) collective-permute-start(bf16[8,80,128]{2,1,0:T(8,128)(2,1)S(1)} %bitcast.18), channel_id=1, source_target_pairs={{0,96},{96,0},{1,97},{97,1},{2,98},{98,2},{3,99},{99,3},{4,100},{1... | collective-permute-start | bytes 491528 | tf_op jit(solution)/shard_map/ppermute | solution.py:249

commit v7 on v3

--- a/solution.py
+++ b/solution.py
@@ -25,15 +25,36 @@
 WINDOW = 2 * PIECE * BS
 
 
-def pack_kernel(right, right_where, left, left_where, out, piece, tail):
+def pack_left_kernel(left, left_where, out):
+    base = lax.axis_index("layer") * (NB // N_LAYER) + lax.axis_index("col") * PIECE
+    out[:BS, :] = jnp.concatenate([left[0], left[1]], axis=-1)
+    lane = lax.broadcasted_iota(jnp.int32, (16, 128), 1)
+    first = jnp.broadcast_to(left_where[0:1, 1:2], (16, 128))
+    second = jnp.broadcast_to(left_where[1:2, 1:2], (16, 128))
+    at = jnp.where(lane < BS, first, second) - base
+    out[BS:, :] = at.astype(jnp.float32).astype(jnp.bfloat16)
+
+
+def pack_left(left, left_where):
+    vmem = pl.BlockSpec(memory_space=pltpu.VMEM)
+    return pl.pallas_call(
+        pack_left_kernel,
+        out_shape=jax.ShapeDtypeStruct((LMSG, 128), jnp.bfloat16),
+        in_specs=[vmem] * 2,
+        out_specs=vmem,
+        cost_estimate=pl.CostEstimate(flops=0, bytes_accessed=1 << 16, transcendentals=0),
+    )(left, left_where)
+
+
+def pack_kernel(right, right_where, pair, out, rows, tail):
     y = lax.axis_index("yh") * 2 + lax.axis_index("yl")
     core = lax.axis_index("core")
     col = lax.axis_index("col")
     base = lax.axis_index("layer") * (NB // N_LAYER)
     for p in range(PAIRS):
-        pair = jnp.concatenate([right[p], right[p + PAIRS]], axis=-1)
+        both = jnp.concatenate([right[p], right[p + PAIRS]], axis=-1)
         for q in range(N_YH):
-            out[q, p * BS : (p + 1) * BS, :] = pair
+            out[q, p * BS : (p + 1) * BS, :] = both
     tail[...] = jnp.zeros_like(tail)
     inner = right_where[0:1, :] - (base + (y * 2 + core) * INNER)
     column = right_where[1:2, :] - col * COLUMNS
@@ -41,29 +62,26 @@
     tail[1:2, 0:SLOTS] = column.astype(jnp.float32)
     for q in range(N_YH):
         out[q, BODY:MSG, :] = tail[...].astype(jnp.bfloat16)
-    lane = lax.broadcasted_iota(jnp.int32, (16, 128), 1)
-    first = jnp.broadcast_to(left_where[0:1, 1:2], (16, 128))
-    second = jnp.broadcast_to(left_where[1:2, 1:2], (16, 128))
-    at = jnp.where(lane < BS, first, second) - (base + col * PIECE)
-    at = at.astype(jnp.float32).astype(jnp.bfloat16)
-    pair = jnp.concatenate([left[0], left[1]], axis=-1)
-    piece[:BS, :] = pair
-    piece[BS:, :] = at
-
-
-def pack(right, right_where, left, left_where):
+    for m in range(2):
+        rows[m * BS : (m + 1) * BS, :] = pair[m, :BS, :]
+    first = lax.broadcasted_iota(jnp.int32, (16, 128), 0) == 0
+    marks = jnp.where(first, pair[0, BS:, :].astype(jnp.float32), pair[1, BS:, :].astype(jnp.float32))
+    rows[2 * BS :, :] = marks.astype(jnp.bfloat16)
+
+
+def pack(right, right_where, pair):
     vmem = pl.BlockSpec(memory_space=pltpu.VMEM)
     return pl.pallas_call(
         pack_kernel,
         out_shape=(
             jax.ShapeDtypeStruct((N_YH, MSG, 128), jnp.bfloat16),
-            jax.ShapeDtypeStruct((LMSG, 128), jnp.bfloat16),
+            jax.ShapeDtypeStruct((2 * BS + 16, 128), jnp.bfloat16),
         ),
-        in_specs=[vmem] * 4,
+        in_specs=[vmem] * 3,
         out_specs=(vmem, vmem),
         scratch_shapes=[pltpu.VMEM((16, 128), jnp.float32)],
         cost_estimate=pl.CostEstimate(flops=0, bytes_accessed=2 << 20, transcendentals=0),
-    )(right, right_where, left, left_where)
+    )(right, right_where, pair)
 
 
 def half_swap():
@@ -103,7 +121,7 @@
     lax.fori_loop(0, PAIRS, place, 0, unroll=2)
 
 
-def place_kernel(own, other, left_own, left_other, out, left, total, where, places, sem, *scratch):
+def place_kernel(own, other, pieces, out, left, total, where, places, sem, *scratch):
     panels, swapped = scratch[:GROUP], scratch[GROUP:]
     yl = lax.axis_index("yl")
     core = lax.axis_index("core")
@@ -113,17 +131,18 @@
 
     lane = lax.broadcasted_iota(jnp.int32, (BS, 128), 1)
     upper = (lane >= BS).astype(jnp.float32)
-    for src, at in ((left_own, yl), (left_other, 1 - yl)):
-        rows = pl.ds(pl.multiple_of(at * BS, BS), BS)
-        for q in range(N_YH):
-            for u in range(2):
-                whole = src[3 * q + yl + u] if src is left_own else src[2 * q + u]
-                there = jnp.dot(whole, swap, preferred_element_type=jnp.float32)
-                here = whole.astype(jnp.float32)
+    for q in range(N_YH):
+        for u in range(2):
+            whole = pieces[3 * q + yl + u]
+            there = jnp.dot(whole, swap, preferred_element_type=jnp.float32)
+            here = whole.astype(jnp.float32)
+            for m in range(2):
+                rows = slice(m * BS, (m + 1) * BS)
+                mark = 2 * BS + m
                 for g in range(PIECE // 2):
                     want = upper + 2.0 * g
-                    value = jnp.where(here[BS : BS + 1] == want, here[:BS], 0.0)
-                    value = value + jnp.where(there[BS : BS + 1] == want, there[:BS], 0.0)
+                    value = jnp.where(here[mark : mark + 1] == want, here[rows], 0.0)
+                    value = value + jnp.where(there[mark : mark + 1] == want, there[rows], 0.0)
                     at_lane = q * WINDOW + (u * PIECE + 2 * g) * BS
                     left[rows, at_lane : at_lane + 128] = value.astype(jnp.bfloat16)
 
@@ -190,20 +209,14 @@
 
 
 def shards(left_blocks, left_coords, right_blocks, right_coords):
-    mine, piece = pack(
-        right_blocks.reshape(SLOTS, BS, BS),
-        right_coords.reshape(SLOTS, 2).T,
-        left_blocks.reshape(2, BS, BS),
-        left_coords.reshape(2, 2),
+    pair = lax.all_gather(pack_left(left_blocks.reshape(2, BS, BS), left_coords.reshape(2, 2)), "yl")
+    mine, rows = pack(
+        right_blocks.reshape(SLOTS, BS, BS), right_coords.reshape(SLOTS, 2).T, pair
     )
-    yl = lax.axis_index("yl")
     own = lax.all_to_all(mine, "yh", 0, 0)
-    pieces = lax.all_gather(piece, "col")
-    wanted = lax.dynamic_slice_in_dim(pieces.reshape(N_YH, 3, LMSG, 128), 1 - yl, 2, 1)
-    wanted = wanted.reshape(2 * N_YH, LMSG, 128)
+    pieces = lax.all_gather(rows, "col")
     other = lax.ppermute(after(own, pieces), "core", [(0, 1), (1, 0)])
-    pieces_other = lax.ppermute(wanted, "yl", [(0, 1), (1, 0)])
-    part = multiply(own, other, pieces, pieces_other)
+    part = multiply(own, other, pieces)
     parts = lax.all_to_all(part, ("yl", "layer"), 0, 0)
     total = jnp.sum(parts.astype(jnp.float32), axis=0)
     return total.reshape(1, BS, COLUMNS // N_LAYER, BS)

time: 78.7 us -> 81.3 us (1.033)
  the two profiles are of different devices: /device:TPU:16 before, /device:TPU:1 now
where the time goes in v7:
time: 81.3 us; the launch traced here: 80.1 us
  blocking collectives  50.4 us (62%)
  starting transfers between devices  15 us (18%)
  Pallas kernels  10.4 us (13%)
  waiting for transfers between devices  2.5 us (3%)
  local copies, waits for them, and re-layouts  1.78 us (2%)
    all_gather x1, blocking collectives, shards(): pieces = lax.all_gather(rows, 'col')  31.5 us
    all_to_all x1, blocking collectives, shards(): parts = lax.all_to_all(part, ('yl', 'layer'), 0, 0)  13.3 us
    ppermute x1, starting transfers between devices, shards(): other = lax.ppermute(after(own, pieces), 'core', [(0, 1), (1, 0)])  8.92 us
    pallas_call x1, Pallas kernels, multiply(): pl.pallas_call(place_kernel, out_shape=jax.ShapeDtypeStruct((2 * N_LAYER,...  6.65 us
    all_to_all x1, starting transfers between devices, shards(): own = lax.all_to_all(mine, 'yh', 0, 0)  6.05 us
    all_gather x1, blocking collectives, shards(): lax.all_gather(pack_left(left_blocks.reshape(2, BS, BS), left_coords.resh...  5.58 us
    ppermute x1, waiting for transfers between devices, shards(): other = lax.ppermute(after(own, pieces), 'core', [(0, 1), (1, 0)])  2.5 us
    pallas_call x1, Pallas kernels, pack(): pl.pallas_call(pack_kernel, out_shape=(jax.ShapeDtypeStruct((N_YH, MSG, 1...  2.24 us
  transfers between devices with their start and end apart: 2, of which 1 were waited for; matrix products, arithmetic and copies ran while one was open for 0% of the time, Pallas kernels for 0%

profile of v7, /device:TPU:1, one launch (start us, length us, event | category | flops | bytes accessed | tf_op | source)
XLA Modules:
  0.0 80.1 jit_solution(1481862991421546957)
XLA Ops:
  0.0 1.5 %shard_map.46 = bf16[80,128]{1,0:T(8,128)(2,1)} custom-call(bf16[2,64,64]{2,1,0:T(8,128)(2,1)} %bitcast.12, s32[2,2]{1,0:T(2,128)} %bitcast.14), custom_call_target="tpu_custom_call" | custom-call | bytes 65536 | tf_op jit(solution)/shard_map/pallas_call | solution.py:40
  1.5 5.6 %all-gather = bf16[160,128]{1,0:T(8,128)(2,1)} all-gather(bf16[80,128]{1,0:T(8,128)(2,1)} %shard_map.46), channel_id=2, replica_groups=mesh['yh'=4,'yl'=2,'core'=2,'col'=12,'layer'=4] {'yl'}, dimensions={0}, use_global_device_ids=true | all-gather | bytes 61440 | tf_op jit(solution)/shard_map/all_gather | solution.py:212
  7.1 2.2 %shard_map.47 = (bf16[4,1040,128]{2,1,0:T(8,128)(2,1)}, bf16[144,128]{1,0:T(8,128)(2,1)}) custom-call(bf16[32,64,64]{2,1,0:T(8,128)(2,1)} %bitcast.10, s32[2,32]{1,0:T(2,128)} %bitcast.13, bf16[2,80,128]{2,1,0:T(8,128)(2,1)} %bitcast.11), custom_call_target="tpu_custom_call" | custom-call | bytes 2097152 | tf_op jit(solution)/shard_map/pallas_call | solution.py:74
  9.3 0.0 copy-start.1
  9.3 6.0 %all-to-all-start = ((bf16[4,1040,128]{2,1,0:T(8,128)(2,1)}), bf16[4,1040,128]{2,1,0:T(8,128)(2,1)S(1)}, u32[]{:S(2)}, u32[]{:S(2)}) async-start(bf16[4,1040,128]{2,1,0:T(8,128)(2,1)} %get-tuple-element.7), calls=%async_computation | async-start | bytes 2129920 | tf_op jit(solution)/shard_map/all_to_all | solution.py:216
  15.3 0.0 copy-done.1
  15.3 31.5 %all-gather.1 = bf16[1728,128]{1,0:T(8,128)(2,1)} all-gather(bf16[144,128]{1,0:T(8,128)(2,1)S(1)} %copy-done.1), channel_id=3, replica_groups=mesh['yh'=4,'yl'=2,'core'=2,'col'=12,'layer'=4] {'col'}, dimensions={0}, use_global_device_ids=true | all-gather | bytes 479232 | tf_op jit(solution)/shard_map/all_gather | solution.py:217
  46.8 0.0 all-to-all-done.own
  46.8 1.0 %copy.6.whole = bf16[4,1040,128]{2,1,0:T(8,128)(2,1)} copy(bf16[4,1040,128]{2,1,0:T(8,128)(2,1)S(1)} %all-to-all-done.own) | data formatting | bytes 2129920
  47.8 0.0 copy-start
  47.8 8.9 %collective-permute-start = (bf16[4,1040,128]{2,1,0:T(8,128)(2,1)}, bf16[4,1040,128]{2,1,0:T(8,128)(2,1)S(1)}, u32[]{:S(2)}, u32[]{:S(2)}) collective-permute-start(bf16[4,1040,128]{2,1,0:T(8,128)(2,1)} %shard_map.48), channel_id=1, source_target_pairs={{0,48},{48,0},{1,49},{49,1},{2,50},{50,2},{3,51},{51,3},{4,52},{52... | collective-permute-start | bytes 3194888 | tf_op jit(solution)/shard_map/ppermute | solution.py:218
  56.7 2.5 %collective-permute-done.other = bf16[4,1040,128]{2,1,0:T(8,128)(2,1)S(1)} collective-permute-done((bf16[4,1040,128]{2,1,0:T(8,128)(2,1)}, bf16[4,1040,128]{2,1,0:T(8,128)(2,1)S(1)}, u32[]{:S(2)}, u32[]{:S(2)}) %collective-permute-start) | collective-permute-done | bytes 1064992 | tf_op jit(solution)/shard_map/ppermute | solution.py:218
  59.2 0.0 copy-done
  59.2 6.7 %shard_map.49 = bf16[8,64,512]{2,1,0:T(8,128)(2,1)S(1)} custom-call(bf16[4,1040,128]{2,1,0:T(8,128)(2,1)S(1)} %all-to-all-done.own, bf16[4,1040,128]{2,1,0:T(8,128)(2,1)S(1)} %collective-permute-done.other, bf16[12,144,128]{2,1,0:T(8,128)(2,1)S(1)} %bitcast.9), custom_call_target="tpu_custom_call" | custom-call | flops 1610612736 | bytes 4194304 | tf_op jit(solution)/shard_map/pallas_call | solution.py:176
  65.9 13.3 %all_to_all.10 = bf16[8,64,512]{2,1,0:T(8,128)(2,1)S(1)} all-to-all(bf16[8,64,512]{2,1,0:T(8,128)(2,1)S(1)} %shard_map.49), channel_id=1, replica_groups=mesh['yh'=4,'yl'=2,'core'=2,'col'=12,'layer'=4] {'yl','layer'}, dimensions={0} | all-to-all | bytes 1048576 | tf_op jit(solution)/shard_map/all_to_all | solution.py:220
  79.2 0.1 convert_reduce_fusion
  79.3 0.8 %reshape.19 = f32[1,64,8,64]{3,2,1,0:T(8,128)} reshape(f32[64,512]{1,0:T(8,128)S(1)} %convert_reduce_fusion) | data formatting | bytes 262144 | tf_op jit(solution)/shard_map/reshape | solution.py:222
  (1 shorter events, 0.0 us)
Async XLA Ops:
  9.3 6.1 %copy-start.1 = (bf16[144,128]{1,0:T(8,128)(2,1)S(1)}, bf16[144,128]{1,0:T(8,128)(2,1)}, u32[]{:S(2)}) copy-start(bf16[144,128]{1,0:T(8,128)(2,1)} %get-tuple-element.8) | copy-start | bytes 110596
  9.3 37.5 %all-to-all-start = ((bf16[4,1040,128]{2,1,0:T(8,128)(2,1)}), bf16[4,1040,128]{2,1,0:T(8,128)(2,1)S(1)}, u32[]{:S(2)}, u32[]{:S(2)}) async-start(bf16[4,1040,128]{2,1,0:T(8,128)(2,1)} %get-tuple-element.7), calls=%async_computation | async-start | bytes 2129920 | tf_op jit(solution)/shard_map/all_to_all | solution.py:216
  47.8 11.4 %copy-start = (bf16[1728,128]{1,0:T(8,128)(2,1)S(1)}, bf16[1728,128]{1,0:T(8,128)(2,1)}, u32[]{:S(2)}) copy-start(bf16[1728,128]{1,0:T(8,128)(2,1)} %all-gather.1) | copy-start | bytes 1327108
  47.8 11.4 %collective-permute-start = (bf16[4,1040,128]{2,1,0:T(8,128)(2,1)}, bf16[4,1040,128]{2,1,0:T(8,128)(2,1)S(1)}, u32[]{:S(2)}, u32[]{:S(2)}) collective-permute-start(bf16[4,1040,128]{2,1,0:T(8,128)(2,1)} %shard_map.48), channel_id=1, source_target_pairs={{0,48},{48,0},{1,49},{49,1},{2,50},{50,2},{3,51},{51,3},{4,52},{52... | collective-permute-start | bytes 3194888 | tf_op jit(solution)/shard_map/ppermute | solution.py:218

commit v8 on v4

--- a/solution.py
+++ b/solution.py
@@ -8,7 +8,7 @@
 
 NB = 384
 BS = 64
-N_YH = 4
+N_Y = 8
 N_COL = 12
 N_LAYER = 4
 SLOTS = 32
@@ -22,22 +22,24 @@
 DEPTH = INNER * BS
 WIDTH = COLUMNS * BS
 GROUP = 4
-WINDOW = 2 * PIECE * BS
 
 
 def pack_kernel(right, right_where, left, left_where, out, piece, tail):
-    y = lax.axis_index("yh") * 2 + lax.axis_index("yl")
+    y = lax.axis_index("y")
     core = lax.axis_index("core")
     col = lax.axis_index("col")
     base = lax.axis_index("layer") * (NB // N_LAYER)
     for p in range(PAIRS):
-        out[p * BS : (p + 1) * BS, :] = jnp.concatenate([right[p], right[p + PAIRS]], axis=-1)
+        pair = jnp.concatenate([right[p], right[p + PAIRS]], axis=-1)
+        for q in range(N_Y):
+            out[q, p * BS : (p + 1) * BS, :] = pair
     tail[...] = jnp.zeros_like(tail)
     inner = right_where[0:1, :] - (base + (y * 2 + core) * INNER)
     column = right_where[1:2, :] - col * COLUMNS
     tail[0:1, 0:SLOTS] = inner.astype(jnp.float32)
     tail[1:2, 0:SLOTS] = column.astype(jnp.float32)
-    out[BODY:MSG, :] = tail[...].astype(jnp.bfloat16)
+    for q in range(N_Y):
+        out[q, BODY:MSG, :] = tail[...].astype(jnp.bfloat16)
     lane = lax.broadcasted_iota(jnp.int32, (16, 128), 1)
     first = jnp.broadcast_to(left_where[0:1, 1:2], (16, 128))
     second = jnp.broadcast_to(left_where[1:2, 1:2], (16, 128))
@@ -53,7 +55,7 @@
     return pl.pallas_call(
         pack_kernel,
         out_shape=(
-            jax.ShapeDtypeStruct((MSG, 128), jnp.bfloat16),
+            jax.ShapeDtypeStruct((N_Y, MSG, 128), jnp.bfloat16),
             jax.ShapeDtypeStruct((LMSG, 128), jnp.bfloat16),
         ),
         in_specs=[vmem] * 4,
@@ -100,30 +102,43 @@
     lax.fori_loop(0, PAIRS, place, 0, unroll=2)
 
 
-def place_kernel(gathered, left_own, left_other, out, left, total, where, places, sem, *scratch):
+def left_kernel(left_own, left_other, left):
+    core = lax.axis_index("core")
+    swap = half_swap()
+    lane = lax.broadcasted_iota(jnp.int32, (BS, 128), 1)
+    upper = (lane >= BS).astype(jnp.float32)
+    for src, at in ((left_own, core), (left_other, 1 - core)):
+        rows = pl.ds(pl.multiple_of(at * BS, BS), BS)
+        for c in range(N_COL):
+            whole = src[c]
+            there = jnp.dot(whole, swap, preferred_element_type=jnp.float32)
+            here = whole.astype(jnp.float32)
+            for g in range(PIECE // 2):
+                want = upper + 2.0 * g
+                value = jnp.where(here[BS : BS + 1] == want, here[:BS], 0.0)
+                value = value + jnp.where(there[BS : BS + 1] == want, there[:BS], 0.0)
+                at_lane = (c * PIECE + 2 * g) * BS
+                left[rows, at_lane : at_lane + 128] = value.astype(jnp.bfloat16)
+
+
+def left_panel(left_own, left_other):
+    vmem = pl.BlockSpec(memory_space=pltpu.VMEM)
+    return pl.pallas_call(
+        left_kernel,
+        out_shape=jax.ShapeDtypeStruct((2 * BS, NB // N_LAYER * BS), jnp.bfloat16),
+        in_specs=[vmem] * 2,
+        out_specs=vmem,
+        cost_estimate=pl.CostEstimate(flops=0, bytes_accessed=2 << 20, transcendentals=0),
+    )(left_own, left_other)
+
+
+def place_kernel(own, left, out, total, where, places, sem, *scratch):
     panels, swapped = scratch[:GROUP], scratch[GROUP:]
-    yl = lax.axis_index("yl")
-    blocks = [gathered.at[j] for j in range(2 * N_YH)]
+    core = lax.axis_index("core")
+    blocks = [own.at[j] for j in range(N_Y)]
     copy = read_places(blocks, where, places, sem)
     swap = half_swap()
-
-    lane = lax.broadcasted_iota(jnp.int32, (BS, 128), 1)
-    upper = (lane >= BS).astype(jnp.float32)
-    for src, at in ((left_own, yl), (left_other, 1 - yl)):
-        rows = pl.ds(pl.multiple_of(at * BS, BS), BS)
-        for q in range(N_YH):
-            for u in range(2):
-                whole = src[3 * q + yl + u] if src is left_own else src[2 * q + u]
-                there = jnp.dot(whole, swap, preferred_element_type=jnp.float32)
-                here = whole.astype(jnp.float32)
-                for g in range(PIECE // 2):
-                    want = upper + 2.0 * g
-                    value = jnp.where(here[BS : BS + 1] == want, here[:BS], 0.0)
-                    value = value + jnp.where(there[BS : BS + 1] == want, there[:BS], 0.0)
-                    at_lane = q * WINDOW + (u * PIECE + 2 * g) * BS
-                    left[rows, at_lane : at_lane + 128] = value.astype(jnp.bfloat16)
-
-    for j0 in range(0, 2 * N_YH, GROUP):
+    for j0 in range(0, N_Y, GROUP):
         now = blocks[j0 : j0 + GROUP]
         for i, block in enumerate(now):
             panels[i][...] = jnp.zeros_like(panels[i])
@@ -134,11 +149,9 @@
             copy.wait()
         place_slots(now, j0, panels, swapped, places)
         for i in range(len(now)):
-            j = j0 + i
-            start = (j // 2) * WINDOW + yl * (4 * BS) + (j % 2) * DEPTH
-            at = pl.ds(pl.multiple_of(start, 128), DEPTH)
+            at = pl.ds(pl.multiple_of((2 * (j0 + i) + core) * DEPTH, 128), DEPTH)
             part = jnp.dot(left[:, at], panels[i][...], preferred_element_type=jnp.float32)
-            total[...] = part if j == 0 else total[...] + part
+            total[...] = part if j0 + i == 0 else total[...] + part
     share = WIDTH // N_LAYER
     for m in range(2):
         for s in range(N_LAYER):
@@ -147,15 +160,14 @@
             )
 
 
-def multiply(*operands):
+def multiply(own, left):
     vmem = pl.BlockSpec(memory_space=pltpu.VMEM)
     return pl.pallas_call(
         place_kernel,
         out_shape=jax.ShapeDtypeStruct((2 * N_LAYER, BS, WIDTH // N_LAYER), jnp.bfloat16),
-        in_specs=[vmem] * len(operands),
+        in_specs=[vmem] * 2,
         out_specs=vmem,
         scratch_shapes=[
-            pltpu.VMEM((2 * BS, N_YH * WINDOW), jnp.bfloat16),
             pltpu.VMEM((2 * BS, WIDTH), jnp.float32),
             pltpu.VMEM((16, 128), jnp.int32),
             pltpu.SMEM((16, 128), jnp.int32),
@@ -167,7 +179,7 @@
         cost_estimate=pl.CostEstimate(
             flops=2 * 128 * 3072 * 2048, bytes_accessed=4 << 20, transcendentals=0
         ),
-    )(*operands)
+    )(own, left)
 
 
 def shards(left_blocks, left_coords, right_blocks, right_coords):
@@ -177,21 +189,18 @@
         left_blocks.reshape(2, BS, BS),
         left_coords.reshape(2, 2),
     )
-    yl = lax.axis_index("yl")
-    gathered = lax.all_gather(mine, ("yh", "core"))
+    own = lax.all_to_all(mine, "y", 0, 0)
     pieces = lax.all_gather(piece, "col")
-    wanted = lax.dynamic_slice_in_dim(pieces.reshape(N_YH, 3, LMSG, 128), 1 - yl, 2, 1)
-    wanted = wanted.reshape(2 * N_YH, LMSG, 128)
-    pieces_other = lax.ppermute(wanted, "yl", [(0, 1), (1, 0)])
-    part = multiply(gathered, pieces, pieces_other)
-    parts = lax.all_to_all(part, ("yl", "layer"), 0, 0)
+    pieces_other = lax.ppermute(pieces, "core", [(0, 1), (1, 0)])
+    part = multiply(own, left_panel(pieces, pieces_other))
+    parts = lax.all_to_all(part, ("core", "layer"), 0, 0)
     total = jnp.sum(parts.astype(jnp.float32), axis=0)
     return total.reshape(1, BS, COLUMNS // N_LAYER, BS)
 
 
 def solution(mesh):
-    grid = Mesh(mesh.devices.reshape(N_YH, 2, 2, N_COL, N_LAYER), ("yh", "yl", "core", "col", "layer"))
-    row = ("yh", "yl", "core")
+    grid = Mesh(mesh.devices.reshape(N_Y, 2, N_COL, N_LAYER), ("y", "core", "col", "layer"))
+    row = ("y", "core")
     return jax.shard_map(
         shards,
         mesh=grid,

time: 91.9 us -> 85.8 us (0.934)
  waiting for transfers between devices: 21.7 us -> 6.55 us
  between operations: 13.4 us -> 0.03 us
  starting transfers between devices: 3.21 us -> 14.6 us
  blocking collectives: 41.8 us -> 49.2 us
  Pallas kernels: 8.63 us -> 12.1 us
    ppermute x1, waiting for transfers between devices: 12.5 us -> 1.12 us  [shards(): pieces_other = lax.ppermute(pieces, 'core', [(0, 1), (1, 0)])]
    all_gather x1 -> x0, waiting for transfers between devices: 9.24 us -> none  [shards(): gathered = lax.all_gather(mine, ('yh', 'core'))]
    all_to_all x0 -> x1, starting transfers between devices: none -> 7.78 us  [shards(): own = lax.all_to_all(mine, 'y', 0, 0)]
    all_to_all x1, blocking collectives: 12.3 us -> 19.6 us  [shards(): parts = lax.all_to_all(part, ('core', 'layer'), 0, 0)]
    all_to_all x0 -> x1, waiting for transfers between devices: none -> 5.44 us  [shards(): own = lax.all_to_all(mine, 'y', 0, 0)]
    pallas_call x1 -> x2, Pallas kernels: 1.92 us -> 5.81 us  [the longest x1 3.04 us: left_panel(): pl.pallas_call(left_kernel, out_shape=jax.ShapeDtypeStruct((2 * BS, NB //...]
    ppermute x1, starting transfers between devices: 3.2 us -> 6.8 us  [shards(): pieces_other = lax.ppermute(pieces, 'core', [(0, 1), (1, 0)])]
    unnamed x2 -> x8, local copies, waits for them, and re-layouts: 1.6 us -> 2.1 us
  transfers between devices with their start and end apart: 2 -> 2, of which waited for: 2 -> 2; matrix products, arithmetic and copies ran while one was open for 0% -> 0% of each run, Pallas kernels for 0% -> 4%
where the time goes in v8:
time: 85.8 us; the launch traced here: 85.4 us
  blocking collectives  49.2 us (57%)
  starting transfers between devices  14.6 us (17%)
  Pallas kernels  12.1 us (14%)
  waiting for transfers between devices  6.55 us (8%)
  local copies, waits for them, and re-layouts  2.9 us (3%)
    all_gather x1, blocking collectives, shards(): pieces = lax.all_gather(piece, 'col')  29.6 us
    all_to_all x1, blocking collectives, shards(): parts = lax.all_to_all(part, ('core', 'layer'), 0, 0)  19.6 us
    all_to_all x1, starting transfers between devices, shards(): own = lax.all_to_all(mine, 'y', 0, 0)  7.78 us
    ppermute x1, starting transfers between devices, shards(): pieces_other = lax.ppermute(pieces, 'core', [(0, 1), (1, 0)])  6.8 us
    pallas_call x1, Pallas kernels, multiply(): pl.pallas_call(place_kernel, out_shape=jax.ShapeDtypeStruct((2 * N_LAYER,...  6.28 us
    all_to_all x1, waiting for transfers between devices, shards(): own = lax.all_to_all(mine, 'y', 0, 0)  5.44 us
    pallas_call x1, Pallas kernels, left_panel(): pl.pallas_call(left_kernel, out_shape=jax.ShapeDtypeStruct((2 * BS, NB //...  3.04 us
    pallas_call x1, Pallas kernels, pack(): pl.pallas_call(pack_kernel, out_shape=(jax.ShapeDtypeStruct((N_Y, MSG, 12...  2.77 us
  transfers between devices with their start and end apart: 2, of which 2 were waited for; matrix products, arithmetic and copies ran while one was open for 0% of the time, Pallas kernels for 4%

profile of v8, /device:TPU:1, one launch (start us, length us, event | category | flops | bytes accessed | tf_op | source)
XLA Modules:
  0.0 85.4 jit_solution(8947022280699185623)
XLA Ops:
  0.0 2.8 %shard_map.46 = (bf16[8,1040,128]{2,1,0:T(8,128)(2,1)}, bf16[80,128]{1,0:T(8,128)(2,1)}) custom-call(bf16[32,64,64]{2,1,0:T(8,128)(2,1)} %bitcast.9, s32[2,32]{1,0:T(2,128)} %bitcast.11, bf16[2,64,64]{2,1,0:T(8,128)(2,1)} %bitcast.10, s32[2,2]{1,0:T(2,128)} %bitcast.12), custom_call_target="tpu_custom_call" | custom-call | bytes 2097152 | tf_op jit(solution)/shard_map/pallas_call | solution.py:55
  2.8 0.0 copy-start.3
  2.8 7.8 %all-to-all-start = ((bf16[8,1040,128]{2,1,0:T(8,128)(2,1)}), bf16[8,1040,128]{2,1,0:T(8,128)(2,1)S(1)}, u32[]{:S(2)}, u32[]{:S(2)}) async-start(bf16[8,1040,128]{2,1,0:T(8,128)(2,1)} %get-tuple-element.7), calls=%async_computation | async-start | bytes 4259840 | tf_op jit(solution)/shard_map/all_to_all | solution.py:192
  10.6 0.0 copy-done.3
  10.6 29.6 %all-gather = bf16[960,128]{1,0:T(8,128)(2,1)S(1)} all-gather(bf16[80,128]{1,0:T(8,128)(2,1)S(1)} %copy-done.3), channel_id=2, replica_groups=mesh['y'=8,'core'=2,'col'=12,'layer'=4] {'col'}, dimensions={0}, use_global_device_ids=true | all-gather | bytes 266240 | tf_op jit(solution)/shard_map/all_gather | solution.py:193
  40.2 0.0 copy-start.1
  40.2 6.8 %collective-permute-start = (bf16[12,80,128]{2,1,0:T(8,128)(2,1)S(1)}, bf16[12,80,128]{2,1,0:T(8,128)(2,1)S(1)}, u32[]{:S(2)}, u32[]{:S(2)}) collective-permute-start(bf16[12,80,128]{2,1,0:T(8,128)(2,1)S(1)} %bitcast.7), channel_id=1, source_target_pairs={{0,48},{48,0},{1,49},{49,1},{2,50},{50,2},{3,51},{51,3},{4,52},{52... | collective-permute-start | bytes 737288 | tf_op jit(solution)/shard_map/ppermute | solution.py:194
  47.0 1.1 %collective-permute-done.left_other = bf16[12,80,128]{2,1,0:T(8,128)(2,1)S(1)} collective-permute-done((bf16[12,80,128]{2,1,0:T(8,128)(2,1)S(1)}, bf16[12,80,128]{2,1,0:T(8,128)(2,1)S(1)}, u32[]{:S(2)}, u32[]{:S(2)}) %collective-permute-start) | collective-permute-done | bytes 245792 | tf_op jit(solution)/shard_map/ppermute | solution.py:194
  48.1 0.0 copy-done.1
  48.1 0.0 copy-start.2
  48.1 0.7 copy-done.2
  48.8 3.0 %shard_map.47.left = bf16[128,6144]{1,0:T(8,128)(2,1)} custom-call(bf16[12,80,128]{2,1,0:T(8,128)(2,1)} %bitcast.8, bf16[12,80,128]{2,1,0:T(8,128)(2,1)} %copy-done.2), custom_call_target="tpu_custom_call" | custom-call | bytes 2097152 | tf_op jit(solution)/shard_map/pallas_call | solution.py:126
  51.8 5.4 %all-to-all-done.own = bf16[8,1040,128]{2,1,0:T(8,128)(2,1)S(1)} async-done(((bf16[8,1040,128]{2,1,0:T(8,128)(2,1)}), bf16[8,1040,128]{2,1,0:T(8,128)(2,1)S(1)}, u32[]{:S(2)}, u32[]{:S(2)}) %all-to-all-start) | async-done | bytes 2129952 | tf_op jit(solution)/shard_map/all_to_all | solution.py:192
  57.3 0.0 copy-start
  57.3 1.4 %copy-done = bf16[128,6144]{1,0:T(8,128)(2,1)S(1)} copy-done((bf16[128,6144]{1,0:T(8,128)(2,1)S(1)}, bf16[128,6144]{1,0:T(8,128)(2,1)}, u32[]{:S(2)}) %copy-start) | copy-done | bytes 1572888
  58.7 6.3 %shard_map.48 = bf16[8,64,512]{2,1,0:T(8,128)(2,1)S(1)} custom-call(bf16[8,1040,128]{2,1,0:T(8,128)(2,1)S(1)} %all-to-all-done.own, bf16[128,6144]{1,0:T(8,128)(2,1)S(1)} %copy-done), custom_call_target="tpu_custom_call" | custom-call | flops 1610612736 | bytes 4194304 | tf_op jit(solution)/shard_map/pallas_call | solution.py:165
  65.0 19.6 %all_to_all.10 = bf16[8,64,512]{2,1,0:T(8,128)(2,1)S(1)} all-to-all(bf16[8,64,512]{2,1,0:T(8,128)(2,1)S(1)} %shard_map.48), channel_id=1, replica_groups=mesh['y'=8,'core'=2,'col'=12,'layer'=4] {'core','layer'}, dimensions={0} | all-to-all | bytes 1048576 | tf_op jit(solution)/shard_map/all_to_all | solution.py:196
  84.6 0.1 convert_reduce_fusion
  84.6 0.8 reshape.19
Async XLA Ops:
  2.8 7.8 %copy-start.3 = (bf16[80,128]{1,0:T(8,128)(2,1)S(1)}, bf16[80,128]{1,0:T(8,128)(2,1)}, u32[]{:S(2)}) copy-start(bf16[80,128]{1,0:T(8,128)(2,1)} %get-tuple-element.8) | copy-start | bytes 61444
  2.8 54.5 %all-to-all-start = ((bf16[8,1040,128]{2,1,0:T(8,128)(2,1)}), bf16[8,1040,128]{2,1,0:T(8,128)(2,1)S(1)}, u32[]{:S(2)}, u32[]{:S(2)}) async-start(bf16[8,1040,128]{2,1,0:T(8,128)(2,1)} %get-tuple-element.7), calls=%async_computation | async-start | bytes 4259840 | tf_op jit(solution)/shard_map/all_to_all | solution.py:192
  40.2 7.9 %copy-start.1 = (bf16[960,128]{1,0:T(8,128)(2,1)}, bf16[960,128]{1,0:T(8,128)(2,1)S(1)}, u32[]{:S(2)}) copy-start(bf16[960,128]{1,0:T(8,128)(2,1)S(1)} %all-gather) | copy-start | bytes 737284
  40.2 7.9 %collective-permute-start = (bf16[12,80,128]{2,1,0:T(8,128)(2,1)S(1)}, bf16[12,80,128]{2,1,0:T(8,128)(2,1)S(1)}, u32[]{:S(2)}, u32[]{:S(2)}) collective-permute-start(bf16[12,80,128]{2,1,0:T(8,128)(2,1)S(1)} %bitcast.7), channel_id=1, source_target_pairs={{0,48},{48,0},{1,49},{49,1},{2,50},{50,2},{3,51},{51,3},{4,52},{52... | collective-permute-start | bytes 737288 | tf_op jit(solution)/shard_map/ppermute | solution.py:194
  48.1 0.7 copy-start.2
  57.3 1.4 %copy-start = (bf16[128,6144]{1,0:T(8,128)(2,1)S(1)}, bf16[128,6144]{1,0:T(8,128)(2,1)}, u32[]{:S(2)}) copy-start(bf16[128,6144]{1,0:T(8,128)(2,1)} %shard_map.47.left) | copy-start | bytes 4718596

commit v9 on v8

--- a/solution.py
+++ b/solution.py
@@ -21,48 +21,58 @@
 PIECE = NB // N_LAYER // N_COL
 DEPTH = INNER * BS
 WIDTH = COLUMNS * BS
+STEPS = (0, 1, 1, 2, 2, 3, 3, 4)
+OTHER = (0, 0, 1, 0, 1, 0, 1, 0)
 GROUP = 4
 
 
-def pack_kernel(right, right_where, left, left_where, out, piece, tail):
+def pack_kernel(right, right_where, out, tail):
     y = lax.axis_index("y")
     core = lax.axis_index("core")
-    col = lax.axis_index("col")
     base = lax.axis_index("layer") * (NB // N_LAYER)
     for p in range(PAIRS):
-        pair = jnp.concatenate([right[p], right[p + PAIRS]], axis=-1)
-        for q in range(N_Y):
-            out[q, p * BS : (p + 1) * BS, :] = pair
+        out[p * BS : (p + 1) * BS, :] = jnp.concatenate([right[p], right[p + PAIRS]], axis=-1)
     tail[...] = jnp.zeros_like(tail)
     inner = right_where[0:1, :] - (base + (y * 2 + core) * INNER)
-    column = right_where[1:2, :] - col * COLUMNS
+    column = right_where[1:2, :] - lax.axis_index("col") * COLUMNS
     tail[0:1, 0:SLOTS] = inner.astype(jnp.float32)
     tail[1:2, 0:SLOTS] = column.astype(jnp.float32)
-    for q in range(N_Y):
-        out[q, BODY:MSG, :] = tail[...].astype(jnp.bfloat16)
+    out[BODY:MSG, :] = tail[...].astype(jnp.bfloat16)
+
+
+def pack(right, right_where):
+    vmem = pl.BlockSpec(memory_space=pltpu.VMEM)
+    return pl.pallas_call(
+        pack_kernel,
+        out_shape=jax.ShapeDtypeStruct((MSG, 128), jnp.bfloat16),
+        in_specs=[vmem] * 2,
+        out_specs=vmem,
+        scratch_shapes=[pltpu.VMEM((16, 128), jnp.float32)],
+        cost_estimate=pl.CostEstimate(flops=0, bytes_accessed=1 << 20, transcendentals=0),
+    )(right, right_where)
+
+
+def spread_kernel(left, left_where, out):
+    base = lax.axis_index("layer") * (NB // N_LAYER) + lax.axis_index("col") * PIECE
     lane = lax.broadcasted_iota(jnp.int32, (16, 128), 1)
     first = jnp.broadcast_to(left_where[0:1, 1:2], (16, 128))
     second = jnp.broadcast_to(left_where[1:2, 1:2], (16, 128))
-    at = jnp.where(lane < BS, first, second) - (base + col * PIECE)
-    at = at.astype(jnp.float32).astype(jnp.bfloat16)
+    at = (jnp.where(lane < BS, first, second) - base).astype(jnp.float32).astype(jnp.bfloat16)
     pair = jnp.concatenate([left[0], left[1]], axis=-1)
-    piece[:BS, :] = pair
-    piece[BS:, :] = at
-
-
-def pack(right, right_where, left, left_where):
+    for c in range(N_COL):
+        out[c, :BS, :] = pair
+        out[c, BS:, :] = at
+
+
+def spread(left, left_where):
     vmem = pl.BlockSpec(memory_space=pltpu.VMEM)
     return pl.pallas_call(
-        pack_kernel,
-        out_shape=(
-            jax.ShapeDtypeStruct((N_Y, MSG, 128), jnp.bfloat16),
-            jax.ShapeDtypeStruct((LMSG, 128), jnp.bfloat16),
-        ),
-        in_specs=[vmem] * 4,
-        out_specs=(vmem, vmem),
-        scratch_shapes=[pltpu.VMEM((16, 128), jnp.float32)],
-        cost_estimate=pl.CostEstimate(flops=0, bytes_accessed=2 << 20, transcendentals=0),
-    )(right, right_where, left, left_where)
+        spread_kernel,
+        out_shape=jax.ShapeDtypeStruct((N_COL, LMSG, 128), jnp.bfloat16),
+        in_specs=[vmem] * 2,
+        out_specs=vmem,
+        cost_estimate=pl.CostEstimate(flops=0, bytes_accessed=1 << 20, transcendentals=0),
+    )(left, left_where)
 
 
 def half_swap():
@@ -102,17 +112,21 @@
     lax.fori_loop(0, PAIRS, place, 0, unroll=2)
 
 
-def left_kernel(left_own, left_other, left):
+def place_kernel(left_own, left_other, *refs):
+    blocks, (out, left, total, where, places, sem), scratch = refs[:N_Y], refs[N_Y : N_Y + 6], refs[N_Y + 6 :]
+    panels, swapped = scratch[:GROUP], scratch[GROUP:]
+    y = lax.axis_index("y")
     core = lax.axis_index("core")
+    copy = read_places(blocks, where, places, sem)
     swap = half_swap()
+
     lane = lax.broadcasted_iota(jnp.int32, (BS, 128), 1)
     upper = (lane >= BS).astype(jnp.float32)
     for src, at in ((left_own, core), (left_other, 1 - core)):
         rows = pl.ds(pl.multiple_of(at * BS, BS), BS)
         for c in range(N_COL):
-            whole = src[c]
-            there = jnp.dot(whole, swap, preferred_element_type=jnp.float32)
-            here = whole.astype(jnp.float32)
+            there = jnp.dot(src[c], swap, preferred_element_type=jnp.float32)
+            here = src[c].astype(jnp.float32)
             for g in range(PIECE // 2):
                 want = upper + 2.0 * g
                 value = jnp.where(here[BS : BS + 1] == want, here[:BS], 0.0)
@@ -120,24 +134,6 @@
                 at_lane = (c * PIECE + 2 * g) * BS
                 left[rows, at_lane : at_lane + 128] = value.astype(jnp.bfloat16)
 
-
-def left_panel(left_own, left_other):
-    vmem = pl.BlockSpec(memory_space=pltpu.VMEM)
-    return pl.pallas_call(
-        left_kernel,
-        out_shape=jax.ShapeDtypeStruct((2 * BS, NB // N_LAYER * BS), jnp.bfloat16),
-        in_specs=[vmem] * 2,
-        out_specs=vmem,
-        cost_estimate=pl.CostEstimate(flops=0, bytes_accessed=2 << 20, transcendentals=0),
-    )(left_own, left_other)
-
-
-def place_kernel(own, left, out, total, where, places, sem, *scratch):
-    panels, swapped = scratch[:GROUP], scratch[GROUP:]
-    core = lax.axis_index("core")
-    blocks = [own.at[j] for j in range(N_Y)]
-    copy = read_places(blocks, where, places, sem)
-    swap = half_swap()
     for j0 in range(0, N_Y, GROUP):
         now = blocks[j0 : j0 + GROUP]
         for i, block in enumerate(now):
@@ -149,7 +145,10 @@
             copy.wait()
         place_slots(now, j0, panels, swapped, places)
         for i in range(len(now)):
-            at = pl.ds(pl.multiple_of((2 * (j0 + i) + core) * DEPTH, 128), DEPTH)
+            steps = STEPS[j0 + i]
+            chip = lax.rem(y + N_Y + jnp.where(core == 0, -steps, steps), N_Y)
+            owner = chip * 2 + (1 - core if OTHER[j0 + i] else core)
+            at = pl.ds(pl.multiple_of(owner * DEPTH, 128), DEPTH)
             part = jnp.dot(left[:, at], panels[i][...], preferred_element_type=jnp.float32)
             total[...] = part if j0 + i == 0 else total[...] + part
     share = WIDTH // N_LAYER
@@ -160,14 +159,15 @@
             )
 
 
-def multiply(own, left):
+def multiply(*operands):
     vmem = pl.BlockSpec(memory_space=pltpu.VMEM)
     return pl.pallas_call(
         place_kernel,
         out_shape=jax.ShapeDtypeStruct((2 * N_LAYER, BS, WIDTH // N_LAYER), jnp.bfloat16),
-        in_specs=[vmem] * 2,
+        in_specs=[vmem] * len(operands),
         out_specs=vmem,
         scratch_shapes=[
+            pltpu.VMEM((2 * BS, NB // N_LAYER * BS), jnp.bfloat16),
             pltpu.VMEM((2 * BS, WIDTH), jnp.float32),
             pltpu.VMEM((16, 128), jnp.int32),
             pltpu.SMEM((16, 128), jnp.int32),
@@ -179,20 +179,25 @@
         cost_estimate=pl.CostEstimate(
             flops=2 * 128 * 3072 * 2048, bytes_accessed=4 << 20, transcendentals=0
         ),
-    )(own, left)
+    )(*operands)
 
 
 def shards(left_blocks, left_coords, right_blocks, right_coords):
-    mine, piece = pack(
-        right_blocks.reshape(SLOTS, BS, BS),
-        right_coords.reshape(SLOTS, 2).T,
-        left_blocks.reshape(2, BS, BS),
-        left_coords.reshape(2, 2),
-    )
-    own = lax.all_to_all(mine, "y", 0, 0)
-    pieces = lax.all_gather(piece, "col")
-    pieces_other = lax.ppermute(pieces, "core", [(0, 1), (1, 0)])
-    part = multiply(own, left_panel(pieces, pieces_other))
+    mine = pack(right_blocks.reshape(SLOTS, BS, BS), right_coords.reshape(SLOTS, 2).T)
+    ring = [(2 * i + c, 2 * ((i + 1 - 2 * c) % N_Y) + c) for i in range(N_Y) for c in (0, 1)]
+    cross = [(0, 1), (1, 0)]
+    axes = ("y", "core")
+    a = lax.ppermute(mine, axes, ring)
+    b = lax.ppermute(mine, "core", cross)
+    left = spread(left_blocks.reshape(2, BS, BS), left_coords.reshape(2, 2))
+    pieces = lax.all_to_all(left, "col", 0, 0)
+    blocks = [mine, a]
+    for _ in range(3):
+        b = lax.ppermute(b, axes, ring)
+        a = lax.ppermute(a, axes, ring)
+        blocks += [b, a]
+    pieces_other = lax.ppermute(pieces, "core", cross)
+    part = multiply(pieces, pieces_other, *blocks)
     parts = lax.all_to_all(part, ("core", "layer"), 0, 0)
     total = jnp.sum(parts.astype(jnp.float32), axis=0)
     return total.reshape(1, BS, COLUMNS // N_LAYER, BS)

time: 85.8 us -> 79.6 us (0.928)
  blocking collectives: 49.2 us -> 17.1 us
  starting transfers between devices: 14.6 us -> 46.7 us
  waiting for transfers between devices: 6.55 us -> 3.71 us
  local copies, waits for them, and re-layouts: 2.9 us -> 0.81 us
  Pallas kernels: 12.1 us -> 10.5 us
    ppermute x1 -> x9, starting transfers between devices: 6.8 us -> 37.6 us  [the longest x1 12.4 us: shards(): b = lax.ppermute(mine, 'core', cross)]
    all_gather x1 -> x0, blocking collectives: 29.6 us -> none  [shards(): pieces = lax.all_gather(piece, 'col')]
    all_to_all x1, waiting for transfers between devices: 5.44 us -> 0.01 us  [shards(): pieces = lax.all_to_all(left, 'col', 0, 0)]
    ppermute x1 -> x9, waiting for transfers between devices: 1.12 us -> 3.71 us  [the longest x3 1.74 us: shards(): b = lax.ppermute(b, axes, ring)]
    all_to_all x1, blocking collectives: 19.6 us -> 17.1 us  [shards(): parts = lax.all_to_all(part, ('core', 'layer'), 0, 0)]
    pallas_call x2, Pallas kernels: 5.81 us -> 3.44 us  [the longest x1 1.88 us: pack(): pl.pallas_call(pack_kernel, out_shape=jax.ShapeDtypeStruct((MSG, 128), jn...]
    unnamed x8 -> x2, local copies, waits for them, and re-layouts: 2.1 us -> 0.01 us
    all_to_all x1, starting transfers between devices: 7.78 us -> 9.17 us  [shards(): pieces = lax.all_to_all(left, 'col', 0, 0)]
  transfers between devices with their start and end apart: 2 -> 10, of which waited for: 2 -> 4; matrix products, arithmetic and copies ran while one was open for 0% -> 0% of each run, Pallas kernels for 4% -> 2%
where the time goes in v9:
time: 79.6 us; the launch traced here: 79.1 us
  starting transfers between devices  46.7 us (59%)
  blocking collectives  17.1 us (21%)
  Pallas kernels  10.5 us (13%)
  waiting for transfers between devices  3.71 us (5%)
  local copies, waits for them, and re-layouts  0.81 us (1%)
    all_to_all x1, blocking collectives, shards(): parts = lax.all_to_all(part, ('core', 'layer'), 0, 0)  17.1 us
    ppermute x1, starting transfers between devices, shards(): b = lax.ppermute(mine, 'core', cross)  12.4 us
    ppermute x3, starting transfers between devices, shards(): b = lax.ppermute(b, axes, ring)  11.9 us
    ppermute x3, starting transfers between devices, shards(): a = lax.ppermute(a, axes, ring)  9.24 us
    all_to_all x1, starting transfers between devices, shards(): pieces = lax.all_to_all(left, 'col', 0, 0)  9.17 us
    pallas_call x1, Pallas kernels, multiply(): pl.pallas_call(place_kernel, out_shape=jax.ShapeDtypeStruct((2 * N_LAYER,...  7.04 us
    ppermute x1, starting transfers between devices, shards(): pieces_other = lax.ppermute(pieces, 'core', cross)  2.04 us
    ppermute x1, starting transfers between devices, shards(): a = lax.ppermute(mine, axes, ring)  1.92 us
  transfers between devices with their start and end apart: 10, of which 4 were waited for; matrix products, arithmetic and copies ran while one was open for 0% of the time, Pallas kernels for 2%

profile of v9, /device:TPU:1, one launch (start us, length us, event | category | flops | bytes accessed | tf_op | source)
XLA Modules:
  0.0 79.1 jit_solution(10531021950960329114)
XLA Ops:
  0.0 1.9 %shard_map.47.refs_0_ = bf16[1040,128]{1,0:T(8,128)(2,1)} custom-call(bf16[32,64,64]{2,1,0:T(8,128)(2,1)} %bitcast.6, s32[2,32]{1,0:T(2,128)} %bitcast.8), custom_call_target="tpu_custom_call" | custom-call | bytes 1048576 | tf_op jit(solution)/shard_map/pallas_call | solution.py:45
  1.9 12.4 %collective-permute-start.2 = (bf16[1040,128]{1,0:T(8,128)(2,1)}, bf16[1040,128]{1,0:T(8,128)(2,1)S(1)}, u32[]{:S(2)}, u32[]{:S(2)}) collective-permute-start(bf16[1040,128]{1,0:T(8,128)(2,1)} %shard_map.47.refs_0_), channel_id=1, source_target_pairs={{0,48},{48,0},{1,49},{49,1},{2,50},{50,2},{3,51},{51,3},{4,52},{52... | collective-permute-start | bytes 798728 | tf_op jit(solution)/shard_map/ppermute | solution.py:191
  14.3 1.9 %collective-permute-start.1 = (bf16[1040,128]{1,0:T(8,128)(2,1)}, bf16[1040,128]{1,0:T(8,128)(2,1)S(1)}, u32[]{:S(2)}, u32[]{:S(2)}) collective-permute-start(bf16[1040,128]{1,0:T(8,128)(2,1)} %shard_map.47.refs_0_), channel_id=1, source_target_pairs={{0,96},{48,720},{96,192},{144,48},{192,288},{240,144},{288,384},{3... | collective-permute-start | bytes 798728 | tf_op jit(solution)/shard_map/ppermute | solution.py:190
  16.2 1.6 %shard_map.46 = bf16[12,80,128]{2,1,0:T(8,128)(2,1)} custom-call(bf16[2,64,64]{2,1,0:T(8,128)(2,1)} %bitcast.7, s32[2,2]{1,0:T(2,128)} %bitcast.9), custom_call_target="tpu_custom_call" | custom-call | bytes 1048576 | tf_op jit(solution)/shard_map/pallas_call | solution.py:69
  17.8 0.0 copy-start
  17.8 9.2 %all-to-all-start = ((bf16[12,80,128]{2,1,0:T(8,128)(2,1)}), bf16[12,80,128]{2,1,0:T(8,128)(2,1)S(1)}, u32[]{:S(2)}, u32[]{:S(2)}) async-start(bf16[12,80,128]{2,1,0:T(8,128)(2,1)} %shard_map.46), calls=%async_computation | async-start | bytes 491520 | tf_op jit(solution)/shard_map/all_to_all | solution.py:193
  27.0 0.0 collective-permute-done.2
  27.0 3.0 %collective-permute-start.3 = (bf16[1040,128]{1,0:T(8,128)(2,1)S(1)}, bf16[1040,128]{1,0:T(8,128)(2,1)S(1)}, u32[]{:S(2)}, u32[]{:S(2)}) collective-permute-start(bf16[1040,128]{1,0:T(8,128)(2,1)S(1)} %collective-permute-done.2), channel_id=1, source_target_pairs={{0,96},{48,720},{96,192},{144,48},{192,288},{240,144},{288,384},{3... | collective-permute-start | bytes 798728 | tf_op jit(solution)/shard_map/ppermute | solution.py:196
  30.0 0.0 collective-permute-done.1.refs_1_
  30.0 3.0 %collective-permute-start.4 = (bf16[1040,128]{1,0:T(8,128)(2,1)S(1)}, bf16[1040,128]{1,0:T(8,128)(2,1)S(1)}, u32[]{:S(2)}, u32[]{:S(2)}) collective-permute-start(bf16[1040,128]{1,0:T(8,128)(2,1)S(1)} %collective-permute-done.1.refs_1_), channel_id=1, source_target_pairs={{0,96},{48,720},{96,192},{144,48},{192,288},{240,144},{288,384},{3... | collective-permute-start | bytes 798728 | tf_op jit(solution)/shard_map/ppermute | solution.py:197
  33.0 1.5 %collective-permute-done.3.refs_2_ = bf16[1040,128]{1,0:T(8,128)(2,1)S(1)} collective-permute-done((bf16[1040,128]{1,0:T(8,128)(2,1)S(1)}, bf16[1040,128]{1,0:T(8,128)(2,1)S(1)}, u32[]{:S(2)}, u32[]{:S(2)}) %collective-permute-start.3) | collective-permute-done | bytes 266272 | tf_op jit(solution)/shard_map/ppermute | solution.py:196
  34.4 4.0 %collective-permute-start.5 = (bf16[1040,128]{1,0:T(8,128)(2,1)S(1)}, bf16[1040,128]{1,0:T(8,128)(2,1)S(1)}, u32[]{:S(2)}, u32[]{:S(2)}) collective-permute-start(bf16[1040,128]{1,0:T(8,128)(2,1)S(1)} %collective-permute-done.3.refs_2_), channel_id=1, source_target_pairs={{0,96},{48,720},{96,192},{144,48},{192,288},{240,144},{288,384},{3... | collective-permute-start | bytes 798728 | tf_op jit(solution)/shard_map/ppermute | solution.py:196
  38.5 0.0 collective-permute-done.4.refs_3_
  38.5 3.1 %collective-permute-start.6 = (bf16[1040,128]{1,0:T(8,128)(2,1)S(1)}, bf16[1040,128]{1,0:T(8,128)(2,1)S(1)}, u32[]{:S(2)}, u32[]{:S(2)}) collective-permute-start(bf16[1040,128]{1,0:T(8,128)(2,1)S(1)} %collective-permute-done.4.refs_3_), channel_id=1, source_target_pairs={{0,96},{48,720},{96,192},{144,48},{192,288},{240,144},{288,384},{3... | collective-permute-start | bytes 798728 | tf_op jit(solution)/shard_map/ppermute | solution.py:197
  41.6 0.3 collective-permute-done.5.refs_4_
  41.9 4.9 %collective-permute-start.7 = (bf16[1040,128]{1,0:T(8,128)(2,1)S(1)}, bf16[1040,128]{1,0:T(8,128)(2,1)S(1)}, u32[]{:S(2)}, u32[]{:S(2)}) collective-permute-start(bf16[1040,128]{1,0:T(8,128)(2,1)S(1)} %collective-permute-done.5.refs_4_), channel_id=1, source_target_pairs={{0,96},{48,720},{96,192},{144,48},{192,288},{240,144},{288,384},{3... | collective-permute-start | bytes 798728 | tf_op jit(solution)/shard_map/ppermute | solution.py:196
  46.8 0.0 collective-permute-done.6.refs_5_
  46.8 3.1 %collective-permute-start.8 = (bf16[1040,128]{1,0:T(8,128)(2,1)S(1)}, bf16[1040,128]{1,0:T(8,128)(2,1)S(1)}, u32[]{:S(2)}, u32[]{:S(2)}) collective-permute-start(bf16[1040,128]{1,0:T(8,128)(2,1)S(1)} %collective-permute-done.6.refs_5_), channel_id=1, source_target_pairs={{0,96},{48,720},{96,192},{144,48},{192,288},{240,144},{288,384},{3... | collective-permute-start | bytes 798728 | tf_op jit(solution)/shard_map/ppermute | solution.py:197
  50.0 0.0 all-to-all-done.left_own
  50.0 2.0 %collective-permute-start = (bf16[12,80,128]{2,1,0:T(8,128)(2,1)S(1)}, bf16[12,80,128]{2,1,0:T(8,128)(2,1)S(1)}, u32[]{:S(2)}, u32[]{:S(2)}) collective-permute-start(bf16[12,80,128]{2,1,0:T(8,128)(2,1)S(1)} %all-to-all-done.left_own), channel_id=1, source_target_pairs={{0,48},{48,0},{1,49},{49,1},{2,50},{50,2},{3,51},{51,3},{4,52},{52... | collective-permute-start | bytes 737288 | tf_op jit(solution)/shard_map/ppermute | solution.py:199
  52.0 1.4 %collective-permute-done.left_other = bf16[12,80,128]{2,1,0:T(8,128)(2,1)S(1)} collective-permute-done((bf16[12,80,128]{2,1,0:T(8,128)(2,1)S(1)}, bf16[12,80,128]{2,1,0:T(8,128)(2,1)S(1)}, u32[]{:S(2)}, u32[]{:S(2)}) %collective-permute-start) | collective-permute-done | bytes 245792 | tf_op jit(solution)/shard_map/ppermute | solution.py:199
  53.4 0.0 collective-permute-done.7.refs_6_
  53.4 0.6 collective-permute-done.8.refs_7_
  54.0 0.0 copy-done
  54.0 7.0 %shard_map.48 = bf16[8,64,512]{2,1,0:T(8,128)(2,1)S(1)} custom-call(bf16[12,80,128]{2,1,0:T(8,128)(2,1)S(1)} %all-to-all-done.left_own, bf16[12,80,128]{2,1,0:T(8,128)(2,1)S(1)} %collective-permute-done.left_other, bf16[1040,128]{1,0:T(8,128)(2,1)S(1)} %copy-done, bf16[1040,128]{1,0:T(8,128)(2,1)S(1)} %collective-permute-done.1.refs_1_, ...), custom_call_target="tpu_custom_call" | custom-call | flops 1610612736 | bytes 4194304 | tf_op jit(solution)/shard_map/pallas_call | solution.py:164
  61.1 17.1 %all_to_all.10 = bf16[8,64,512]{2,1,0:T(8,128)(2,1)S(1)} all-to-all(bf16[8,64,512]{2,1,0:T(8,128)(2,1)S(1)} %shard_map.48), channel_id=1, replica_groups=mesh['y'=8,'core'=2,'col'=12,'layer'=4] {'core','layer'}, dimensions={0} | all-to-all | bytes 1048576 | tf_op jit(solution)/shard_map/all_to_all | solution.py:201
  78.2 0.1 convert_reduce_fusion
  78.3 0.8 %reshape.19 = f32[1,64,8,64]{3,2,1,0:T(8,128)} reshape(f32[64,512]{1,0:T(8,128)S(1)} %convert_reduce_fusion) | data formatting | bytes 262144 | tf_op jit(solution)/shard_map/reshape | solution.py:203
Async XLA Ops:
  1.9 25.1 %collective-permute-start.2 = (bf16[1040,128]{1,0:T(8,128)(2,1)}, bf16[1040,128]{1,0:T(8,128)(2,1)S(1)}, u32[]{:S(2)}, u32[]{:S(2)}) collective-permute-start(bf16[1040,128]{1,0:T(8,128)(2,1)} %shard_map.47.refs_0_), channel_id=1, source_target_pairs={{0,48},{48,0},{1,49},{49,1},{2,50},{50,2},{3,51},{51,3},{4,52},{52... | collective-permute-start | bytes 798728 | tf_op jit(solution)/shard_map/ppermute | solution.py:191
  14.3 15.7 %collective-permute-start.1 = (bf16[1040,128]{1,0:T(8,128)(2,1)}, bf16[1040,128]{1,0:T(8,128)(2,1)S(1)}, u32[]{:S(2)}, u32[]{:S(2)}) collective-permute-start(bf16[1040,128]{1,0:T(8,128)(2,1)} %shard_map.47.refs_0_), channel_id=1, source_target_pairs={{0,96},{48,720},{96,192},{144,48},{192,288},{240,144},{288,384},{3... | collective-permute-start | bytes 798728 | tf_op jit(solution)/shard_map/ppermute | solution.py:190
  17.8 36.2 %copy-start = (bf16[1040,128]{1,0:T(8,128)(2,1)S(1)}, bf16[1040,128]{1,0:T(8,128)(2,1)}, u32[]{:S(2)}) copy-start(bf16[1040,128]{1,0:T(8,128)(2,1)} %shard_map.47.refs_0_) | copy-start | bytes 798724
  17.8 32.2 %all-to-all-start = ((bf16[12,80,128]{2,1,0:T(8,128)(2,1)}), bf16[12,80,128]{2,1,0:T(8,128)(2,1)S(1)}, u32[]{:S(2)}, u32[]{:S(2)}) async-start(bf16[12,80,128]{2,1,0:T(8,128)(2,1)} %shard_map.46), calls=%async_computation | async-start | bytes 491520 | tf_op jit(solution)/shard_map/all_to_all | solution.py:193
  27.0 7.5 %collective-permute-start.3 = (bf16[1040,128]{1,0:T(8,128)(2,1)S(1)}, bf16[1040,128]{1,0:T(8,128)(2,1)S(1)}, u32[]{:S(2)}, u32[]{:S(2)}) collective-permute-start(bf16[1040,128]{1,0:T(8,128)(2,1)S(1)} %collective-permute-done.2), channel_id=1, source_target_pairs={{0,96},{48,720},{96,192},{144,48},{192,288},{240,144},{288,384},{3... | collective-permute-start | bytes 798728 | tf_op jit(solution)/shard_map/ppermute | solution.py:196
  30.0 8.5 %collective-permute-start.4 = (bf16[1040,128]{1,0:T(8,128)(2,1)S(1)}, bf16[1040,128]{1,0:T(8,128)(2,1)S(1)}, u32[]{:S(2)}, u32[]{:S(2)}) collective-permute-start(bf16[1040,128]{1,0:T(8,128)(2,1)S(1)} %collective-permute-done.1.refs_1_), channel_id=1, source_target_pairs={{0,96},{48,720},{96,192},{144,48},{192,288},{240,144},{288,384},{3... | collective-permute-start | bytes 798728 | tf_op jit(solution)/shard_map/ppermute | solution.py:197
  34.4 7.4 %collective-permute-start.5 = (bf16[1040,128]{1,0:T(8,128)(2,1)S(1)}, bf16[1040,128]{1,0:T(8,128)(2,1)S(1)}, u32[]{:S(2)}, u32[]{:S(2)}) collective-permute-start(bf16[1040,128]{1,0:T(8,128)(2,1)S(1)} %collective-permute-done.3.refs_2_), channel_id=1, source_target_pairs={{0,96},{48,720},{96,192},{144,48},{192,288},{240,144},{288,384},{3... | collective-permute-start | bytes 798728 | tf_op jit(solution)/shard_map/ppermute | solution.py:196
  38.5 8.4 %collective-permute-start.6 = (bf16[1040,128]{1,0:T(8,128)(2,1)S(1)}, bf16[1040,128]{1,0:T(8,128)(2,1)S(1)}, u32[]{:S(2)}, u32[]{:S(2)}) collective-permute-start(bf16[1040,128]{1,0:T(8,128)(2,1)S(1)} %collective-permute-done.4.refs_3_), channel_id=1, source_target_pairs={{0,96},{48,720},{96,192},{144,48},{192,288},{240,144},{288,384},{3... | collective-permute-start | bytes 798728 | tf_op jit(solution)/shard_map/ppermute | solution.py:197
  41.9 11.5 %collective-permute-start.7 = (bf16[1040,128]{1,0:T(8,128)(2,1)S(1)}, bf16[1040,128]{1,0:T(8,128)(2,1)S(1)}, u32[]{:S(2)}, u32[]{:S(2)}) collective-permute-start(bf16[1040,128]{1,0:T(8,128)(2,1)S(1)} %collective-permute-done.5.refs_4_), channel_id=1, source_target_pairs={{0,96},{48,720},{96,192},{144,48},{192,288},{240,144},{288,384},{3... | collective-permute-start | bytes 798728 | tf_op jit(solution)/shard_map/ppermute | solution.py:196
  46.8 7.2 %collective-permute-start.8 = (bf16[1040,128]{1,0:T(8,128)(2,1)S(1)}, bf16[1040,128]{1,0:T(8,128)(2,1)S(1)}, u32[]{:S(2)}, u32[]{:S(2)}) collective-permute-start(bf16[1040,128]{1,0:T(8,128)(2,1)S(1)} %collective-permute-done.6.refs_5_), channel_id=1, source_target_pairs={{0,96},{48,720},{96,192},{144,48},{192,288},{240,144},{288,384},{3... | collective-permute-start | bytes 798728 | tf_op jit(solution)/shard_map/ppermute | solution.py:197
  50.0 3.4 %collective-permute-start = (bf16[12,80,128]{2,1,0:T(8,128)(2,1)S(1)}, bf16[12,80,128]{2,1,0:T(8,128)(2,1)S(1)}, u32[]{:S(2)}, u32[]{:S(2)}) collective-permute-start(bf16[12,80,128]{2,1,0:T(8,128)(2,1)S(1)} %all-to-all-done.left_own), channel_id=1, source_target_pairs={{0,48},{48,0},{1,49},{49,1},{2,50},{50,2},{3,51},{51,3},{4,52},{52... | collective-permute-start | bytes 737288 | tf_op jit(solution)/shard_map/ppermute | solution.py:199

commit v10 on v9

--- a/solution.py
+++ b/solution.py
@@ -21,8 +21,7 @@
 PIECE = NB // N_LAYER // N_COL
 DEPTH = INNER * BS
 WIDTH = COLUMNS * BS
-STEPS = (0, 1, 1, 2, 2, 3, 3, 4)
-OTHER = (0, 0, 1, 0, 1, 0, 1, 0)
+STEPS = (0, -1, 1, -2, 2, -3, 3, 4)
 GROUP = 4
 
 
@@ -145,10 +144,8 @@
             copy.wait()
         place_slots(now, j0, panels, swapped, places)
         for i in range(len(now)):
-            steps = STEPS[j0 + i]
-            chip = lax.rem(y + N_Y + jnp.where(core == 0, -steps, steps), N_Y)
-            owner = chip * 2 + (1 - core if OTHER[j0 + i] else core)
-            at = pl.ds(pl.multiple_of(owner * DEPTH, 128), DEPTH)
+            chip = lax.rem(y + N_Y + STEPS[j0 + i], N_Y)
+            at = pl.ds(pl.multiple_of((2 * chip + core) * DEPTH, 128), DEPTH)
             part = jnp.dot(left[:, at], panels[i][...], preferred_element_type=jnp.float32)
             total[...] = part if j0 + i == 0 else total[...] + part
     share = WIDTH // N_LAYER
@@ -184,18 +181,16 @@
 
 def shards(left_blocks, left_coords, right_blocks, right_coords):
     mine = pack(right_blocks.reshape(SLOTS, BS, BS), right_coords.reshape(SLOTS, 2).T)
-    ring = [(2 * i + c, 2 * ((i + 1 - 2 * c) % N_Y) + c) for i in range(N_Y) for c in (0, 1)]
     cross = [(0, 1), (1, 0)]
-    axes = ("y", "core")
-    a = lax.ppermute(mine, axes, ring)
-    b = lax.ppermute(mine, "core", cross)
+    away = {d: [(i, (i + d) % N_Y) for i in range(N_Y)] for d in (-2, -1, 1, 2)}
+    far = [(2 * i + c, 2 * ((i + 2 - 4 * c) % N_Y) + c) for i in range(N_Y) for c in (0, 1)]
+    one = [lax.ppermute(mine, "y", away[d]) for d in (1, -1)]
+    two = [lax.ppermute(mine, "y", away[d]) for d in (2, -2)]
     left = spread(left_blocks.reshape(2, BS, BS), left_coords.reshape(2, 2))
     pieces = lax.all_to_all(left, "col", 0, 0)
-    blocks = [mine, a]
-    for _ in range(3):
-        b = lax.ppermute(b, axes, ring)
-        a = lax.ppermute(a, axes, ring)
-        blocks += [b, a]
+    three = [lax.ppermute(two[0], "y", away[1]), lax.ppermute(two[1], "y", away[-1])]
+    four = lax.ppermute(jnp.where(lax.axis_index("core") == 0, *two), ("y", "core"), far)
+    blocks = [mine, *one, *two, *three, four]
     pieces_other = lax.ppermute(pieces, "core", cross)
     part = multiply(pieces, pieces_other, *blocks)
     parts = lax.all_to_all(part, ("core", "layer"), 0, 0)

time: 79.6 us -> 78.9 us (level)
  starting transfers between devices: 46.7 us -> 43.6 us
  waiting for transfers between devices: 3.71 us -> 6.35 us
    ppermute x8 -> x7, starting transfers between devices: 35.5 us -> 24.8 us  [the longest x2 8.62 us: shards(): two = [lax.ppermute(mine, 'y', away[d]) for d in (2, -2)]]
    all_to_all x1, starting transfers between devices: 9.17 us -> 15 us  [shards(): pieces = lax.all_to_all(left, 'col', 0, 0)]
    ppermute x8 -> x7, waiting for transfers between devices: 2.35 us -> 6.35 us  [the longest x1 3.34 us: shards(): lax.ppermute(two[0], 'y', away[1])]
    ppermute x1, starting transfers between devices: 2.04 us -> 3.78 us  [shards(): pieces_other = lax.ppermute(pieces, 'core', cross)]
    ppermute x1, waiting for transfers between devices: 1.35 us -> 0.01 us  [shards(): pieces_other = lax.ppermute(pieces, 'core', cross)]
  transfers between devices with their start and end apart: 10 -> 9, of which waited for: 4 -> 2; matrix products, arithmetic and copies ran while one was open for 0% -> 0% of each run, Pallas kernels for 2% -> 2%
where the time goes in v10:
time: 78.9 us; the launch traced here: 78.4 us
  starting transfers between devices  43.6 us (55%)
  blocking collectives  16.9 us (21%)
  Pallas kernels  10.4 us (13%)
  waiting for transfers between devices  6.35 us (8%)
  local copies, waits for them, and re-layouts  0.81 us (1%)
    all_to_all x1, blocking collectives, shards(): parts = lax.all_to_all(part, ('core', 'layer'), 0, 0)  16.9 us
    all_to_all x1, starting transfers between devices, shards(): pieces = lax.all_to_all(left, 'col', 0, 0)  15 us
    ppermute x2, starting transfers between devices, shards(): two = [lax.ppermute(mine, 'y', away[d]) for d in (2, -2)]  8.62 us
    pallas_call x1, Pallas kernels, multiply(): pl.pallas_call(place_kernel, out_shape=jax.ShapeDtypeStruct((2 * N_LAYER,...  7 us
    ppermute x2, starting transfers between devices, shards(): one = [lax.ppermute(mine, 'y', away[d]) for d in (1, -1)]  6.61 us
    ppermute x1, starting transfers between devices, shards(): lax.ppermute(two[1], 'y', away[-1])  4.57 us
    ppermute x1, starting transfers between devices, shards(): pieces_other = lax.ppermute(pieces, 'core', cross)  3.78 us
    ppermute x1, waiting for transfers between devices, shards(): lax.ppermute(two[0], 'y', away[1])  3.34 us
  transfers between devices with their start and end apart: 9, of which 2 were waited for; matrix products, arithmetic and copies ran while one was open for 0% of the time, Pallas kernels for 2%

profile of v10, /device:TPU:1, one launch (start us, length us, event | category | flops | bytes accessed | tf_op | source)
XLA Modules:
  0.0 78.4 jit_solution(11189998478632044194)
XLA Ops:
  0.0 1.9 %shard_map.47.refs_0_ = bf16[1040,128]{1,0:T(8,128)(2,1)} custom-call(bf16[32,64,64]{2,1,0:T(8,128)(2,1)} %bitcast.6, s32[2,32]{1,0:T(2,128)} %bitcast.8), custom_call_target="tpu_custom_call" | custom-call | bytes 1048576 | tf_op jit(solution)/shard_map/pallas_call | solution.py:44
  1.9 6.7 %collective-permute-start.4 = (bf16[1040,128]{1,0:T(8,128)(2,1)}, bf16[1040,128]{1,0:T(8,128)(2,1)S(1)}, u32[]{:S(2)}, u32[]{:S(2)}) collective-permute-start(bf16[1040,128]{1,0:T(8,128)(2,1)} %shard_map.47.refs_0_), channel_id=1, source_target_pairs={{0,576},{96,672},{192,0},{288,96},{384,192},{480,288},{576,384},{6... | collective-permute-start | bytes 798728 | tf_op jit(solution)/shard_map/ppermute | solution.py:188
  8.6 1.9 %collective-permute-start.3 = (bf16[1040,128]{1,0:T(8,128)(2,1)}, bf16[1040,128]{1,0:T(8,128)(2,1)S(1)}, u32[]{:S(2)}, u32[]{:S(2)}) collective-permute-start(bf16[1040,128]{1,0:T(8,128)(2,1)} %shard_map.47.refs_0_), channel_id=1, source_target_pairs={{0,192},{96,288},{192,384},{288,480},{384,576},{480,672},{576,0},{... | collective-permute-start | bytes 798728 | tf_op jit(solution)/shard_map/ppermute | solution.py:188
  10.5 1.6 %shard_map.46 = bf16[12,80,128]{2,1,0:T(8,128)(2,1)} custom-call(bf16[2,64,64]{2,1,0:T(8,128)(2,1)} %bitcast.7, s32[2,2]{1,0:T(2,128)} %bitcast.9), custom_call_target="tpu_custom_call" | custom-call | bytes 1048576 | tf_op jit(solution)/shard_map/pallas_call | solution.py:68
  12.1 0.0 copy-start
  12.1 15.0 %all-to-all-start = ((bf16[12,80,128]{2,1,0:T(8,128)(2,1)}), bf16[12,80,128]{2,1,0:T(8,128)(2,1)S(1)}, u32[]{:S(2)}, u32[]{:S(2)}) async-start(bf16[12,80,128]{2,1,0:T(8,128)(2,1)} %shard_map.46), calls=%async_computation | async-start | bytes 491520 | tf_op jit(solution)/shard_map/all_to_all | solution.py:190
  27.1 0.0 copy-done
  27.1 4.7 %collective-permute-start.2 = (bf16[1040,128]{1,0:T(8,128)(2,1)S(1)}, bf16[1040,128]{1,0:T(8,128)(2,1)S(1)}, u32[]{:S(2)}, u32[]{:S(2)}) collective-permute-start(bf16[1040,128]{1,0:T(8,128)(2,1)S(1)} %copy-done), channel_id=1, source_target_pairs={{0,672},{96,0},{192,96},{288,192},{384,288},{480,384},{576,480},{6... | collective-permute-start | bytes 798728 | tf_op jit(solution)/shard_map/ppermute | solution.py:187
  31.8 1.9 %collective-permute-start.1 = (bf16[1040,128]{1,0:T(8,128)(2,1)S(1)}, bf16[1040,128]{1,0:T(8,128)(2,1)S(1)}, u32[]{:S(2)}, u32[]{:S(2)}) collective-permute-start(bf16[1040,128]{1,0:T(8,128)(2,1)S(1)} %copy-done), channel_id=1, source_target_pairs={{0,96},{96,192},{192,288},{288,384},{384,480},{480,576},{576,672},... | collective-permute-start | bytes 798728 | tf_op jit(solution)/shard_map/ppermute | solution.py:187
  33.7 0.0 collective-permute-done.4.refs_4_
  33.7 4.6 %collective-permute-start.6 = (bf16[1040,128]{1,0:T(8,128)(2,1)S(1)}, bf16[1040,128]{1,0:T(8,128)(2,1)S(1)}, u32[]{:S(2)}, u32[]{:S(2)}) collective-permute-start(bf16[1040,128]{1,0:T(8,128)(2,1)S(1)} %collective-permute-done.4.refs_4_), channel_id=1, source_target_pairs={{0,672},{96,0},{192,96},{288,192},{384,288},{480,384},{576,480},{6... | collective-permute-start | bytes 798728 | tf_op jit(solution)/shard_map/ppermute | solution.py:191
  38.3 0.0 collective-permute-done.3.refs_3_
  38.4 1.9 %collective-permute-start.7 = (bf16[1040,128]{1,0:T(8,128)(2,1)S(1)}, bf16[1040,128]{1,0:T(8,128)(2,1)S(1)}, u32[]{:S(2)}, u32[]{:S(2)}) collective-permute-start(bf16[1040,128]{1,0:T(8,128)(2,1)S(1)} %broadcast_select_fusion), channel_id=1, source_target_pairs={{0,192},{48,624},{96,288},{144,720},{192,384},{240,48},{288,480},{... | collective-permute-start | bytes 798728 | tf_op jit(solution)/shard_map/ppermute | solution.py:192
  40.3 3.1 %collective-permute-start.5 = (bf16[1040,128]{1,0:T(8,128)(2,1)S(1)}, bf16[1040,128]{1,0:T(8,128)(2,1)S(1)}, u32[]{:S(2)}, u32[]{:S(2)}) collective-permute-start(bf16[1040,128]{1,0:T(8,128)(2,1)S(1)} %collective-permute-done.3.refs_3_), channel_id=1, source_target_pairs={{0,96},{96,192},{192,288},{288,384},{384,480},{480,576},{576,672},... | collective-permute-start | bytes 798728 | tf_op jit(solution)/shard_map/ppermute | solution.py:191
  43.4 0.0 collective-permute-done.2.refs_2_
  43.4 0.0 all-to-all-done.left_own
  43.4 3.8 %collective-permute-start = (bf16[12,80,128]{2,1,0:T(8,128)(2,1)S(1)}, bf16[12,80,128]{2,1,0:T(8,128)(2,1)S(1)}, u32[]{:S(2)}, u32[]{:S(2)}) collective-permute-start(bf16[12,80,128]{2,1,0:T(8,128)(2,1)S(1)} %all-to-all-done.left_own), channel_id=1, source_target_pairs={{0,48},{48,0},{1,49},{49,1},{2,50},{50,2},{3,51},{51,3},{4,52},{52... | collective-permute-start | bytes 737288 | tf_op jit(solution)/shard_map/ppermute | solution.py:194
  47.2 0.0 collective-permute-done.1.refs_1_
  47.2 0.0 collective-permute-done.6.refs_6_
  47.2 3.0 %collective-permute-done.7.refs_7_ = bf16[1040,128]{1,0:T(8,128)(2,1)S(1)} collective-permute-done((bf16[1040,128]{1,0:T(8,128)(2,1)S(1)}, bf16[1040,128]{1,0:T(8,128)(2,1)S(1)}, u32[]{:S(2)}, u32[]{:S(2)}) %collective-permute-start.7) | collective-permute-done | bytes 266272 | tf_op jit(solution)/shard_map/ppermute | solution.py:192
  50.2 3.3 %collective-permute-done.5.refs_5_ = bf16[1040,128]{1,0:T(8,128)(2,1)S(1)} collective-permute-done((bf16[1040,128]{1,0:T(8,128)(2,1)S(1)}, bf16[1040,128]{1,0:T(8,128)(2,1)S(1)}, u32[]{:S(2)}, u32[]{:S(2)}) %collective-permute-start.5) | collective-permute-done | bytes 266272 | tf_op jit(solution)/shard_map/ppermute | solution.py:191
  53.6 0.0 collective-permute-done.left_other
  53.6 7.0 %shard_map.48 = bf16[8,64,512]{2,1,0:T(8,128)(2,1)S(1)} custom-call(bf16[12,80,128]{2,1,0:T(8,128)(2,1)S(1)} %all-to-all-done.left_own, bf16[12,80,128]{2,1,0:T(8,128)(2,1)S(1)} %collective-permute-done.left_other, bf16[1040,128]{1,0:T(8,128)(2,1)S(1)} %copy-done, bf16[1040,128]{1,0:T(8,128)(2,1)S(1)} %collective-permute-done.1.refs_1_, ...), custom_call_target="tpu_custom_call" | custom-call | flops 1610612736 | bytes 4194304 | tf_op jit(solution)/shard_map/pallas_call | solution.py:161
  60.6 16.9 %all_to_all.10 = bf16[8,64,512]{2,1,0:T(8,128)(2,1)S(1)} all-to-all(bf16[8,64,512]{2,1,0:T(8,128)(2,1)S(1)} %shard_map.48), channel_id=1, replica_groups=mesh['y'=8,'core'=2,'col'=12,'layer'=4] {'core','layer'}, dimensions={0} | all-to-all | bytes 1048576 | tf_op jit(solution)/shard_map/all_to_all | solution.py:196
  77.5 0.1 convert_reduce_fusion
  77.6 0.8 %reshape.19 = f32[1,64,8,64]{3,2,1,0:T(8,128)} reshape(f32[64,512]{1,0:T(8,128)S(1)} %convert_reduce_fusion) | data formatting | bytes 262144 | tf_op jit(solution)/shard_map/reshape | solution.py:198
  (1 shorter events, 0.0 us)
Async XLA Ops:
  1.9 31.9 %collective-permute-start.4 = (bf16[1040,128]{1,0:T(8,128)(2,1)}, bf16[1040,128]{1,0:T(8,128)(2,1)S(1)}, u32[]{:S(2)}, u32[]{:S(2)}) collective-permute-start(bf16[1040,128]{1,0:T(8,128)(2,1)} %shard_map.47.refs_0_), channel_id=1, source_target_pairs={{0,576},{96,672},{192,0},{288,96},{384,192},{480,288},{576,384},{6... | collective-permute-start | bytes 798728 | tf_op jit(solution)/shard_map/ppermute | solution.py:188
  8.6 29.7 %collective-permute-start.3 = (bf16[1040,128]{1,0:T(8,128)(2,1)}, bf16[1040,128]{1,0:T(8,128)(2,1)S(1)}, u32[]{:S(2)}, u32[]{:S(2)}) collective-permute-start(bf16[1040,128]{1,0:T(8,128)(2,1)} %shard_map.47.refs_0_), channel_id=1, source_target_pairs={{0,192},{96,288},{192,384},{288,480},{384,576},{480,672},{576,0},{... | collective-permute-start | bytes 798728 | tf_op jit(solution)/shard_map/ppermute | solution.py:188
  12.1 15.0 %copy-start = (bf16[1040,128]{1,0:T(8,128)(2,1)S(1)}, bf16[1040,128]{1,0:T(8,128)(2,1)}, u32[]{:S(2)}) copy-start(bf16[1040,128]{1,0:T(8,128)(2,1)} %shard_map.47.refs_0_) | copy-start | bytes 798724
  12.1 31.3 %all-to-all-start = ((bf16[12,80,128]{2,1,0:T(8,128)(2,1)}), bf16[12,80,128]{2,1,0:T(8,128)(2,1)S(1)}, u32[]{:S(2)}, u32[]{:S(2)}) async-start(bf16[12,80,128]{2,1,0:T(8,128)(2,1)} %shard_map.46), calls=%async_computation | async-start | bytes 491520 | tf_op jit(solution)/shard_map/all_to_all | solution.py:190
  27.1 16.3 %collective-permute-start.2 = (bf16[1040,128]{1,0:T(8,128)(2,1)S(1)}, bf16[1040,128]{1,0:T(8,128)(2,1)S(1)}, u32[]{:S(2)}, u32[]{:S(2)}) collective-permute-start(bf16[1040,128]{1,0:T(8,128)(2,1)S(1)} %copy-done), channel_id=1, source_target_pairs={{0,672},{96,0},{192,96},{288,192},{384,288},{480,384},{576,480},{6... | collective-permute-start | bytes 798728 | tf_op jit(solution)/shard_map/ppermute | solution.py:187
  31.8 15.4 %collective-permute-start.1 = (bf16[1040,128]{1,0:T(8,128)(2,1)S(1)}, bf16[1040,128]{1,0:T(8,128)(2,1)S(1)}, u32[]{:S(2)}, u32[]{:S(2)}) collective-permute-start(bf16[1040,128]{1,0:T(8,128)(2,1)S(1)} %copy-done), channel_id=1, source_target_pairs={{0,96},{96,192},{192,288},{288,384},{384,480},{480,576},{576,672},... | collective-permute-start | bytes 798728 | tf_op jit(solution)/shard_map/ppermute | solution.py:187
  33.7 13.5 %collective-permute-start.6 = (bf16[1040,128]{1,0:T(8,128)(2,1)S(1)}, bf16[1040,128]{1,0:T(8,128)(2,1)S(1)}, u32[]{:S(2)}, u32[]{:S(2)}) collective-permute-start(bf16[1040,128]{1,0:T(8,128)(2,1)S(1)} %collective-permute-done.4.refs_4_), channel_id=1, source_target_pairs={{0,672},{96,0},{192,96},{288,192},{384,288},{480,384},{576,480},{6... | collective-permute-start | bytes 798728 | tf_op jit(solution)/shard_map/ppermute | solution.py:191
  38.4 11.8 %collective-permute-start.7 = (bf16[1040,128]{1,0:T(8,128)(2,1)S(1)}, bf16[1040,128]{1,0:T(8,128)(2,1)S(1)}, u32[]{:S(2)}, u32[]{:S(2)}) collective-permute-start(bf16[1040,128]{1,0:T(8,128)(2,1)S(1)} %broadcast_select_fusion), channel_id=1, source_target_pairs={{0,192},{48,624},{96,288},{144,720},{192,384},{240,48},{288,480},{... | collective-permute-start | bytes 798728 | tf_op jit(solution)/shard_map/ppermute | solution.py:192
  40.3 13.3 %collective-permute-start.5 = (bf16[1040,128]{1,0:T(8,128)(2,1)S(1)}, bf16[1040,128]{1,0:T(8,128)(2,1)S(1)}, u32[]{:S(2)}, u32[]{:S(2)}) collective-permute-start(bf16[1040,128]{1,0:T(8,128)(2,1)S(1)} %collective-permute-done.3.refs_3_), channel_id=1, source_target_pairs={{0,96},{96,192},{192,288},{288,384},{384,480},{480,576},{576,672},... | collective-permute-start | bytes 798728 | tf_op jit(solution)/shard_map/ppermute | solution.py:191
  43.4 10.1 %collective-permute-start = (bf16[12,80,128]{2,1,0:T(8,128)(2,1)S(1)}, bf16[12,80,128]{2,1,0:T(8,128)(2,1)S(1)}, u32[]{:S(2)}, u32[]{:S(2)}) collective-permute-start(bf16[12,80,128]{2,1,0:T(8,128)(2,1)S(1)} %all-to-all-done.left_own), channel_id=1, source_target_pairs={{0,48},{48,0},{1,49},{49,1},{2,50},{50,2},{3,51},{51,3},{4,52},{52... | collective-permute-start | bytes 737288 | tf_op jit(solution)/shard_map/ppermute | solution.py:194

commit v11 on v10

--- a/solution.py
+++ b/solution.py
@@ -8,7 +8,7 @@
 
 NB = 384
 BS = 64
-N_Y = 8
+N_YH = 4
 N_COL = 12
 N_LAYER = 4
 SLOTS = 32
@@ -21,12 +21,13 @@
 PIECE = NB // N_LAYER // N_COL
 DEPTH = INNER * BS
 WIDTH = COLUMNS * BS
-STEPS = (0, -1, 1, -2, 2, -3, 3, 4)
 GROUP = 4
+WINDOW = 2 * PIECE * BS
+AWAY = (0, 3, 1, 2)
 
 
 def pack_kernel(right, right_where, out, tail):
-    y = lax.axis_index("y")
+    y = lax.axis_index("yh") * 2 + lax.axis_index("yl")
     core = lax.axis_index("core")
     base = lax.axis_index("layer") * (NB // N_LAYER)
     for p in range(PAIRS):
@@ -111,29 +112,33 @@
     lax.fori_loop(0, PAIRS, place, 0, unroll=2)
 
 
-def place_kernel(left_own, left_other, *refs):
-    blocks, (out, left, total, where, places, sem), scratch = refs[:N_Y], refs[N_Y : N_Y + 6], refs[N_Y + 6 :]
+def place_kernel(left_own, left_other, mine, below, above, far, others, last, *refs):
+    (out, left, total, where, places, sem), scratch = refs[:6], refs[6:]
     panels, swapped = scratch[:GROUP], scratch[GROUP:]
-    y = lax.axis_index("y")
+    blocks = [mine, below, above, far, others.at[0], last, others.at[1], others.at[2]]
+    yh = lax.axis_index("yh")
+    yl = lax.axis_index("yl")
     core = lax.axis_index("core")
     copy = read_places(blocks, where, places, sem)
     swap = half_swap()
 
     lane = lax.broadcasted_iota(jnp.int32, (BS, 128), 1)
     upper = (lane >= BS).astype(jnp.float32)
-    for src, at in ((left_own, core), (left_other, 1 - core)):
+    for src, at in ((left_own, yl), (left_other, 1 - yl)):
         rows = pl.ds(pl.multiple_of(at * BS, BS), BS)
-        for c in range(N_COL):
-            there = jnp.dot(src[c], swap, preferred_element_type=jnp.float32)
-            here = src[c].astype(jnp.float32)
-            for g in range(PIECE // 2):
-                want = upper + 2.0 * g
-                value = jnp.where(here[BS : BS + 1] == want, here[:BS], 0.0)
-                value = value + jnp.where(there[BS : BS + 1] == want, there[:BS], 0.0)
-                at_lane = (c * PIECE + 2 * g) * BS
-                left[rows, at_lane : at_lane + 128] = value.astype(jnp.bfloat16)
-
-    for j0 in range(0, N_Y, GROUP):
+        for q in range(N_YH):
+            for u in range(2):
+                whole = src[3 * q + yl + u] if src is left_own else src[2 * q + u]
+                there = jnp.dot(whole, swap, preferred_element_type=jnp.float32)
+                here = whole.astype(jnp.float32)
+                for g in range(PIECE // 2):
+                    want = upper + 2.0 * g
+                    value = jnp.where(here[BS : BS + 1] == want, here[:BS], 0.0)
+                    value = value + jnp.where(there[BS : BS + 1] == want, there[:BS], 0.0)
+                    at_lane = q * WINDOW + (u * PIECE + 2 * g) * BS
+                    left[rows, at_lane : at_lane + 128] = value.astype(jnp.bfloat16)
+
+    for j0 in range(0, 2 * N_YH, GROUP):
         now = blocks[j0 : j0 + GROUP]
         for i, block in enumerate(now):
             panels[i][...] = jnp.zeros_like(panels[i])
@@ -144,8 +149,11 @@
             copy.wait()
         place_slots(now, j0, panels, swapped, places)
         for i in range(len(now)):
-            chip = lax.rem(y + N_Y + STEPS[j0 + i], N_Y)
-            at = pl.ds(pl.multiple_of((2 * chip + core) * DEPTH, 128), DEPTH)
+            j = j0 + i
+            side = core if j < N_YH else 1 - core
+            window = lax.rem(yh + AWAY[j % N_YH], N_YH)
+            start = window * WINDOW + yl * (4 * BS) + side * DEPTH
+            at = pl.ds(pl.multiple_of(start, 128), DEPTH)
             part = jnp.dot(left[:, at], panels[i][...], preferred_element_type=jnp.float32)
             total[...] = part if j0 + i == 0 else total[...] + part
     share = WIDTH // N_LAYER
@@ -164,7 +172,7 @@
         in_specs=[vmem] * len(operands),
         out_specs=vmem,
         scratch_shapes=[
-            pltpu.VMEM((2 * BS, NB // N_LAYER * BS), jnp.bfloat16),
+            pltpu.VMEM((2 * BS, N_YH * WINDOW), jnp.bfloat16),
             pltpu.VMEM((2 * BS, WIDTH), jnp.float32),
             pltpu.VMEM((16, 128), jnp.int32),
             pltpu.SMEM((16, 128), jnp.int32),
@@ -181,26 +189,26 @@
 
 def shards(left_blocks, left_coords, right_blocks, right_coords):
     mine = pack(right_blocks.reshape(SLOTS, BS, BS), right_coords.reshape(SLOTS, 2).T)
+    yl = lax.axis_index("yl")
     cross = [(0, 1), (1, 0)]
-    away = {d: [(i, (i + d) % N_Y) for i in range(N_Y)] for d in (-2, -1, 1, 2)}
-    far = [(2 * i + c, 2 * ((i + 2 - 4 * c) % N_Y) + c) for i in range(N_Y) for c in (0, 1)]
-    one = [lax.ppermute(mine, "y", away[d]) for d in (1, -1)]
-    two = [lax.ppermute(mine, "y", away[d]) for d in (2, -2)]
+    below, far, above = (
+        lax.ppermute(mine, "yh", [(i, (i + d) % N_YH) for i in range(N_YH)]) for d in (1, 2, 3)
+    )
     left = spread(left_blocks.reshape(2, BS, BS), left_coords.reshape(2, 2))
     pieces = lax.all_to_all(left, "col", 0, 0)
-    three = [lax.ppermute(two[0], "y", away[1]), lax.ppermute(two[1], "y", away[-1])]
-    four = lax.ppermute(jnp.where(lax.axis_index("core") == 0, *two), ("y", "core"), far)
-    blocks = [mine, *one, *two, *three, four]
-    pieces_other = lax.ppermute(pieces, "core", cross)
-    part = multiply(pieces, pieces_other, *blocks)
-    parts = lax.all_to_all(part, ("core", "layer"), 0, 0)
+    others = lax.ppermute(jnp.stack([mine, above, far]), "core", cross)
+    last = lax.ppermute(below, "core", cross)
+    wanted = lax.dynamic_slice_in_dim(pieces.reshape(N_YH, 3, LMSG, 128), 1 - yl, 2, 1)
+    pieces_other = lax.ppermute(wanted.reshape(2 * N_YH, LMSG, 128), "yl", cross)
+    part = multiply(pieces, pieces_other, mine, below, above, far, others, last)
+    parts = lax.all_to_all(part, ("yl", "layer"), 0, 0)
     total = jnp.sum(parts.astype(jnp.float32), axis=0)
     return total.reshape(1, BS, COLUMNS // N_LAYER, BS)
 
 
 def solution(mesh):
-    grid = Mesh(mesh.devices.reshape(N_Y, 2, N_COL, N_LAYER), ("y", "core", "col", "layer"))
-    row = ("y", "core")
+    grid = Mesh(mesh.devices.reshape(N_YH, 2, 2, N_COL, N_LAYER), ("yh", "yl", "core", "col", "layer"))
+    row = ("yh", "yl", "core")
     return jax.shard_map(
         shards,
         mesh=grid,

time: 78.9 us -> 87.4 us (1.11); the launches traced: 78.4 us -> 85.8 us
  waiting for transfers between devices: 6.35 us -> 21.4 us
  blocking collectives: 16.9 us -> 13.2 us
  starting transfers between devices: 43.6 us -> 40 us
    ppermute x8 -> x6, waiting for transfers between devices: 6.35 us -> 21.4 us  [the longest x3 16.8 us: shards(): lax.ppermute(mine, 'yh', [(i, (i + d) % N_YH) for i in range(N_YH)])]
    all_to_all x1, blocking collectives: 16.9 us -> 13.2 us  [shards(): parts = lax.all_to_all(part, ('yl', 'layer'), 0, 0)]
    ppermute x8 -> x6, starting transfers between devices: 28.6 us -> 25 us  [the longest x3 12.2 us: shards(): lax.ppermute(mine, 'yh', [(i, (i + d) % N_YH) for i in range(N_YH)])]
  transfers between devices with their start and end apart: 9 -> 7, of which waited for: 2 -> 2; matrix products, arithmetic and copies ran while one was open for 0% -> 0% of each run, Pallas kernels for 2% -> 2%
where the time goes in v11:
time: 87.4 us; the launch traced here: 85.8 us
  starting transfers between devices  40 us (46%)
  waiting for transfers between devices  21.4 us (24%)
  blocking collectives  13.2 us (15%)
  Pallas kernels  10.2 us (12%)
    ppermute x3, waiting for transfers between devices, shards(): lax.ppermute(mine, 'yh', [(i, (i + d) % N_YH) for i in range(N_YH)])  16.8 us
    all_to_all x1, starting transfers between devices, shards(): pieces = lax.all_to_all(left, 'col', 0, 0)  15 us
    all_to_all x1, blocking collectives, shards(): parts = lax.all_to_all(part, ('yl', 'layer'), 0, 0)  13.2 us
    ppermute x3, starting transfers between devices, shards(): lax.ppermute(mine, 'yh', [(i, (i + d) % N_YH) for i in range(N_YH)])  12.2 us
    pallas_call x1, Pallas kernels, multiply(): pl.pallas_call(place_kernel, out_shape=jax.ShapeDtypeStruct((2 * N_LAYER,...  6.73 us
    ppermute x1, starting transfers between devices, shards(): others = lax.ppermute(jnp.stack([mine, above, far]), 'core', cross)  5.8 us
    ppermute x1, starting transfers between devices, shards(): lax.ppermute(wanted.reshape(2 * N_YH, LMSG, 128), 'yl', cross)  4.68 us
    ppermute x1, waiting for transfers between devices, shards(): lax.ppermute(wanted.reshape(2 * N_YH, LMSG, 128), 'yl', cross)  4.54 us
  transfers between devices with their start and end apart: 7, of which 2 were waited for; matrix products, arithmetic and copies ran while one was open for 0% of the time, Pallas kernels for 2%

profile of v11, /device:TPU:1, one launch (start us, length us, event | category | flops | bytes accessed | tf_op | source)
XLA Modules:
  0.0 85.8 jit_solution(9831525479825575332)
XLA Ops:
  0.0 1.9 %shard_map.47.mine = bf16[1040,128]{1,0:T(8,128)(2,1)} custom-call(bf16[32,64,64]{2,1,0:T(8,128)(2,1)} %bitcast.15, s32[2,32]{1,0:T(2,128)} %bitcast.18), custom_call_target="tpu_custom_call" | custom-call | bytes 1048576 | tf_op jit(solution)/shard_map/pallas_call | solution.py:45
  1.9 6.7 %collective-permute-start.2 = (bf16[1040,128]{1,0:T(8,128)(2,1)}, bf16[1040,128]{1,0:T(8,128)(2,1)S(1)}, u32[]{:S(2)}, u32[]{:S(2)}) collective-permute-start(bf16[1040,128]{1,0:T(8,128)(2,1)} %shard_map.47.mine), channel_id=1, source_target_pairs={{0,576},{192,0},{384,192},{576,384},{1,577},{193,1},{385,193},{577... | collective-permute-start | bytes 798728 | tf_op jit(solution)/shard_map/ppermute | solution.py:195
  8.6 3.5 %collective-permute-start.3 = (bf16[1040,128]{1,0:T(8,128)(2,1)}, bf16[1040,128]{1,0:T(8,128)(2,1)S(1)}, u32[]{:S(2)}, u32[]{:S(2)}) collective-permute-start(bf16[1040,128]{1,0:T(8,128)(2,1)} %shard_map.47.mine), channel_id=1, source_target_pairs={{0,384},{192,576},{384,0},{576,192},{1,385},{193,577},{385,1},{577... | collective-permute-start | bytes 798728 | tf_op jit(solution)/shard_map/ppermute | solution.py:195
  12.1 1.6 %shard_map.46 = bf16[12,80,128]{2,1,0:T(8,128)(2,1)} custom-call(bf16[2,64,64]{2,1,0:T(8,128)(2,1)} %bitcast.17, s32[2,2]{1,0:T(2,128)} %bitcast.19), custom_call_target="tpu_custom_call" | custom-call | bytes 1048576 | tf_op jit(solution)/shard_map/pallas_call | solution.py:69
  13.7 0.0 copy-start
  13.7 15.0 %all-to-all-start = ((bf16[12,80,128]{2,1,0:T(8,128)(2,1)}), bf16[12,80,128]{2,1,0:T(8,128)(2,1)S(1)}, u32[]{:S(2)}, u32[]{:S(2)}) async-start(bf16[12,80,128]{2,1,0:T(8,128)(2,1)} %shard_map.46), calls=%async_computation | async-start | bytes 491520 | tf_op jit(solution)/shard_map/all_to_all | solution.py:198
  28.7 0.0 collective-permute-done.2.above
  28.7 0.0 collective-permute-done.3.far
  28.7 0.0 copy-done
  28.7 0.1 pad_maximum_fusion
  28.8 5.8 %collective-permute-start.4 = (bf16[3,1040,128]{2,1,0:T(8,128)(2,1)S(1)}, bf16[3,1040,128]{2,1,0:T(8,128)(2,1)S(1)}, u32[]{:S(2)}, u32[]{:S(2)}) collective-permute-start(bf16[3,1040,128]{2,1,0:T(8,128)(2,1)S(1)} %pad_maximum_fusion), channel_id=1, source_target_pairs={{0,48},{48,0},{1,49},{49,1},{2,50},{50,2},{3,51},{51,3},{4,52},{52... | collective-permute-start | bytes 2396168 | tf_op jit(solution)/shard_map/ppermute | solution.py:199
  34.7 1.9 %collective-permute-start.1 = (bf16[1040,128]{1,0:T(8,128)(2,1)S(1)}, bf16[1040,128]{1,0:T(8,128)(2,1)S(1)}, u32[]{:S(2)}, u32[]{:S(2)}) collective-permute-start(bf16[1040,128]{1,0:T(8,128)(2,1)S(1)} %copy-done), channel_id=1, source_target_pairs={{0,192},{192,384},{384,576},{576,0},{1,193},{193,385},{385,577},{5... | collective-permute-start | bytes 798728 | tf_op jit(solution)/shard_map/ppermute | solution.py:195
  36.6 16.8 %collective-permute-done.1.below = bf16[1040,128]{1,0:T(8,128)(2,1)S(1)} collective-permute-done((bf16[1040,128]{1,0:T(8,128)(2,1)S(1)}, bf16[1040,128]{1,0:T(8,128)(2,1)S(1)}, u32[]{:S(2)}, u32[]{:S(2)}) %collective-permute-start.1) | collective-permute-done | bytes 266272 | tf_op jit(solution)/shard_map/ppermute | solution.py:195
  53.4 2.4 %collective-permute-start.5 = (bf16[1040,128]{1,0:T(8,128)(2,1)S(1)}, bf16[1040,128]{1,0:T(8,128)(2,1)S(1)}, u32[]{:S(2)}, u32[]{:S(2)}) collective-permute-start(bf16[1040,128]{1,0:T(8,128)(2,1)S(1)} %collective-permute-done.1.below), channel_id=1, source_target_pairs={{0,48},{48,0},{1,49},{49,1},{2,50},{50,2},{3,51},{51,3},{4,52},{52... | collective-permute-start | bytes 798728 | tf_op jit(solution)/shard_map/ppermute | solution.py:200
  55.8 0.0 all-to-all-done.left_own
  55.8 4.7 %collective-permute-start = (bf16[8,80,128]{2,1,0:T(8,128)(2,1)S(1)}, bf16[8,80,128]{2,1,0:T(8,128)(2,1)S(1)}, u32[]{:S(2)}, u32[]{:S(2)}) collective-permute-start(bf16[8,80,128]{2,1,0:T(8,128)(2,1)S(1)} %bitcast.16), channel_id=1, source_target_pairs={{0,96},{96,0},{1,97},{97,1},{2,98},{98,2},{3,99},{99,3},{4,100},{1... | collective-permute-start | bytes 491528 | tf_op jit(solution)/shard_map/ppermute | solution.py:202
  60.5 0.0 collective-permute-done.5.last
  60.5 4.5 %collective-permute-done.left_other = bf16[8,80,128]{2,1,0:T(8,128)(2,1)S(1)} collective-permute-done((bf16[8,80,128]{2,1,0:T(8,128)(2,1)S(1)}, bf16[8,80,128]{2,1,0:T(8,128)(2,1)S(1)}, u32[]{:S(2)}, u32[]{:S(2)}) %collective-permute-start) | collective-permute-done | bytes 163872 | tf_op jit(solution)/shard_map/ppermute | solution.py:202
  65.0 0.0 collective-permute-done.4.others
  65.0 6.7 %shard_map.48 = bf16[8,64,512]{2,1,0:T(8,128)(2,1)S(1)} custom-call(bf16[12,80,128]{2,1,0:T(8,128)(2,1)S(1)} %all-to-all-done.left_own, bf16[8,80,128]{2,1,0:T(8,128)(2,1)S(1)} %collective-permute-done.left_other, bf16[1040,128]{1,0:T(8,128)(2,1)S(1)} %copy-done, bf16[1040,128]{1,0:T(8,128)(2,1)S(1)} %collective-permute-done.1.below, ...), custom_call_target="tpu_custom_call" | custom-call | flops 1610612736 | bytes 4194304 | tf_op jit(solution)/shard_map/pallas_call | solution.py:169
  71.8 13.2 %all_to_all.10 = bf16[8,64,512]{2,1,0:T(8,128)(2,1)S(1)} all-to-all(bf16[8,64,512]{2,1,0:T(8,128)(2,1)S(1)} %shard_map.48), channel_id=1, replica_groups=mesh['yh'=4,'yl'=2,'core'=2,'col'=12,'layer'=4] {'yl','layer'}, dimensions={0} | all-to-all | bytes 1048576 | tf_op jit(solution)/shard_map/all_to_all | solution.py:204
  85.0 0.1 convert_reduce_fusion
  85.0 0.8 reshape.27
  (1 shorter events, 0.0 us)
Async XLA Ops:
  1.9 26.8 %collective-permute-start.2 = (bf16[1040,128]{1,0:T(8,128)(2,1)}, bf16[1040,128]{1,0:T(8,128)(2,1)S(1)}, u32[]{:S(2)}, u32[]{:S(2)}) collective-permute-start(bf16[1040,128]{1,0:T(8,128)(2,1)} %shard_map.47.mine), channel_id=1, source_target_pairs={{0,576},{192,0},{384,192},{576,384},{1,577},{193,1},{385,193},{577... | collective-permute-start | bytes 798728 | tf_op jit(solution)/shard_map/ppermute | solution.py:195
  8.6 20.1 %collective-permute-start.3 = (bf16[1040,128]{1,0:T(8,128)(2,1)}, bf16[1040,128]{1,0:T(8,128)(2,1)S(1)}, u32[]{:S(2)}, u32[]{:S(2)}) collective-permute-start(bf16[1040,128]{1,0:T(8,128)(2,1)} %shard_map.47.mine), channel_id=1, source_target_pairs={{0,384},{192,576},{384,0},{576,192},{1,385},{193,577},{385,1},{577... | collective-permute-start | bytes 798728 | tf_op jit(solution)/shard_map/ppermute | solution.py:195
  13.7 15.0 %copy-start = (bf16[1040,128]{1,0:T(8,128)(2,1)S(1)}, bf16[1040,128]{1,0:T(8,128)(2,1)}, u32[]{:S(2)}) copy-start(bf16[1040,128]{1,0:T(8,128)(2,1)} %shard_map.47.mine) | copy-start | bytes 798724
  13.7 42.1 %all-to-all-start = ((bf16[12,80,128]{2,1,0:T(8,128)(2,1)}), bf16[12,80,128]{2,1,0:T(8,128)(2,1)S(1)}, u32[]{:S(2)}, u32[]{:S(2)}) async-start(bf16[12,80,128]{2,1,0:T(8,128)(2,1)} %shard_map.46), calls=%async_computation | async-start | bytes 491520 | tf_op jit(solution)/shard_map/all_to_all | solution.py:198
  28.8 36.2 %collective-permute-start.4 = (bf16[3,1040,128]{2,1,0:T(8,128)(2,1)S(1)}, bf16[3,1040,128]{2,1,0:T(8,128)(2,1)S(1)}, u32[]{:S(2)}, u32[]{:S(2)}) collective-permute-start(bf16[3,1040,128]{2,1,0:T(8,128)(2,1)S(1)} %pad_maximum_fusion), channel_id=1, source_target_pairs={{0,48},{48,0},{1,49},{49,1},{2,50},{50,2},{3,51},{51,3},{4,52},{52... | collective-permute-start | bytes 2396168 | tf_op jit(solution)/shard_map/ppermute | solution.py:199
  34.7 18.7 %collective-permute-start.1 = (bf16[1040,128]{1,0:T(8,128)(2,1)S(1)}, bf16[1040,128]{1,0:T(8,128)(2,1)S(1)}, u32[]{:S(2)}, u32[]{:S(2)}) collective-permute-start(bf16[1040,128]{1,0:T(8,128)(2,1)S(1)} %copy-done), channel_id=1, source_target_pairs={{0,192},{192,384},{384,576},{576,0},{1,193},{193,385},{385,577},{5... | collective-permute-start | bytes 798728 | tf_op jit(solution)/shard_map/ppermute | solution.py:195
  53.4 7.1 %collective-permute-start.5 = (bf16[1040,128]{1,0:T(8,128)(2,1)S(1)}, bf16[1040,128]{1,0:T(8,128)(2,1)S(1)}, u32[]{:S(2)}, u32[]{:S(2)}) collective-permute-start(bf16[1040,128]{1,0:T(8,128)(2,1)S(1)} %collective-permute-done.1.below), channel_id=1, source_target_pairs={{0,48},{48,0},{1,49},{49,1},{2,50},{50,2},{3,51},{51,3},{4,52},{52... | collective-permute-start | bytes 798728 | tf_op jit(solution)/shard_map/ppermute | solution.py:200
  55.8 9.2 %collective-permute-start = (bf16[8,80,128]{2,1,0:T(8,128)(2,1)S(1)}, bf16[8,80,128]{2,1,0:T(8,128)(2,1)S(1)}, u32[]{:S(2)}, u32[]{:S(2)}) collective-permute-start(bf16[8,80,128]{2,1,0:T(8,128)(2,1)S(1)} %bitcast.16), channel_id=1, source_target_pairs={{0,96},{96,0},{1,97},{97,1},{2,98},{98,2},{3,99},{99,3},{4,100},{1... | collective-permute-start | bytes 491528 | tf_op jit(solution)/shard_map/ppermute | solution.py:202

commit v12 on v9

--- a/solution.py
+++ b/solution.py
@@ -112,8 +112,9 @@
     lax.fori_loop(0, PAIRS, place, 0, unroll=2)
 
 
-def place_kernel(left_own, left_other, *refs):
-    blocks, (out, left, total, where, places, sem), scratch = refs[:N_Y], refs[N_Y : N_Y + 6], refs[N_Y + 6 :]
+def place_kernel(left_own, left_other, mine, one, two, three, four, *refs):
+    (out, left, total, where, places, sem), scratch = refs[:6], refs[6:]
+    blocks = [mine, one.at[0], one.at[1], two.at[0], two.at[1], three.at[0], three.at[1], four]
     panels, swapped = scratch[:GROUP], scratch[GROUP:]
     y = lax.axis_index("y")
     core = lax.axis_index("core")
@@ -184,18 +185,20 @@
 
 def shards(left_blocks, left_coords, right_blocks, right_coords):
     mine = pack(right_blocks.reshape(SLOTS, BS, BS), right_coords.reshape(SLOTS, 2).T)
-    ring = [(2 * i + c, 2 * ((i + 1 - 2 * c) % N_Y) + c) for i in range(N_Y) for c in (0, 1)]
     cross = [(0, 1), (1, 0)]
+    on = [
+        [(2 * i + c, 2 * ((i + d * (1 - 2 * c)) % N_Y) + c) for i in range(N_Y) for c in (0, 1)]
+        for d in range(3)
+    ]
     axes = ("y", "core")
-    a = lax.ppermute(mine, axes, ring)
-    b = lax.ppermute(mine, "core", cross)
+    both = jnp.stack([mine, lax.ppermute(mine, "core", cross)])
+    one = lax.ppermute(both, axes, on[1])
+    two = lax.ppermute(both, axes, on[2])
     left = spread(left_blocks.reshape(2, BS, BS), left_coords.reshape(2, 2))
     pieces = lax.all_to_all(left, "col", 0, 0)
-    blocks = [mine, a]
-    for _ in range(3):
-        b = lax.ppermute(b, axes, ring)
-        a = lax.ppermute(a, axes, ring)
-        blocks += [b, a]
+    three = lax.ppermute(two, axes, on[1])
+    four = lax.ppermute(two[0], axes, on[2])
+    blocks = [mine, one, two, three, four]
     pieces_other = lax.ppermute(pieces, "core", cross)
     part = multiply(pieces, pieces_other, *blocks)
     parts = lax.all_to_all(part, ("core", "layer"), 0, 0)

time: 79.6 us -> 74.6 us (0.937)
  starting transfers between devices: 46.7 us -> 34.1 us
  waiting for transfers between devices: 3.71 us -> 13.3 us
  blocking collectives: 17.1 us -> 14.2 us
  other arithmetic: 0.07 us -> 1.07 us
    ppermute x8 -> x5, starting transfers between devices: 35.5 us -> 22.4 us  [the longest x1 12.4 us: shards(): both = jnp.stack([mine, lax.ppermute(mine, 'core', cross)])]
    all_to_all x1, waiting for transfers between devices: 0.01 us -> 6.95 us  [shards(): pieces = lax.all_to_all(left, 'col', 0, 0)]
    all_to_all x1, blocking collectives: 17.1 us -> 14.2 us  [shards(): parts = lax.all_to_all(part, ('core', 'layer'), 0, 0)]
    ppermute x8 -> x5, waiting for transfers between devices: 2.35 us -> 4.88 us  [the longest x1 3.51 us: shards(): four = lax.ppermute(two[0], axes, on[2])]
    another operation x0 -> x1, other arithmetic: none -> 1 us  [shards(): both = jnp.stack([mine, lax.ppermute(mine, 'core', cross)])]
  transfers between devices with their start and end apart: 10 -> 7, of which waited for: 4 -> 4; matrix products, arithmetic and copies ran while one was open for 0% -> 0% of each run, Pallas kernels for 2% -> 2%
where the time goes in v12:
time: 74.6 us; the launch traced here: 74.1 us
  starting transfers between devices  34.1 us (46%)
  blocking collectives  14.2 us (19%)
  waiting for transfers between devices  13.3 us (18%)
  Pallas kernels  10.4 us (14%)
  other arithmetic  1.07 us (1%)
  local copies, waits for them, and re-layouts  0.83 us (1%)
    all_to_all x1, blocking collectives, shards(): parts = lax.all_to_all(part, ('core', 'layer'), 0, 0)  14.2 us
    ppermute x1, starting transfers between devices, shards(): both = jnp.stack([mine, lax.ppermute(mine, 'core', cross)])  12.4 us
    all_to_all x1, starting transfers between devices, shards(): pieces = lax.all_to_all(left, 'col', 0, 0)  9.83 us
    pallas_call x1, Pallas kernels, multiply(): pl.pallas_call(place_kernel, out_shape=jax.ShapeDtypeStruct((2 * N_LAYER,...  7 us
    all_to_all x1, waiting for transfers between devices, shards(): pieces = lax.all_to_all(left, 'col', 0, 0)  6.95 us
    ppermute x1, waiting for transfers between devices, shards(): four = lax.ppermute(two[0], axes, on[2])  3.51 us
    ppermute x1, starting transfers between devices, shards(): one = lax.ppermute(both, axes, on[1])  3.11 us
    ppermute x1, starting transfers between devices, shards(): three = lax.ppermute(two, axes, on[1])  2.98 us
  transfers between devices with their start and end apart: 7, of which 4 were waited for; matrix products, arithmetic and copies ran while one was open for 0% of the time, Pallas kernels for 2%

profile of v12, /device:TPU:1, one launch (start us, length us, event | category | flops | bytes accessed | tf_op | source)
XLA Modules:
  0.0 74.1 jit_solution(16891800242254231906)
XLA Ops:
  0.0 1.9 %shard_map.47.mine = bf16[1040,128]{1,0:T(8,128)(2,1)} custom-call(bf16[32,64,64]{2,1,0:T(8,128)(2,1)} %bitcast.11, s32[2,32]{1,0:T(2,128)} %bitcast.14), custom_call_target="tpu_custom_call" | custom-call | bytes 1048576 | tf_op jit(solution)/shard_map/pallas_call | solution.py:45
  1.9 12.4 %collective-permute-start.1 = (bf16[1040,128]{1,0:T(8,128)(2,1)}, bf16[1040,128]{1,0:T(8,128)(2,1)S(1)}, u32[]{:S(2)}, u32[]{:S(2)}) collective-permute-start(bf16[1040,128]{1,0:T(8,128)(2,1)} %shard_map.47.mine), channel_id=1, source_target_pairs={{0,48},{48,0},{1,49},{49,1},{2,50},{50,2},{3,51},{51,3},{4,52},{52... | collective-permute-start | bytes 798728 | tf_op jit(solution)/shard_map/ppermute | solution.py:194
  14.3 1.4 %collective-permute-done.1 = bf16[1040,128]{1,0:T(8,128)(2,1)S(1)} collective-permute-done((bf16[1040,128]{1,0:T(8,128)(2,1)}, bf16[1040,128]{1,0:T(8,128)(2,1)S(1)}, u32[]{:S(2)}, u32[]{:S(2)}) %collective-permute-start.1) | collective-permute-done | bytes 266272 | tf_op jit(solution)/shard_map/ppermute | solution.py:194
  15.7 1.0 %pad_maximum_fusion = bf16[2,1040,128]{2,1,0:T(8,128)(2,1)S(1)} fusion(bf16[1,1040,128]{2,1,0:T(8,128)(2,1)S(1)} %bitcast.12, bf16[1,1040,128]{2,1,0:T(8,128)(2,1)} %bitcast.10), kind=kLoop, calls=%fused_computation.1 | loop fusion | flops 266240 | bytes 1064960 | tf_op jit(solution)/shard_map/stack | solution.py:194
  16.7 1.9 %collective-permute-start.3 = (bf16[2,1040,128]{2,1,0:T(8,128)(2,1)S(1)}, bf16[2,1040,128]{2,1,0:T(8,128)(2,1)S(1)}, u32[]{:S(2)}, u32[]{:S(2)}) collective-permute-start(bf16[2,1040,128]{2,1,0:T(8,128)(2,1)S(1)} %pad_maximum_fusion), channel_id=1, source_target_pairs={{0,192},{48,624},{96,288},{144,720},{192,384},{240,48},{288,480},{... | collective-permute-start | bytes 1597448 | tf_op jit(solution)/shard_map/ppermute | solution.py:196
  18.6 1.6 %shard_map.46 = bf16[12,80,128]{2,1,0:T(8,128)(2,1)} custom-call(bf16[2,64,64]{2,1,0:T(8,128)(2,1)} %bitcast.13, s32[2,2]{1,0:T(2,128)} %bitcast.15), custom_call_target="tpu_custom_call" | custom-call | bytes 1048576 | tf_op jit(solution)/shard_map/pallas_call | solution.py:69
  20.2 9.8 %all-to-all-start = ((bf16[12,80,128]{2,1,0:T(8,128)(2,1)}), bf16[12,80,128]{2,1,0:T(8,128)(2,1)S(1)}, u32[]{:S(2)}, u32[]{:S(2)}) async-start(bf16[12,80,128]{2,1,0:T(8,128)(2,1)} %shard_map.46), calls=%async_computation | async-start | bytes 491520 | tf_op jit(solution)/shard_map/all_to_all | solution.py:198
  30.0 0.0 copy-start
  30.0 3.1 %collective-permute-start.2 = (bf16[2,1040,128]{2,1,0:T(8,128)(2,1)S(1)}, bf16[2,1040,128]{2,1,0:T(8,128)(2,1)S(1)}, u32[]{:S(2)}, u32[]{:S(2)}) collective-permute-start(bf16[2,1040,128]{2,1,0:T(8,128)(2,1)S(1)} %pad_maximum_fusion), channel_id=1, source_target_pairs={{0,96},{48,720},{96,192},{144,48},{192,288},{240,144},{288,384},{3... | collective-permute-start | bytes 1597448 | tf_op jit(solution)/shard_map/ppermute | solution.py:195
  33.1 0.0 collective-permute-done.3.two
  33.1 3.0 %collective-permute-start.4 = (bf16[2,1040,128]{2,1,0:T(8,128)(2,1)S(1)}, bf16[2,1040,128]{2,1,0:T(8,128)(2,1)S(1)}, u32[]{:S(2)}, u32[]{:S(2)}) collective-permute-start(bf16[2,1040,128]{2,1,0:T(8,128)(2,1)S(1)} %collective-permute-done.3.two), channel_id=1, source_target_pairs={{0,96},{48,720},{96,192},{144,48},{192,288},{240,144},{288,384},{3... | collective-permute-start | bytes 1597448 | tf_op jit(solution)/shard_map/ppermute | solution.py:199
  36.1 2.0 %collective-permute-start.5 = (bf16[1040,128]{1,0:T(8,128)(2,1)S(1)}, bf16[1040,128]{1,0:T(8,128)(2,1)S(1)}, u32[]{:S(2)}, u32[]{:S(2)}) collective-permute-start(bf16[1040,128]{1,0:T(8,128)(2,1)S(1)} %slice_bitcast_fusion), channel_id=1, source_target_pairs={{0,192},{48,624},{96,288},{144,720},{192,384},{240,48},{288,480},{... | collective-permute-start | bytes 798728 | tf_op jit(solution)/shard_map/ppermute | solution.py:200
  38.1 6.9 %all-to-all-done.left_own = bf16[12,80,128]{2,1,0:T(8,128)(2,1)S(1)} async-done(((bf16[12,80,128]{2,1,0:T(8,128)(2,1)}), bf16[12,80,128]{2,1,0:T(8,128)(2,1)S(1)}, u32[]{:S(2)}, u32[]{:S(2)}) %all-to-all-start) | async-done | bytes 245792 | tf_op jit(solution)/shard_map/all_to_all | solution.py:198
  45.1 1.9 %collective-permute-start = (bf16[12,80,128]{2,1,0:T(8,128)(2,1)S(1)}, bf16[12,80,128]{2,1,0:T(8,128)(2,1)S(1)}, u32[]{:S(2)}, u32[]{:S(2)}) collective-permute-start(bf16[12,80,128]{2,1,0:T(8,128)(2,1)S(1)} %all-to-all-done.left_own), channel_id=1, source_target_pairs={{0,48},{48,0},{1,49},{49,1},{2,50},{50,2},{3,51},{51,3},{4,52},{52... | collective-permute-start | bytes 737288 | tf_op jit(solution)/shard_map/ppermute | solution.py:202
  47.0 0.0 collective-permute-done.2.one
  47.0 1.5 %collective-permute-done.left_other = bf16[12,80,128]{2,1,0:T(8,128)(2,1)S(1)} collective-permute-done((bf16[12,80,128]{2,1,0:T(8,128)(2,1)S(1)}, bf16[12,80,128]{2,1,0:T(8,128)(2,1)S(1)}, u32[]{:S(2)}, u32[]{:S(2)}) %collective-permute-start) | collective-permute-done | bytes 245792 | tf_op jit(solution)/shard_map/ppermute | solution.py:202
  48.5 3.5 %collective-permute-done.5.four = bf16[1040,128]{1,0:T(8,128)(2,1)S(1)} collective-permute-done((bf16[1040,128]{1,0:T(8,128)(2,1)S(1)}, bf16[1040,128]{1,0:T(8,128)(2,1)S(1)}, u32[]{:S(2)}, u32[]{:S(2)}) %collective-permute-start.5) | collective-permute-done | bytes 266272 | tf_op jit(solution)/shard_map/ppermute | solution.py:200
  52.0 0.0 collective-permute-done.4.three
  52.0 0.0 copy-done
  52.0 7.0 %shard_map.48 = bf16[8,64,512]{2,1,0:T(8,128)(2,1)S(1)} custom-call(bf16[12,80,128]{2,1,0:T(8,128)(2,1)S(1)} %all-to-all-done.left_own, bf16[12,80,128]{2,1,0:T(8,128)(2,1)S(1)} %collective-permute-done.left_other, bf16[1040,128]{1,0:T(8,128)(2,1)S(1)} %copy-done, bf16[2,1040,128]{2,1,0:T(8,128)(2,1)S(1)} %collective-permute-done.2.one, ...), custom_call_target="tpu_custom_call" | custom-call | flops 1610612736 | bytes 4194304 | tf_op jit(solution)/shard_map/pallas_call | solution.py:165
  59.0 14.2 %all_to_all.10 = bf16[8,64,512]{2,1,0:T(8,128)(2,1)S(1)} all-to-all(bf16[8,64,512]{2,1,0:T(8,128)(2,1)S(1)} %shard_map.48), channel_id=1, replica_groups=mesh['y'=8,'core'=2,'col'=12,'layer'=4] {'core','layer'}, dimensions={0} | all-to-all | bytes 1048576 | tf_op jit(solution)/shard_map/all_to_all | solution.py:204
  73.2 0.1 convert_reduce_fusion
  73.3 0.8 %reshape.19 = f32[1,64,8,64]{3,2,1,0:T(8,128)} reshape(f32[64,512]{1,0:T(8,128)S(1)} %convert_reduce_fusion) | data formatting | bytes 262144 | tf_op jit(solution)/shard_map/reshape | solution.py:206
  (1 shorter events, 0.0 us)
Async XLA Ops:
  1.9 13.8 %collective-permute-start.1 = (bf16[1040,128]{1,0:T(8,128)(2,1)}, bf16[1040,128]{1,0:T(8,128)(2,1)S(1)}, u32[]{:S(2)}, u32[]{:S(2)}) collective-permute-start(bf16[1040,128]{1,0:T(8,128)(2,1)} %shard_map.47.mine), channel_id=1, source_target_pairs={{0,48},{48,0},{1,49},{49,1},{2,50},{50,2},{3,51},{51,3},{4,52},{52... | collective-permute-start | bytes 798728 | tf_op jit(solution)/shard_map/ppermute | solution.py:194
  16.7 16.5 %collective-permute-start.3 = (bf16[2,1040,128]{2,1,0:T(8,128)(2,1)S(1)}, bf16[2,1040,128]{2,1,0:T(8,128)(2,1)S(1)}, u32[]{:S(2)}, u32[]{:S(2)}) collective-permute-start(bf16[2,1040,128]{2,1,0:T(8,128)(2,1)S(1)} %pad_maximum_fusion), channel_id=1, source_target_pairs={{0,192},{48,624},{96,288},{144,720},{192,384},{240,48},{288,480},{... | collective-permute-start | bytes 1597448 | tf_op jit(solution)/shard_map/ppermute | solution.py:196
  20.2 24.9 %all-to-all-start = ((bf16[12,80,128]{2,1,0:T(8,128)(2,1)}), bf16[12,80,128]{2,1,0:T(8,128)(2,1)S(1)}, u32[]{:S(2)}, u32[]{:S(2)}) async-start(bf16[12,80,128]{2,1,0:T(8,128)(2,1)} %shard_map.46), calls=%async_computation | async-start | bytes 491520 | tf_op jit(solution)/shard_map/all_to_all | solution.py:198
  30.0 22.0 %copy-start = (bf16[1040,128]{1,0:T(8,128)(2,1)S(1)}, bf16[1040,128]{1,0:T(8,128)(2,1)}, u32[]{:S(2)}) copy-start(bf16[1040,128]{1,0:T(8,128)(2,1)} %shard_map.47.mine) | copy-start | bytes 798724
  30.0 17.0 %collective-permute-start.2 = (bf16[2,1040,128]{2,1,0:T(8,128)(2,1)S(1)}, bf16[2,1040,128]{2,1,0:T(8,128)(2,1)S(1)}, u32[]{:S(2)}, u32[]{:S(2)}) collective-permute-start(bf16[2,1040,128]{2,1,0:T(8,128)(2,1)S(1)} %pad_maximum_fusion), channel_id=1, source_target_pairs={{0,96},{48,720},{96,192},{144,48},{192,288},{240,144},{288,384},{3... | collective-permute-start | bytes 1597448 | tf_op jit(solution)/shard_map/ppermute | solution.py:195
  33.1 18.8 %collective-permute-start.4 = (bf16[2,1040,128]{2,1,0:T(8,128)(2,1)S(1)}, bf16[2,1040,128]{2,1,0:T(8,128)(2,1)S(1)}, u32[]{:S(2)}, u32[]{:S(2)}) collective-permute-start(bf16[2,1040,128]{2,1,0:T(8,128)(2,1)S(1)} %collective-permute-done.3.two), channel_id=1, source_target_pairs={{0,96},{48,720},{96,192},{144,48},{192,288},{240,144},{288,384},{3... | collective-permute-start | bytes 1597448 | tf_op jit(solution)/shard_map/ppermute | solution.py:199
  36.1 15.8 %collective-permute-start.5 = (bf16[1040,128]{1,0:T(8,128)(2,1)S(1)}, bf16[1040,128]{1,0:T(8,128)(2,1)S(1)}, u32[]{:S(2)}, u32[]{:S(2)}) collective-permute-start(bf16[1040,128]{1,0:T(8,128)(2,1)S(1)} %slice_bitcast_fusion), channel_id=1, source_target_pairs={{0,192},{48,624},{96,288},{144,720},{192,384},{240,48},{288,480},{... | collective-permute-start | bytes 798728 | tf_op jit(solution)/shard_map/ppermute | solution.py:200
  45.1 3.4 %collective-permute-start = (bf16[12,80,128]{2,1,0:T(8,128)(2,1)S(1)}, bf16[12,80,128]{2,1,0:T(8,128)(2,1)S(1)}, u32[]{:S(2)}, u32[]{:S(2)}) collective-permute-start(bf16[12,80,128]{2,1,0:T(8,128)(2,1)S(1)} %all-to-all-done.left_own), channel_id=1, source_target_pairs={{0,48},{48,0},{1,49},{49,1},{2,50},{50,2},{3,51},{51,3},{4,52},{52... | collective-permute-start | bytes 737288 | tf_op jit(solution)/shard_map/ppermute | solution.py:202

commit v13 on v12

--- a/solution.py
+++ b/solution.py
@@ -197,7 +197,7 @@
     left = spread(left_blocks.reshape(2, BS, BS), left_coords.reshape(2, 2))
     pieces = lax.all_to_all(left, "col", 0, 0)
     three = lax.ppermute(two, axes, on[1])
-    four = lax.ppermute(two[0], axes, on[2])
+    four = lax.ppermute(jnp.where(one[0, BODY, 0] >= 0, two[0], 0), axes, on[2])
     blocks = [mine, one, two, three, four]
     pieces_other = lax.ppermute(pieces, "core", cross)
     part = multiply(pieces, pieces_other, *blocks)

time: 74.6 us -> 77.2 us (1.035)
  starting transfers between devices: 34.1 us -> 39.5 us
  waiting for transfers between devices: 13.3 us -> 9.36 us
    ppermute x1, starting transfers between devices: 2.98 us -> 7.12 us  [shards(): three = lax.ppermute(two, axes, on[1])]
    all_to_all x1, waiting for transfers between devices: 6.95 us -> 2.95 us  [shards(): pieces = lax.all_to_all(left, 'col', 0, 0)]
    ppermute x1, waiting for transfers between devices: 0.01 us -> 1.4 us  [shards(): two = lax.ppermute(both, axes, on[2])]
    ppermute x1, starting transfers between devices: 1.91 us -> 3.19 us  [shards(): pieces_other = lax.ppermute(pieces, 'core', cross)]
    ppermute x1, starting transfers between devices: 3.11 us -> 1.92 us  [shards(): one = lax.ppermute(both, axes, on[1])]
    all_to_all x1, starting transfers between devices: 9.83 us -> 10.9 us  [shards(): pieces = lax.all_to_all(left, 'col', 0, 0)]
    ppermute x1, waiting for transfers between devices: 3.51 us -> 2.53 us  [shards(): four = lax.ppermute(jnp.where(one[0, BODY, 0] >= 0, two[0], 0), axes, on[2])]
  transfers between devices with their start and end apart: 7 -> 7, of which waited for: 4 -> 5; matrix products, arithmetic and copies ran while one was open for 0% -> 1% of each run, Pallas kernels for 2% -> 2%
where the time goes in v13:
time: 77.2 us; the launch traced here: 76.7 us
  starting transfers between devices  39.5 us (51%)
  blocking collectives  14.2 us (18%)
  Pallas kernels  10.4 us (13%)
  waiting for transfers between devices  9.36 us (12%)
  local copies, waits for them, and re-layouts  1.38 us (2%)
  other arithmetic  1.09 us (1%)
    all_to_all x1, blocking collectives, shards(): parts = lax.all_to_all(part, ('core', 'layer'), 0, 0)  14.2 us
    ppermute x1, starting transfers between devices, shards(): both = jnp.stack([mine, lax.ppermute(mine, 'core', cross)])  12.4 us
    all_to_all x1, starting transfers between devices, shards(): pieces = lax.all_to_all(left, 'col', 0, 0)  10.9 us
    ppermute x1, starting transfers between devices, shards(): three = lax.ppermute(two, axes, on[1])  7.12 us
    pallas_call x1, Pallas kernels, multiply(): pl.pallas_call(place_kernel, out_shape=jax.ShapeDtypeStruct((2 * N_LAYER,...  6.95 us
    ppermute x1, starting transfers between devices, shards(): pieces_other = lax.ppermute(pieces, 'core', cross)  3.19 us
    all_to_all x1, waiting for transfers between devices, shards(): pieces = lax.all_to_all(left, 'col', 0, 0)  2.95 us
    ppermute x1, waiting for transfers between devices, shards(): four = lax.ppermute(jnp.where(one[0, BODY, 0] >= 0, two[0], 0), axes, on[2])  2.53 us
  transfers between devices with their start and end apart: 7, of which 5 were waited for; matrix products, arithmetic and copies ran while one was open for 1% of the time, Pallas kernels for 2%

profile of v13, /device:TPU:1, one launch (start us, length us, event | category | flops | bytes accessed | tf_op | source)
XLA Modules:
  0.0 76.7 jit_solution(872104660124040105)
XLA Ops:
  0.0 1.9 %shard_map.47.mine = bf16[1040,128]{1,0:T(8,128)(2,1)} custom-call(bf16[32,64,64]{2,1,0:T(8,128)(2,1)} %bitcast.12, s32[2,32]{1,0:T(2,128)} %bitcast.15), custom_call_target="tpu_custom_call" | custom-call | bytes 1048576 | tf_op jit(solution)/shard_map/pallas_call | solution.py:45
  1.9 12.4 %collective-permute-start.1 = (bf16[1040,128]{1,0:T(8,128)(2,1)}, bf16[1040,128]{1,0:T(8,128)(2,1)S(1)}, u32[]{:S(2)}, u32[]{:S(2)}) collective-permute-start(bf16[1040,128]{1,0:T(8,128)(2,1)} %shard_map.47.mine), channel_id=1, source_target_pairs={{0,48},{48,0},{1,49},{49,1},{2,50},{50,2},{3,51},{51,3},{4,52},{52... | collective-permute-start | bytes 798728 | tf_op jit(solution)/shard_map/ppermute | solution.py:194
  14.3 1.4 %collective-permute-done.1 = bf16[1040,128]{1,0:T(8,128)(2,1)S(1)} collective-permute-done((bf16[1040,128]{1,0:T(8,128)(2,1)}, bf16[1040,128]{1,0:T(8,128)(2,1)S(1)}, u32[]{:S(2)}, u32[]{:S(2)}) %collective-permute-start.1) | collective-permute-done | bytes 266272 | tf_op jit(solution)/shard_map/ppermute | solution.py:194
  15.7 1.0 %pad_maximum_fusion = bf16[2,1040,128]{2,1,0:T(8,128)(2,1)S(1)} fusion(bf16[1,1040,128]{2,1,0:T(8,128)(2,1)S(1)} %bitcast.13, bf16[1,1040,128]{2,1,0:T(8,128)(2,1)} %bitcast.11), kind=kLoop, calls=%fused_computation.1 | loop fusion | flops 266240 | bytes 1064960 | tf_op jit(solution)/shard_map/stack | solution.py:194
  16.7 1.9 %collective-permute-start.2 = (bf16[2,1040,128]{2,1,0:T(8,128)(2,1)S(1)}, bf16[2,1040,128]{2,1,0:T(8,128)(2,1)S(1)}, u32[]{:S(2)}, u32[]{:S(2)}) collective-permute-start(bf16[2,1040,128]{2,1,0:T(8,128)(2,1)S(1)} %pad_maximum_fusion), channel_id=1, source_target_pairs={{0,96},{48,720},{96,192},{144,48},{192,288},{240,144},{288,384},{3... | collective-permute-start | bytes 1597448 | tf_op jit(solution)/shard_map/ppermute | solution.py:195
  18.6 1.9 %collective-permute-start.3 = (bf16[2,1040,128]{2,1,0:T(8,128)(2,1)S(1)}, bf16[2,1040,128]{2,1,0:T(8,128)(2,1)S(1)}, u32[]{:S(2)}, u32[]{:S(2)}) collective-permute-start(bf16[2,1040,128]{2,1,0:T(8,128)(2,1)S(1)} %pad_maximum_fusion), channel_id=1, source_target_pairs={{0,192},{48,624},{96,288},{144,720},{192,384},{240,48},{288,480},{... | collective-permute-start | bytes 1597448 | tf_op jit(solution)/shard_map/ppermute | solution.py:196
  20.5 1.6 %shard_map.46 = bf16[12,80,128]{2,1,0:T(8,128)(2,1)} custom-call(bf16[2,64,64]{2,1,0:T(8,128)(2,1)} %bitcast.14, s32[2,2]{1,0:T(2,128)} %bitcast.16), custom_call_target="tpu_custom_call" | custom-call | bytes 1048576 | tf_op jit(solution)/shard_map/pallas_call | solution.py:69
  22.1 10.9 %all-to-all-start = ((bf16[12,80,128]{2,1,0:T(8,128)(2,1)}), bf16[12,80,128]{2,1,0:T(8,128)(2,1)S(1)}, u32[]{:S(2)}, u32[]{:S(2)}) async-start(bf16[12,80,128]{2,1,0:T(8,128)(2,1)} %shard_map.46), calls=%async_computation | async-start | bytes 491520 | tf_op jit(solution)/shard_map/all_to_all | solution.py:198
  33.0 0.0 collective-permute-done.2.one
  33.0 0.6 slice.8
  34.2 1.4 %collective-permute-done.3.two = bf16[2,1040,128]{2,1,0:T(8,128)(2,1)S(1)} collective-permute-done((bf16[2,1040,128]{2,1,0:T(8,128)(2,1)S(1)}, bf16[2,1040,128]{2,1,0:T(8,128)(2,1)S(1)}, u32[]{:S(2)}, u32[]{:S(2)}) %collective-permute-start.3) | collective-permute-done | bytes 532512 | tf_op jit(solution)/shard_map/ppermute | solution.py:196
  35.6 7.1 %collective-permute-start.4 = (bf16[2,1040,128]{2,1,0:T(8,128)(2,1)S(1)}, bf16[2,1040,128]{2,1,0:T(8,128)(2,1)S(1)}, u32[]{:S(2)}, u32[]{:S(2)}) collective-permute-start(bf16[2,1040,128]{2,1,0:T(8,128)(2,1)S(1)} %collective-permute-done.3.two), channel_id=1, source_target_pairs={{0,96},{48,720},{96,192},{144,48},{192,288},{240,144},{288,384},{3... | collective-permute-start | bytes 1597448 | tf_op jit(solution)/shard_map/ppermute | solution.py:199
  42.7 0.0 copy-start
  42.8 2.1 %collective-permute-start.5 = (bf16[1040,128]{1,0:T(8,128)(2,1)S(1)}, bf16[1040,128]{1,0:T(8,128)(2,1)S(1)}, u32[]{:S(2)}, u32[]{:S(2)}) collective-permute-start(bf16[1040,128]{1,0:T(8,128)(2,1)S(1)} %fusion), channel_id=1, source_target_pairs={{0,192},{48,624},{96,288},{144,720},{192,384},{240,48},{288,480},{... | collective-permute-start | bytes 798728 | tf_op jit(solution)/shard_map/ppermute | solution.py:200
  44.8 2.9 %all-to-all-done.left_own = bf16[12,80,128]{2,1,0:T(8,128)(2,1)S(1)} async-done(((bf16[12,80,128]{2,1,0:T(8,128)(2,1)}), bf16[12,80,128]{2,1,0:T(8,128)(2,1)S(1)}, u32[]{:S(2)}, u32[]{:S(2)}) %all-to-all-start) | async-done | bytes 245792 | tf_op jit(solution)/shard_map/all_to_all | solution.py:198
  47.8 3.2 %collective-permute-start = (bf16[12,80,128]{2,1,0:T(8,128)(2,1)S(1)}, bf16[12,80,128]{2,1,0:T(8,128)(2,1)S(1)}, u32[]{:S(2)}, u32[]{:S(2)}) collective-permute-start(bf16[12,80,128]{2,1,0:T(8,128)(2,1)S(1)} %all-to-all-done.left_own), channel_id=1, source_target_pairs={{0,48},{48,0},{1,49},{49,1},{2,50},{50,2},{3,51},{51,3},{4,52},{52... | collective-permute-start | bytes 737288 | tf_op jit(solution)/shard_map/ppermute | solution.py:202
  51.0 1.1 %collective-permute-done.left_other = bf16[12,80,128]{2,1,0:T(8,128)(2,1)S(1)} collective-permute-done((bf16[12,80,128]{2,1,0:T(8,128)(2,1)S(1)}, bf16[12,80,128]{2,1,0:T(8,128)(2,1)S(1)}, u32[]{:S(2)}, u32[]{:S(2)}) %collective-permute-start) | collective-permute-done | bytes 245792 | tf_op jit(solution)/shard_map/ppermute | solution.py:202
  52.1 2.5 %collective-permute-done.5.four = bf16[1040,128]{1,0:T(8,128)(2,1)S(1)} collective-permute-done((bf16[1040,128]{1,0:T(8,128)(2,1)S(1)}, bf16[1040,128]{1,0:T(8,128)(2,1)S(1)}, u32[]{:S(2)}, u32[]{:S(2)}) %collective-permute-start.5) | collective-permute-done | bytes 266272 | tf_op jit(solution)/shard_map/ppermute | solution.py:200
  54.6 0.0 collective-permute-done.4.three
  54.6 0.0 copy-done
  54.6 6.9 %shard_map.48 = bf16[8,64,512]{2,1,0:T(8,128)(2,1)S(1)} custom-call(bf16[12,80,128]{2,1,0:T(8,128)(2,1)S(1)} %all-to-all-done.left_own, bf16[12,80,128]{2,1,0:T(8,128)(2,1)S(1)} %collective-permute-done.left_other, bf16[1040,128]{1,0:T(8,128)(2,1)S(1)} %copy-done, bf16[2,1040,128]{2,1,0:T(8,128)(2,1)S(1)} %collective-permute-done.2.one, ...), custom_call_target="tpu_custom_call" | custom-call | flops 1610612736 | bytes 4194304 | tf_op jit(solution)/shard_map/pallas_call | solution.py:165
  61.6 14.2 %all_to_all.10 = bf16[8,64,512]{2,1,0:T(8,128)(2,1)S(1)} all-to-all(bf16[8,64,512]{2,1,0:T(8,128)(2,1)S(1)} %shard_map.48), channel_id=1, replica_groups=mesh['y'=8,'core'=2,'col'=12,'layer'=4] {'core','layer'}, dimensions={0} | all-to-all | bytes 1048576 | tf_op jit(solution)/shard_map/all_to_all | solution.py:204
  75.8 0.1 convert_reduce_fusion
  75.9 0.8 %reshape.24 = f32[1,64,8,64]{3,2,1,0:T(8,128)} reshape(f32[64,512]{1,0:T(8,128)S(1)} %convert_reduce_fusion) | data formatting | bytes 262144 | tf_op jit(solution)/shard_map/reshape | solution.py:206
  (1 shorter events, 0.0 us)
Async XLA Ops:
  1.9 13.8 %collective-permute-start.1 = (bf16[1040,128]{1,0:T(8,128)(2,1)}, bf16[1040,128]{1,0:T(8,128)(2,1)S(1)}, u32[]{:S(2)}, u32[]{:S(2)}) collective-permute-start(bf16[1040,128]{1,0:T(8,128)(2,1)} %shard_map.47.mine), channel_id=1, source_target_pairs={{0,48},{48,0},{1,49},{49,1},{2,50},{50,2},{3,51},{51,3},{4,52},{52... | collective-permute-start | bytes 798728 | tf_op jit(solution)/shard_map/ppermute | solution.py:194
  16.7 16.3 %collective-permute-start.2 = (bf16[2,1040,128]{2,1,0:T(8,128)(2,1)S(1)}, bf16[2,1040,128]{2,1,0:T(8,128)(2,1)S(1)}, u32[]{:S(2)}, u32[]{:S(2)}) collective-permute-start(bf16[2,1040,128]{2,1,0:T(8,128)(2,1)S(1)} %pad_maximum_fusion), channel_id=1, source_target_pairs={{0,96},{48,720},{96,192},{144,48},{192,288},{240,144},{288,384},{3... | collective-permute-start | bytes 1597448 | tf_op jit(solution)/shard_map/ppermute | solution.py:195
  18.6 17.0 %collective-permute-start.3 = (bf16[2,1040,128]{2,1,0:T(8,128)(2,1)S(1)}, bf16[2,1040,128]{2,1,0:T(8,128)(2,1)S(1)}, u32[]{:S(2)}, u32[]{:S(2)}) collective-permute-start(bf16[2,1040,128]{2,1,0:T(8,128)(2,1)S(1)} %pad_maximum_fusion), channel_id=1, source_target_pairs={{0,192},{48,624},{96,288},{144,720},{192,384},{240,48},{288,480},{... | collective-permute-start | bytes 1597448 | tf_op jit(solution)/shard_map/ppermute | solution.py:196
  22.1 25.7 %all-to-all-start = ((bf16[12,80,128]{2,1,0:T(8,128)(2,1)}), bf16[12,80,128]{2,1,0:T(8,128)(2,1)S(1)}, u32[]{:S(2)}, u32[]{:S(2)}) async-start(bf16[12,80,128]{2,1,0:T(8,128)(2,1)} %shard_map.46), calls=%async_computation | async-start | bytes 491520 | tf_op jit(solution)/shard_map/all_to_all | solution.py:198
  35.6 19.0 %collective-permute-start.4 = (bf16[2,1040,128]{2,1,0:T(8,128)(2,1)S(1)}, bf16[2,1040,128]{2,1,0:T(8,128)(2,1)S(1)}, u32[]{:S(2)}, u32[]{:S(2)}) collective-permute-start(bf16[2,1040,128]{2,1,0:T(8,128)(2,1)S(1)} %collective-permute-done.3.two), channel_id=1, source_target_pairs={{0,96},{48,720},{96,192},{144,48},{192,288},{240,144},{288,384},{3... | collective-permute-start | bytes 1597448 | tf_op jit(solution)/shard_map/ppermute | solution.py:199
  42.7 11.9 %copy-start = (bf16[1040,128]{1,0:T(8,128)(2,1)S(1)}, bf16[1040,128]{1,0:T(8,128)(2,1)}, u32[]{:S(2)}) copy-start(bf16[1040,128]{1,0:T(8,128)(2,1)} %shard_map.47.mine) | copy-start | bytes 798724
  42.8 11.9 %collective-permute-start.5 = (bf16[1040,128]{1,0:T(8,128)(2,1)S(1)}, bf16[1040,128]{1,0:T(8,128)(2,1)S(1)}, u32[]{:S(2)}, u32[]{:S(2)}) collective-permute-start(bf16[1040,128]{1,0:T(8,128)(2,1)S(1)} %fusion), channel_id=1, source_target_pairs={{0,192},{48,624},{96,288},{144,720},{192,384},{240,48},{288,480},{... | collective-permute-start | bytes 798728 | tf_op jit(solution)/shard_map/ppermute | solution.py:200
  47.8 4.3 %collective-permute-start = (bf16[12,80,128]{2,1,0:T(8,128)(2,1)S(1)}, bf16[12,80,128]{2,1,0:T(8,128)(2,1)S(1)}, u32[]{:S(2)}, u32[]{:S(2)}) collective-permute-start(bf16[12,80,128]{2,1,0:T(8,128)(2,1)S(1)} %all-to-all-done.left_own), channel_id=1, source_target_pairs={{0,48},{48,0},{1,49},{49,1},{2,50},{50,2},{3,51},{51,3},{4,52},{52... | collective-permute-start | bytes 737288 | tf_op jit(solution)/shard_map/ppermute | solution.py:202
